TPU v7x, 32 devices: a whole 2x2x4 slice. The times are simulated.
32 devices in a mesh: gx: 8 (over z, x), gy: 4 (over y, core).
Axes of the slice: x: 2, y: 2, z: 4, core: 2. Of those that a mesh axis runs over, the one named last changes fastest.
Arguments:
- velocity: float32 [3, 128, 128, 128], P(None, 'gx', 'gy'), may hold values from -3 to 3
- theta: float32 [128, 128, 128], P('gx', 'gy'), may hold values from -4 to 4
- vapour: float32 [128, 128, 128], P('gx', 'gy'), may hold values from 0.5 to 1.5
- radius_sq: float32 [64, 1024], P(None, ('gx', 'gy')), may hold values from 0.5 to 2
- multiplicity: float32 [64, 1024], P(None, ('gx', 'gy')), may hold values from 0.5 to 2
- counts: int32 [1024], P(('gx', 'gy')), may hold values from 16 to 64
- pairing: int32 [1024, 64], P(('gx', 'gy')), may hold values from 0 to 63, each once within a row
- destination: int32 [64, 1024], P(None, ('gx', 'gy')), may hold values from 0 to 1023
Outputs:
- velocity_new: float32 [3, 128, 128, 128], P(None, 'gx', 'gy')
- theta_new: float32 [128, 128, 128], P('gx', 'gy')
- vapour_new: float32 [128, 128, 128], P('gx', 'gy')
- moments: float32 [3, 1024], P(None, ('gx', 'gy'))
Inputs may be any that keep to these rules, and one draw needn't show every extreme that they name: `pairing`: each row is a permutation of 0 to 63.
All inputs are finite; a program needn't handle non-finite values.
Results may differ from a plain program's by a relative error of at most 0.0003.
Values sent between devices are 32-bit elements; how exact they have to be, the bound alone decides.
No kernel may reach another device: no remote copies, remote signals or barrier semaphores. Data moves between devices by JAX's collectives and lax.ppermute only.
A program may use at most 64 MiB of HBM per device.

v0:
```python
import math

import jax
import jax.numpy as jnp
from jax import lax
from jax.sharding import PartitionSpec as P

BW = 4


TIME_STEP = 0.2
DIFFUSION = 0.05
BUOYANCY = 0.5
GROWTH = 0.5
COLLISION = 0.05
CONDENSE = 0.002
HIGHEST = lax.Precision.HIGHEST


def extended(shard, sides, width):
    for axis, dim in sides:
        count, length = (lax.axis_size(axis), shard.shape[dim])
        up = [(i, (i + 1) % count) for i in range(count)]
        down = [(j, i) for i, j in up]
        last = lax.slice_in_dim(shard, length - width, length, axis=dim)
        initial = lax.slice_in_dim(shard, 0, width, axis=dim)
        before = lax.ppermute(last, axis, up)
        after = lax.ppermute(initial, axis, down)
        shard = jnp.concatenate([before, shard, after], axis=dim)
    return shard


def from_behind(block, axis, distance):
    devices = range(lax.axis_size(axis))
    route = [((i - distance) % len(devices), i) for i in devices]
    return lax.ppermute(block, axis, route)


def vertical_pair(values):
    upper_cell = jnp.concatenate([values[..., 1:], values[..., -1:]], axis=-1)
    lower_cell = jnp.concatenate([values[..., :1], values[..., :-1]], axis=-1)
    return (upper_cell, lower_cell)


def advect_fields(centre, east_cell, west_cell, north_cell, south_cell):
    upper_cell, lower_cell = vertical_pair(centre)
    carried = -0.5 * (
        centre[0] * (east_cell - west_cell)
        + centre[1] * (north_cell - south_cell)
        + centre[2] * (upper_cell - lower_cell)
    )
    spread = (
        east_cell + west_cell + north_cell + south_cell + upper_cell + lower_cell - 6.0 * centre
    )
    return centre + TIME_STEP * (carried + DIFFUSION * spread)


def cosine_table(levels):
    level_index = jnp.arange(levels).astype(jnp.float32)
    return jnp.cos(math.pi * (level_index[:, None] + 0.5) * level_index[None, :] / levels)


def fourier_table(length, blocks, block_width):
    wave_index = jnp.arange(length)
    positions = jnp.arange(blocks)[:, None] * block_width + jnp.arange(block_width)[None, :]
    residue = wave_index[:, None, None] * positions[None] % length
    angles = 2.0 * math.pi / length * residue.astype(jnp.float32)
    return (jnp.cos(angles), jnp.sin(angles))


def forward_planes(planes, cosine_x, sine_x, cosine_y, sine_y):
    real_x = jnp.einsum("kai,mabij->mkbj", cosine_x, planes, precision=HIGHEST)
    imag_x = -jnp.einsum("kai,mabij->mkbj", sine_x, planes, precision=HIGHEST)
    real_xy = jnp.einsum("lbj,mkbj->mkl", cosine_y, real_x, precision=HIGHEST) + jnp.einsum(
        "lbj,mkbj->mkl", sine_y, imag_x, precision=HIGHEST
    )
    imag_xy = jnp.einsum("lbj,mkbj->mkl", cosine_y, imag_x, precision=HIGHEST) - jnp.einsum(
        "lbj,mkbj->mkl", sine_y, real_x, precision=HIGHEST
    )
    return (real_xy, imag_xy)


def solve_modes(real_xy, imag_xy, first_mode, levels):
    mode_count, span_kx, span_ky = real_xy.shape
    mode_index = first_mode + jnp.arange(mode_count)
    wave_x = 2.0 * jnp.cos(2.0 * math.pi * jnp.arange(span_kx).astype(jnp.float32) / span_kx) - 2.0
    wave_y = 2.0 * jnp.cos(2.0 * math.pi * jnp.arange(span_ky).astype(jnp.float32) / span_ky) - 2.0
    wave_z = 2.0 * jnp.cos(math.pi * mode_index.astype(jnp.float32) / levels) - 2.0
    eigenvalue = wave_x[None, :, None] + wave_y[None, None, :] + wave_z[:, None, None]
    anchor = (
        (mode_index == 0)[:, None, None]
        & (jnp.arange(span_kx) == 0)[None, :, None]
        & (jnp.arange(span_ky) == 0)[None, None, :]
    )
    safe_value = jnp.where(anchor, 1.0, eigenvalue)
    return (
        jnp.where(anchor, 0.0, real_xy / safe_value),
        jnp.where(anchor, 0.0, imag_xy / safe_value),
    )


def inverse_planes(real_part, imag_part, cosine_x, sine_x, cosine_y, sine_y):
    real_y = jnp.einsum("lbj,fmkl->fmkbj", cosine_y, real_part, precision=HIGHEST) - jnp.einsum(
        "lbj,fmkl->fmkbj", sine_y, imag_part, precision=HIGHEST
    )
    imag_y = jnp.einsum("lbj,fmkl->fmkbj", sine_y, real_part, precision=HIGHEST) + jnp.einsum(
        "lbj,fmkl->fmkbj", cosine_y, imag_part, precision=HIGHEST
    )
    summed = jnp.einsum("kai,fmkbj->fmabij", cosine_x, real_y, precision=HIGHEST) - jnp.einsum(
        "kai,fmkbj->fmabij", sine_x, imag_y, precision=HIGHEST
    )
    return summed / (cosine_x.shape[0] * cosine_y.shape[0])


def shards(velocity, theta, vapour, radius_sq, multiplicity, counts, pairing, destination):
    span_x, span_y, levels = theta.shape
    grid_x = lax.axis_size("gx")
    grid_y = lax.axis_size("gy")
    device_count = grid_x * grid_y
    rank_x = lax.axis_index("gx")
    rank_y = lax.axis_index("gy")
    stacked = jnp.concatenate([velocity, theta[None], vapour[None]], axis=0)
    widened = extended(stacked, (("gx", 1), ("gy", 2)), 2)
    centre = widened[:, 1 : span_x + 2, 1 : span_y + 2]
    east_cell = widened[:, 2 : span_x + 3, 1 : span_y + 2]
    west_cell = widened[:, 0 : span_x + 1, 1 : span_y + 2]
    north_cell = widened[:, 1 : span_x + 2, 2 : span_y + 3]
    south_cell = widened[:, 1 : span_x + 2, 0 : span_y + 1]
    wide_advected = advect_fields(centre, east_cell, west_cell, north_cell, south_cell)
    wide_x = wide_advected[0]
    wide_y = wide_advected[1]
    star_z = wide_advected[2, 1:, 1:] + TIME_STEP * BUOYANCY * centre[3, 1:, 1:]
    below_z = jnp.concatenate([jnp.zeros_like(star_z[..., :1]), star_z[..., :-1]], axis=-1)
    divergence = (
        wide_x[1:, 1:] - wide_x[:-1, 1:] + (wide_y[1:, 1:] - wide_y[1:, :-1]) + (star_z - below_z)
    )
    advected = wide_advected[:, 1:, 1:]
    star_x = advected[0]
    star_y = advected[1]
    level_table = cosine_table(levels)
    spectral = jnp.einsum("ijz,zm->mij", divergence, level_table, precision=HIGHEST).reshape(
        levels, 1, span_x, span_y
    )
    planes = lax.all_to_all(spectral, ("gx", "gy"), split_axis=0, concat_axis=1, tiled=True)
    per_device = levels // device_count
    planes = planes.reshape(per_device, grid_x, grid_y, span_x, span_y)
    total_x = span_x * grid_x
    total_y = span_y * grid_y
    cosine_x, sine_x = fourier_table(total_x, grid_x, span_x)
    cosine_y, sine_y = fourier_table(total_y, grid_y, span_y)
    real_xy, imag_xy = forward_planes(planes, cosine_x, sine_x, cosine_y, sine_y)
    device_rank = rank_x * grid_y + rank_y
    real_xy, imag_xy = solve_modes(real_xy, imag_xy, device_rank * per_device, levels)
    weight = jnp.where(jnp.arange(levels) == 0, 1.0 / levels, 2.0 / levels)
    back_table = level_table * weight[None, :]
    single = inverse_planes(real_xy[None], imag_xy[None], cosine_x, sine_x, cosine_y, sine_y)
    single = single.reshape(1, per_device, device_count, span_x, span_y)
    returned = lax.all_to_all(
        single, ("gx", "gy"), split_axis=2, concat_axis=1, tiled=True
    ).reshape(levels, span_x, span_y)
    pressure = jnp.einsum("mij,zm->ijz", returned, back_table, precision=HIGHEST)
    next_plane = from_behind(pressure[0:1], "gx", -1)
    step_east = jnp.concatenate([pressure[1:], next_plane], axis=0) - pressure
    next_row = from_behind(pressure[:, 0:1], "gy", -1)
    step_north = jnp.concatenate([pressure[:, 1:], next_row], axis=1) - pressure
    step_up = jnp.concatenate([pressure[..., 1:], pressure[..., -1:]], axis=-1) - pressure
    velocity_new = jnp.stack([star_x - step_east, star_y - step_north, star_z - step_up])
    theta_new = advected[3]
    moist_field = advected[4]
    box_x = span_x // BW
    box_y = span_y // BW
    box_count = box_x * box_y
    slot_count = radius_sq.shape[0]
    column_sums = moist_field.reshape(box_x, BW, box_y, BW, levels).sum(axis=(1, 3, 4))
    box_mean = (column_sums / (BW * BW * levels)).reshape(box_count)
    slot_index = jnp.arange(slot_count)[:, None]
    live_weight = jnp.where(slot_index < counts[None, :], multiplicity, 0.0)
    grown_sq = radius_sq + GROWTH * jax.nn.softplus(box_mean)[None, :]
    mass_before = radius_sq * jnp.sqrt(radius_sq)
    mass_grown = grown_sq * jnp.sqrt(grown_sq)
    condensed = jnp.sum(live_weight * (mass_grown - mass_before), axis=0)
    vapour_new = (
        moist_field.reshape(box_x, BW, box_y, BW, levels)
        - CONDENSE * condensed.reshape(box_x, 1, box_y, 1, 1)
    ).reshape(span_x, span_y, levels)
    half_count = slot_count // 2
    one_hot = (pairing.T[:, None, :] == jnp.arange(slot_count)[None, :, None]).astype(jnp.float32)
    paired = jnp.einsum(
        "kib,kjb->ijb", one_hot[:half_count], one_hot[half_count:], precision=HIGHEST
    )
    paired = paired + jnp.transpose(paired, (1, 0, 2))
    radius_now = jnp.sqrt(grown_sq)
    radius_sum = radius_now[:, None, :] + radius_now[None, :, :]
    rate_tile = (
        radius_sum
        * radius_sum
        * jnp.abs(grown_sq[:, None, :] - grown_sq[None, :, :])
        * live_weight[None, :, :]
        * paired
    )
    collide_rate = jnp.sum(rate_tile, axis=1)
    gained = jnp.sum(rate_tile * mass_grown[None, :, :], axis=1)
    mass_final = (mass_grown + COLLISION * gained) / (1.0 + COLLISION * collide_rate)
    local_box = jnp.arange(box_count)
    source_x = rank_x * box_x + local_box // box_y
    source_y = rank_y * box_y + local_box % box_y
    target_device = destination // box_count
    target_local = destination % box_count
    target_x = target_device // grid_y * box_x + target_local // box_y
    target_y = target_device % grid_y * box_y + target_local % box_y
    offset_x = (target_x - source_x[None, :] + 1) % (box_x * grid_x) - 1
    offset_y = (target_y - source_y[None, :] + 1) % (box_y * grid_y) - 1
    carried_load = jnp.stack(
        [live_weight, live_weight * mass_final, live_weight * mass_final * mass_final]
    )
    packed = jnp.concatenate(
        [carried_load, offset_x[None].astype(jnp.float32), offset_y[None].astype(jnp.float32)],
        axis=0,
    )
    packed = packed.reshape(5, slot_count, box_x, box_y)
    bordered = extended(packed, (("gx", 2), ("gy", 3)), 1)
    arrived = jnp.zeros((3, box_x, box_y), jnp.float32)
    for step_x in (-1, 0, 1):
        for step_y in (-1, 0, 1):
            source = bordered[
                :, :, 1 - step_x : 1 - step_x + box_x, 1 - step_y : 1 - step_y + box_y
            ]
            chosen = ((source[3] == step_x) & (source[4] == step_y)).astype(jnp.float32)
            arrived = arrived + jnp.sum(source[:3] * chosen[None], axis=1)
    moments = arrived.reshape(3, box_count) / slot_count
    return (velocity_new, theta_new, vapour_new, moments)


def solution(mesh):
    placed = (
        P(None, "gx", "gy", None),
        P("gx", "gy", None),
        P("gx", "gy", None),
        P(None, ("gx", "gy")),
        P(None, ("gx", "gy")),
        P(("gx", "gy")),
        P(("gx", "gy"), None),
        P(None, ("gx", "gy")),
    )
    return jax.shard_map(
        shards,
        mesh=mesh,
        in_specs=placed,
        out_specs=(
            P(None, "gx", "gy", None),
            P("gx", "gy", None),
            P("gx", "gy", None),
            P(None, ("gx", "gy")),
        ),
        check_vma=False,
    )
```

profile of v0, /device:TPU:0, one launch (start us, length us, event | category | flops | bytes accessed | tf_op | source)
XLA Modules:
  0.0 96.7 jit_solution(11454866646278678586)
XLA Ops:
  0.7 1.1 %pad_maximum_fusion.11 = (f32[5,2,32,128]{3,2,1,0:T(8,128)S(1)}, f32[5,2,32,128]{3,2,1,0:T(8,128)S(1)}) fusion(f32[1,16,32,128]{3,2,1,0:T(8,128)} %bitcast.222, f32[1,16,32,128]{3,2,1,0:T(8,128)} %bitcast.218, f32[3,16,32,128]{3,2,1,0:T(8,128)} %param.8), kind=kLoop, calls=%fused_computation.79 | loop fusion | flops 163840 | bytes 1638400 | tf_op jit(solution)/shard_map/slice | solution.py:25
  1.7 3.0 %collective-permute-start = (f32[5,2,32,128]{3,2,1,0:T(8,128)S(1)}, f32[5,2,32,128]{3,2,1,0:T(8,128)S(1)}, u32[]{:S(2)}, u32[]{:S(2)}) collective-permute-start(f32[5,2,32,128]{3,2,1,0:T(8,128)S(1)} %get-tuple-element.38), channel_id=1, source_target_pairs={{0,4},{4,8},{8,12},{12,16},{16,20},{20,24},{24,28},{28,0},{1,5},{5... | collective-permute-start | bytes 491528 | tf_op jit(solution)/shard_map/ppermute | solution.py:27
  4.7 3.1 %collective-permute-start.1 = (f32[5,2,32,128]{3,2,1,0:T(8,128)S(1)}, f32[5,2,32,128]{3,2,1,0:T(8,128)S(1)}, u32[]{:S(2)}, u32[]{:S(2)}) collective-permute-start(f32[5,2,32,128]{3,2,1,0:T(8,128)S(1)} %get-tuple-element.39), channel_id=1, source_target_pairs={{4,0},{8,4},{12,8},{16,12},{20,16},{24,20},{28,24},{0,28},{5,1},{9... | collective-permute-start | bytes 491528 | tf_op jit(solution)/shard_map/ppermute | solution.py:28
  7.9 1.1 %iota_compare_fusion = pred[64,64,32]{1,0,2:T(32,128)(4,1)S(1)} fusion(s32[64,32]{0,1:T(8,128)} %bitcast.231), kind=kLoop, calls=%fused_computation.38 | loop fusion | flops 131072 | bytes 139264 | tf_op jit(solution)/shard_map/eq | solution.py:187
  9.7 0.7 broadcast_add_fusion
  10.4 0.7 broadcast_and_fusion
  11.1 0.7 and_convert_fusion
  11.8 1.3 %copy.28 = f32[32,64,64]{1,2,0:T(8,128)} copy(f32[32,64,64]{2,1,0:T(8,128)S(1)} %fusion.19) | data formatting | bytes 1048576 | tf_op jit(solution)/shard_map/kib,kjb->ijb/dot_general | solution.py:188
  13.1 0.6 multiply_add_fusion.1
  14.1 0.5 broadcast_select_fusion
  14.5 1.7 %collective-permute-start.3 = (f32[5,20,2,128]{3,2,1,0:T(2,128)S(1)}, f32[5,20,2,128]{3,2,1,0:T(2,128)S(1)}, u32[]{:S(2)}, u32[]{:S(2)}) collective-permute-start(f32[5,20,2,128]{3,2,1,0:T(2,128)S(1)} %get-tuple-element.36), channel_id=1, source_target_pairs={{1,0},{2,1},{3,2},{0,3},{5,4},{6,5},{7,6},{4,7},{9,8},{10,9},{11,1... | collective-permute-start | bytes 307208 | tf_op jit(solution)/shard_map/ppermute | solution.py:28
  16.3 1.9 %collective-permute-done.2 = f32[5,20,2,128]{3,2,1,0:T(2,128)S(1)} collective-permute-done((f32[5,20,2,128]{3,2,1,0:T(2,128)S(1)}, f32[5,20,2,128]{3,2,1,0:T(2,128)S(1)}, u32[]{:S(2)}, u32[]{:S(2)}) %collective-permute-start.2) | collective-permute-done | bytes 102432 | tf_op jit(solution)/shard_map/ppermute | solution.py:27
  18.4 0.6 fusion.194
  19.0 0.6 fusion.195
  19.8 2.9 %multiply_add_fusion = f32[5,17,33,128]{3,2,1,0:T(8,128)S(1)} fusion(f32[5,20,34,128]{3,2,1,0:T(8,128)S(1)} %maximum_maximum_fusion, f32[5,17,33,127]{3,2,1,0:T(8,128)S(1)} %get-tuple-element.25, f32[5,17,33,1]{3,2,1,0:T(8,128)S(1)} %get-tuple-element.27, f32[5,17,33,1]{3,2,1,0:T(8,128)S(1)} %get-tuple-element.26, ...), kind=kLoop, calls=%fused_computation.8 | loop fusion | flops 9694080 | bytes 12655616 | tf_op jit(solution)/shard_map/add | solution.py:55
  22.7 0.9 slice_reduce_fusion
  24.0 0.8 slice_bitcast_fusion.1
  24.8 0.7 reduce_sum.133
  25.5 0.9 reduce_sum.134
  26.5 0.8 fusion.190
  27.3 2.5 %multiply_reduce_fusion = (f32[64,32]{0,1:T(8,128)S(1)}, f32[64,32]{0,1:T(8,128)S(1)}) fusion(f32[64,32]{0,1:T(8,128)S(1)} %get-tuple-element.57, f32[32,64,64]{2,1,0:T(8,128)S(1)} %fusion.19, f32[32,64,64]{1,2,0:T(8,128)} %copy.28, f32[64,32]{0,1:T(8,128)S(1)} %get-tuple-element.20, f32[64,32]{0,1:T(8,128)S(1)} %get-tuple-element.58, ...), kind=kLoop, calls=%fused_computation.37 | loop fusion | flops 1437696 | bytes 1097728 | tf_op jit(solution)/shard_map/reduce_sum | solution.py:202
  29.9 1.6 %multiply_bitcast_fusion.1 = (f32[1,64,32]{1,2,0:T(8,128)}, f32[64,32]{0,1:T(8,128)S(1)}, f32[32]{0:T(128)S(1)}) fusion(f32[64,32]{0,1:T(8,128)S(1)} %get-tuple-element.20, f32[64,32]{0,1:T(8,128)S(1)} %get-tuple-element.5, f32[64,32]{0,1:T(8,128)S(1)} %get-tuple-element.4, f32[64,32]{0,1:T(8,128)} %param.11, f32[32]{0:T(128)S(1)} %fusion.137), kind=kLoop, calls=%fused_computation.256 | loop fusion | flops 24544 | bytes 49408 | tf_op jit(solution)/shard_map/stack | solution.py:213
  31.4 0.6 multiply_bitcast_fusion
  32.0 0.7 bitcast_dynamic-update-slice_fusion.1
  32.8 0.7 bitcast_dynamic-update-slice_fusion
  33.5 0.6 fusion.196
  34.4 4.4 %collective-permute-start.7 = (f32[5,64,1,8]{1,3,2,0:T(8,128)}, f32[5,64,1,8]{1,3,2,0:T(8,128)S(1)}, u32[]{:S(2)}, u32[]{:S(2)}) collective-permute-start(f32[5,64,1,8]{1,3,2,0:T(8,128)} %get-tuple-element.54), channel_id=1, source_target_pairs={{4,0},{8,4},{12,8},{16,12},{20,16},{24,20},{28,24},{0,28},{5,1},{9... | collective-permute-start | bytes 30728 | tf_op jit(solution)/shard_map/ppermute | solution.py:28
  39.1 0.9 bitcast_subtract_fusion
  39.9 1.4 %convolution_bitcast_fusion.6 = f32[128,1,16,32]{0,3,2,1:T(8,128)} fusion(f32[17,33,128]{2,1,0:T(8,128)S(1)} %copy-done.5, f32[17,33,128]{2,1,0:T(8,128)S(1)} %get-tuple-element.34, f32[16,32,128]{2,1,0:T(8,128)S(1)} %get-tuple-element.31, f32[16,32,127]{2,1,0:T(8,128)S(1)} %bitcast.229, f32[128]{0:T(128)S(1)} %iota_convert_fusion, ...), kind=kOutput, calls=%fused_computation.24 | convolution fusion | flops 101023744 | bytes 1836032 | tf_op jit(solution)/shard_map/ijz,zm->mij/dot_general | solution.py:141
  41.3 1.5 %copy.21 = f32[128,1,16,32]{3,2,1,0:T(8,128)S(1)} copy(f32[128,1,16,32]{0,3,2,1:T(8,128)} %convolution_bitcast_fusion.6) | data formatting | bytes 524288 | tf_op jit(solution)/shard_map/reshape | solution.py:141
  42.8 1.2 %reshape.351 = f32[32,1,2048]{2,1,0:T(1,128)} reshape(f32[128,1,16,32]{3,2,1,0:T(8,128)S(1)} %copy.21) | data formatting | bytes 524288
  44.0 2.8 %all-to-all-start = ((f32[32,1,2048]{2,1,0:T(1,128)}), f32[32,1,2048]{2,1,0:T(1,128)S(1)}, u32[]{:S(2)}, u32[]{:S(2)}) async-start(f32[32,1,2048]{2,1,0:T(1,128)} %reshape.351), calls=%async_computation | async-start | bytes 524288 | tf_op jit(solution)/shard_map/all_to_all | solution.py:144
  47.0 1.6 %collective-permute-start.8 = (f32[5,64,6,1]{1,3,2,0:T(1,128)S(1)}, f32[5,64,6,1]{1,3,2,0:T(1,128)S(1)}, u32[]{:S(2)}, u32[]{:S(2)}) collective-permute-start(f32[5,64,6,1]{1,3,2,0:T(1,128)S(1)} %get-tuple-element.49), channel_id=1, source_target_pairs={{1,0},{2,1},{3,2},{0,3},{5,4},{6,5},{7,6},{4,7},{9,8},{10,9},{11,1... | collective-permute-start | bytes 23048 | tf_op jit(solution)/shard_map/ppermute | solution.py:28
  48.7 0.7 reduce_sum.148
  49.3 0.8 collective-permute-done.8
  50.1 0.6 convert_bitcast_fusion.4
  50.8 1.2 %collective-permute-done.9 = f32[5,64,6,1]{1,3,2,0:T(1,128)S(1)} collective-permute-done((f32[5,64,6,1]{1,3,2,0:T(1,128)S(1)}, f32[5,64,6,1]{1,3,2,0:T(1,128)S(1)}, u32[]{:S(2)}, u32[]{:S(2)}) %collective-permute-start.9) | collective-permute-done | bytes 7712 | tf_op jit(solution)/shard_map/ppermute | solution.py:27
  52.0 0.6 convert_bitcast_fusion.7
  52.6 0.8 pad_maximum_fusion.8
  53.4 4.0 %all-to-all-done = f32[32,1,2048]{2,1,0:T(1,128)S(1)} async-done(((f32[32,1,2048]{2,1,0:T(1,128)}), f32[32,1,2048]{2,1,0:T(1,128)S(1)}, u32[]{:S(2)}, u32[]{:S(2)}) %all-to-all-start) | async-done | bytes 262176 | tf_op jit(solution)/shard_map/all_to_all | solution.py:144
  57.4 0.6 broadcast.490
  58.0 1.3 %reduce.3 = f32[32,2048]{1,0:T(8,128)S(1)} reduce(f32[32,1,2048]{2,1,0:T(1,128)S(1)} %all-to-all-done, f32[]{:T(128)} %broadcast.490), dimensions={1}, to_apply=%all_to_all.22.reduce_sub_computation | reduce | bytes 524292 | tf_op jit(solution)/shard_map/all_to_all | solution.py:144
  59.7 1.9 %convolution_bitcast_fusion.1 = f32[4,128,4,32]{1,3,2,0:T(8,128)S(1)} fusion(f32[4,8,4,16,32]{4,3,0,2,1:T(8,128)S(1)} %bitcast.216, s32[8,16]{1,0:T(8,128)S(1)} %iota_add_fusion), kind=kOutput, calls=%fused_computation.17 | convolution fusion | flops 100892672 | bytes 524800 | tf_op jit(solution)/shard_map/kai,mabij->mkbj/dot_general | solution.py:72
  61.6 1.9 %fusion.5 = f32[4,128,4,32]{1,3,2,0:T(8,128)S(1)} fusion(f32[4,8,4,16,32]{4,3,0,2,1:T(8,128)S(1)} %bitcast.217, s32[8,16]{1,0:T(8,128)S(1)} %iota_add_fusion), kind=kOutput, calls=%fused_computation.19 | convolution fusion | flops 100958208 | bytes 524800 | tf_op jit(solution)/shard_map/kai,mabij->mkbj/dot_general | solution.py:73
  63.6 0.8 convolution_bitcast_fusion.2
  64.3 0.8 convolution_bitcast_fusion.4
  65.1 0.8 fusion.9
  65.9 0.7 fusion.48
  66.6 0.7 fusion.55
  67.3 0.8 fusion.13
  68.1 0.7 fusion.2
  68.8 0.7 fusion.3
  69.5 1.4 %fusion.42 = f32[4,4,32,8,16]{2,4,3,1,0:T(8,128)S(1)} fusion(f32[4,128,4,32,1]{1,3,4,2,0:T(8,128)S(1)} %fusion.3, s32[8,16]{1,0:T(8,128)S(1)} %iota_add_fusion), kind=kOutput, calls=%fused_computation.105 | convolution fusion | flops 100892672 | bytes 524800 | tf_op jit(solution)/shard_map/kai,fmkbj->fmabij/dot_general | solution.py:109
  70.9 1.7 %fusion.1 = f32[1,4,8,4,16,32]{5,4,2,3,1,0:T(8,128)S(1)} fusion(f32[4,4,32,8,16]{2,4,3,1,0:T(8,128)S(1)} %fusion.42, f32[4,128,4,32,1]{1,3,4,2,0:T(8,128)S(1)} %fusion.2, s32[8,16]{1,0:T(8,128)S(1)} %iota_add_fusion), kind=kOutput, calls=%fused_computation.11 | convolution fusion | flops 101023744 | bytes 786944 | tf_op jit(solution)/shard_map/kai,fmkbj->fmabij/dot_general | solution.py:109
  73.0 1.2 %reshape.353 = f32[32,1,2048]{2,1,0:T(1,128)} reshape(f32[32,1,4,16,32]{4,3,2,1,0:T(8,128)S(1)} %bitcast.227) | data formatting | bytes 524288
  74.1 2.6 %all-to-all-start.1 = ((f32[32,1,2048]{2,1,0:T(1,128)}), f32[32,1,2048]{2,1,0:T(1,128)S(1)}, u32[]{:S(2)}, u32[]{:S(2)}) async-start(f32[32,1,2048]{2,1,0:T(1,128)} %reshape.353), calls=%async_computation.1 | async-start | bytes 524288 | tf_op jit(solution)/shard_map/all_to_all | solution.py:158
  76.8 1.0 %fusion.76 = (f32[3,4,8]{2,1,0:T(4,128)S(1)}, f32[3,4,8]{2,1,0:T(4,128)S(1)}, f32[3,4,8]{2,1,0:T(4,128)S(1)}) fusion(f32[5,64,6,9]{1,3,2,0:T(8,128)} %get-tuple-element.48, f32[64,4,8]{0,2,1:T(8,128)S(1)} %copy-done.11, f32[64,4,8]{0,2,1:T(8,128)S(1)} %get-tuple-element.44, f32[64,4,8]{0,2,1:T(8,128)S(1)} %get-tuple-element.43), kind=kLoop, calls=%fused_computation.145 | loop fusion | flops 36576 | bytes 99456 | tf_op jit(solution)/shard_map/reduce_sum | solution.py:229
  78.3 9.0 %all-to-all-done.1 = f32[32,1,2048]{2,1,0:T(1,128)S(1)} async-done(((f32[32,1,2048]{2,1,0:T(1,128)}), f32[32,1,2048]{2,1,0:T(1,128)S(1)}, u32[]{:S(2)}, u32[]{:S(2)}) %all-to-all-start.1) | async-done | bytes 262176 | tf_op jit(solution)/shard_map/all_to_all | solution.py:158
  87.3 1.3 %reduce.4 = f32[32,2048]{1,0:T(8,128)S(1)} reduce(f32[32,1,2048]{2,1,0:T(1,128)S(1)} %all-to-all-done.1, f32[]{:T(128)} %broadcast.490), dimensions={1}, to_apply=%all_to_all.25.reduce_sub_computation | reduce | bytes 524292 | tf_op jit(solution)/shard_map/all_to_all | solution.py:158
  89.0 2.8 %fusion.15 = f32[16,32,128]{2,1,0:T(8,128)S(1)} fusion(f32[128,16,32]{2,1,0:T(8,128)S(1)} %bitcast.226, f32[128]{0:T(128)} %broadcast_select_fusion, f32[128]{0:T(128)} %copy-done.18, f32[128]{0:T(128)} %copy-done.17), kind=kOutput, calls=%fused_computation.35 | convolution fusion | flops 100712448 | bytes 525824 | tf_op jit(solution)/shard_map/mij,zm->ijz/dot_general | solution.py:161
  91.8 1.5 %collective-permute-start.4 = (f32[1,32,128]{2,1,0:T(8,128)S(1)}, f32[1,32,128]{2,1,0:T(8,128)S(1)}, u32[]{:S(2)}, u32[]{:S(2)}) collective-permute-start(f32[1,32,128]{2,1,0:T(8,128)S(1)} %slice.345), channel_id=1, source_target_pairs={{4,0},{8,4},{12,8},{16,12},{20,16},{24,20},{28,24},{0,28},{5,1},{9... | collective-permute-start | bytes 49160 | tf_op jit(solution)/shard_map/ppermute | solution.py:36
  93.5 0.6 add_multiply_fusion
  94.8 0.8 collective-permute-done.4
  95.8 0.9 pad_maximum_fusion.7
  (104 shorter events, 5.5 us)
Async XLA Ops:
  0.6 9.7 %copy-start.14 = (f32[64,32]{0,1:T(8,128)S(1)}, f32[64,32]{0,1:T(8,128)}, u32[]{:S(2)}) copy-start(f32[64,32]{0,1:T(8,128)} %param.12) | copy-start | bytes 24580
  0.6 9.7 %copy-start.19 = (s32[32]{0:T(128)S(1)}, s32[32]{0:T(128)}, u32[]{:S(2)}) copy-start(s32[32]{0:T(128)} %param.13) | copy-start | bytes 388
  0.7 10.5 %copy-start.15 = (s32[64,32]{0,1:T(8,128)S(1)}, s32[64,32]{0,1:T(8,128)}, u32[]{:S(2)}) copy-start(s32[64,32]{0,1:T(8,128)} %param.15) | copy-start | bytes 24580
  1.7 12.0 %collective-permute-start = (f32[5,2,32,128]{3,2,1,0:T(8,128)S(1)}, f32[5,2,32,128]{3,2,1,0:T(8,128)S(1)}, u32[]{:S(2)}, u32[]{:S(2)}) collective-permute-start(f32[5,2,32,128]{3,2,1,0:T(8,128)S(1)} %get-tuple-element.38), channel_id=1, source_target_pairs={{0,4},{4,8},{8,12},{12,16},{16,20},{20,24},{24,28},{28,0},{1,5},{5... | collective-permute-start | bytes 491528 | tf_op jit(solution)/shard_map/ppermute | solution.py:27
  4.7 9.2 %collective-permute-start.1 = (f32[5,2,32,128]{3,2,1,0:T(8,128)S(1)}, f32[5,2,32,128]{3,2,1,0:T(8,128)S(1)}, u32[]{:S(2)}, u32[]{:S(2)}) collective-permute-start(f32[5,2,32,128]{3,2,1,0:T(8,128)S(1)} %get-tuple-element.39), channel_id=1, source_target_pairs={{4,0},{8,4},{12,8},{16,12},{20,16},{24,20},{28,24},{0,28},{5,1},{9... | collective-permute-start | bytes 491528 | tf_op jit(solution)/shard_map/ppermute | solution.py:28
  7.8 32.1 %copy-start.17 = (f32[128]{0:T(128)}, f32[128]{0:T(128)S(1)}, u32[]{:S(2)}) copy-start(f32[128]{0:T(128)S(1)} %add_multiply_fusion.1) | copy-start | bytes 1540
  7.9 5.3 %copy-start.20 = (pred[128]{0:T(512)(128)(4,1)}, pred[128]{0:T(512)(128)(4,1)S(1)}, u32[]{:S(2)}) copy-start(pred[128]{0:T(512)(128)(4,1)S(1)} %iota_compare_fusion.2) | copy-start | bytes 388
  9.0 4.9 %copy-start = (f32[3,16,32,128]{3,2,1,0:T(8,128)S(1)}, f32[3,16,32,128]{3,2,1,0:T(8,128)}, u32[]{:S(2)}) copy-start(f32[3,16,32,128]{3,2,1,0:T(8,128)} %param.8) | copy-start | bytes 2359300
  9.0 4.9 %copy-start.3 = (f32[16,32,128]{2,1,0:T(8,128)S(1)}, f32[16,32,128]{2,1,0:T(8,128)}, u32[]{:S(2)}) copy-start(f32[16,32,128]{2,1,0:T(8,128)} %param.9) | copy-start | bytes 786436
  9.0 4.9 %copy-start.4 = (f32[16,32,128]{2,1,0:T(8,128)S(1)}, f32[16,32,128]{2,1,0:T(8,128)}, u32[]{:S(2)}) copy-start(f32[16,32,128]{2,1,0:T(8,128)} %param.10) | copy-start | bytes 786436
  11.8 28.1 %copy-start.18 = (f32[128]{0:T(128)}, f32[128]{0:T(128)S(1)}, u32[]{:S(2)}) copy-start(f32[128]{0:T(128)S(1)} %iota_convert_fusion) | copy-start | bytes 1540
  14.0 4.1 %collective-permute-start.2 = (f32[5,20,2,128]{3,2,1,0:T(2,128)S(1)}, f32[5,20,2,128]{3,2,1,0:T(2,128)S(1)}, u32[]{:S(2)}, u32[]{:S(2)}) collective-permute-start(f32[5,20,2,128]{3,2,1,0:T(2,128)S(1)} %get-tuple-element.37), channel_id=1, source_target_pairs={{0,1},{1,2},{2,3},{3,0},{4,5},{5,6},{6,7},{7,4},{8,9},{9,10},{10,1... | collective-permute-start | bytes 307208 | tf_op jit(solution)/shard_map/ppermute | solution.py:27
  14.5 5.2 %collective-permute-start.3 = (f32[5,20,2,128]{3,2,1,0:T(2,128)S(1)}, f32[5,20,2,128]{3,2,1,0:T(2,128)S(1)}, u32[]{:S(2)}, u32[]{:S(2)}) collective-permute-start(f32[5,20,2,128]{3,2,1,0:T(2,128)S(1)} %get-tuple-element.36), channel_id=1, source_target_pairs={{1,0},{2,1},{3,2},{0,3},{5,4},{6,5},{7,6},{4,7},{9,8},{10,9},{11,1... | collective-permute-start | bytes 307208 | tf_op jit(solution)/shard_map/ppermute | solution.py:28
  22.7 1.3 %copy-start.1 = (f32[5,17,33,128]{3,2,1,0:T(8,128)}, f32[5,17,33,128]{3,2,1,0:T(8,128)S(1)}, u32[]{:S(2)}) copy-start(f32[5,17,33,128]{3,2,1,0:T(8,128)S(1)} %multiply_add_fusion) | copy-start | bytes 4308484
  24.8 14.3 %copy-start.2 = (f32[5,17,33,128]{3,2,1,0:T(8,128)S(1)}, f32[5,17,33,128]{3,2,1,0:T(8,128)}, u32[]{:S(2)}) copy-start(f32[5,17,33,128]{3,2,1,0:T(8,128)} %copy-done.1) | copy-start | bytes 4308484
  29.9 10.1 %copy-start.5 = (f32[17,33,128]{2,1,0:T(8,128)S(1)}, f32[17,33,128]{2,1,0:T(8,128)}, u32[]{:S(2)}) copy-start(f32[17,33,128]{2,1,0:T(8,128)} %get-tuple-element.35) | copy-start | bytes 861700
  34.1 12.8 %collective-permute-start.6 = (f32[5,64,1,8]{1,3,2,0:T(8,128)}, f32[5,64,1,8]{1,3,2,0:T(8,128)S(1)}, u32[]{:S(2)}, u32[]{:S(2)}) collective-permute-start(f32[5,64,1,8]{1,3,2,0:T(8,128)} %get-tuple-element.53), channel_id=1, source_target_pairs={{0,4},{4,8},{8,12},{12,16},{16,20},{20,24},{24,28},{28,0},{1,5},{5... | collective-permute-start | bytes 30728 | tf_op jit(solution)/shard_map/ppermute | solution.py:27
  34.4 12.5 %collective-permute-start.7 = (f32[5,64,1,8]{1,3,2,0:T(8,128)}, f32[5,64,1,8]{1,3,2,0:T(8,128)S(1)}, u32[]{:S(2)}, u32[]{:S(2)}) collective-permute-start(f32[5,64,1,8]{1,3,2,0:T(8,128)} %get-tuple-element.54), channel_id=1, source_target_pairs={{4,0},{8,4},{12,8},{16,12},{20,16},{24,20},{28,24},{0,28},{5,1},{9... | collective-permute-start | bytes 30728 | tf_op jit(solution)/shard_map/ppermute | solution.py:28
  41.3 5.5 %copy-start.8 = (f32[1,64,32]{1,2,0:T(8,128)S(1)}, f32[1,64,32]{1,2,0:T(8,128)}, u32[]{:S(2)}) copy-start(f32[1,64,32]{1,2,0:T(8,128)} %get-tuple-element.17) | copy-start | bytes 24580
  41.3 5.5 %copy-start.9 = (f32[1,64,32]{1,2,0:T(8,128)S(1)}, f32[1,64,32]{1,2,0:T(8,128)}, u32[]{:S(2)}) copy-start(f32[1,64,32]{1,2,0:T(8,128)} %multiply_bitcast_fusion) | copy-start | bytes 24580
  41.3 5.5 %copy-start.10 = (f32[64,32]{0,1:T(8,128)S(1)}, f32[64,32]{0,1:T(8,128)}, u32[]{:S(2)}) copy-start(f32[64,32]{0,1:T(8,128)} %get-tuple-element.14) | copy-start | bytes 24580
  44.0 13.4 %all-to-all-start = ((f32[32,1,2048]{2,1,0:T(1,128)}), f32[32,1,2048]{2,1,0:T(1,128)S(1)}, u32[]{:S(2)}, u32[]{:S(2)}) async-start(f32[32,1,2048]{2,1,0:T(1,128)} %reshape.351), calls=%async_computation | async-start | bytes 524288 | tf_op jit(solution)/shard_map/all_to_all | solution.py:144
  47.0 3.2 %collective-permute-start.8 = (f32[5,64,6,1]{1,3,2,0:T(1,128)S(1)}, f32[5,64,6,1]{1,3,2,0:T(1,128)S(1)}, u32[]{:S(2)}, u32[]{:S(2)}) collective-permute-start(f32[5,64,6,1]{1,3,2,0:T(1,128)S(1)} %get-tuple-element.49), channel_id=1, source_target_pairs={{1,0},{2,1},{3,2},{0,3},{5,4},{6,5},{7,6},{4,7},{9,8},{10,9},{11,1... | collective-permute-start | bytes 23048 | tf_op jit(solution)/shard_map/ppermute | solution.py:28
  48.5 3.4 %collective-permute-start.9 = (f32[5,64,6,1]{1,3,2,0:T(1,128)S(1)}, f32[5,64,6,1]{1,3,2,0:T(1,128)S(1)}, u32[]{:S(2)}, u32[]{:S(2)}) collective-permute-start(f32[5,64,6,1]{1,3,2,0:T(1,128)S(1)} %get-tuple-element.50), channel_id=1, source_target_pairs={{0,1},{1,2},{2,3},{3,0},{4,5},{5,6},{6,7},{7,4},{8,9},{9,10},{10,1... | collective-permute-start | bytes 23048 | tf_op jit(solution)/shard_map/ppermute | solution.py:27
  59.6 5.5 %copy-start.7 = (f32[128,128]{1,0:T(8,128)S(1)}, f32[128,128]{1,0:T(8,128)}, u32[]{:S(2)}) copy-start(f32[128,128]{1,0:T(8,128)} %broadcast_add_fusion) | copy-start | bytes 196612
  59.7 5.5 %copy-start.21 = (pred[128]{0:T(512)(128)(4,1)S(1)}, pred[128]{0:T(512)(128)(4,1)}, u32[]{:S(2)}) copy-start(pred[128]{0:T(512)(128)(4,1)} %copy-done.20) | copy-start | bytes 388
  59.7 5.5 %copy-start.22 = (pred[4,128]{1,0:T(4,128)(4,1)S(1)}, pred[4,128]{1,0:T(4,128)(4,1)}, u32[]{:S(2)}) copy-start(pred[4,128]{1,0:T(4,128)(4,1)} %broadcast_and_fusion) | copy-start | bytes 1540
  59.7 5.5 %copy-start.23 = (f32[4]{0:T(128)S(1)}, f32[4]{0:T(128)}, u32[]{:S(2)}) copy-start(f32[4]{0:T(128)} %multiply_add_fusion.1) | copy-start | bytes 52
  72.8 4.0 %copy-start.11 = (f32[64,4,8]{0,2,1:T(8,128)S(1)}, f32[64,4,8]{0,2,1:T(8,128)}, u32[]{:S(2)}) copy-start(f32[64,4,8]{0,2,1:T(8,128)} %get-tuple-element.46) | copy-start | bytes 24580
  72.8 5.0 %copy-start.6 = (f32[5,64,6,9]{1,3,2,0:T(8,128)S(1)}, f32[5,64,6,9]{1,3,2,0:T(8,128)}, u32[]{:S(2)}) copy-start(f32[5,64,6,9]{1,3,2,0:T(8,128)} %get-tuple-element.47) | copy-start | bytes 207364
  72.8 5.0 %copy-start.12 = (f32[64,4,8]{0,2,1:T(8,128)S(1)}, f32[64,4,8]{0,2,1:T(8,128)}, u32[]{:S(2)}) copy-start(f32[64,4,8]{0,2,1:T(8,128)} %get-tuple-element.41) | copy-start | bytes 24580
  72.8 5.0 %copy-start.13 = (f32[64,4,8]{0,2,1:T(8,128)S(1)}, f32[64,4,8]{0,2,1:T(8,128)}, u32[]{:S(2)}) copy-start(f32[64,4,8]{0,2,1:T(8,128)} %get-tuple-element.42) | copy-start | bytes 24580
  74.1 13.2 %all-to-all-start.1 = ((f32[32,1,2048]{2,1,0:T(1,128)}), f32[32,1,2048]{2,1,0:T(1,128)S(1)}, u32[]{:S(2)}, u32[]{:S(2)}) async-start(f32[32,1,2048]{2,1,0:T(1,128)} %reshape.353), calls=%async_computation.1 | async-start | bytes 524288 | tf_op jit(solution)/shard_map/all_to_all | solution.py:158
  77.8 15.6 %copy-start.16 = (f32[3,32]{1,0:T(4,128)S(1)}, f32[3,32]{1,0:T(4,128)}, u32[]{:S(2)}) copy-start(f32[3,32]{1,0:T(4,128)} %reduce_sum.148) | copy-start | bytes 1156
  91.8 3.8 %collective-permute-start.4 = (f32[1,32,128]{2,1,0:T(8,128)S(1)}, f32[1,32,128]{2,1,0:T(8,128)S(1)}, u32[]{:S(2)}, u32[]{:S(2)}) collective-permute-start(f32[1,32,128]{2,1,0:T(8,128)S(1)} %slice.345), channel_id=1, source_target_pairs={{4,0},{8,4},{12,8},{16,12},{20,16},{24,20},{28,24},{0,28},{5,1},{9... | collective-permute-start | bytes 49160 | tf_op jit(solution)/shard_map/ppermute | solution.py:36
  93.3 1.6 %collective-permute-start.5 = (f32[16,1,128]{2,1,0:T(1,128)S(1)}, f32[16,1,128]{2,1,0:T(1,128)S(1)}, u32[]{:S(2)}, u32[]{:S(2)}) collective-permute-start(f32[16,1,128]{2,1,0:T(1,128)S(1)} %slice.348), channel_id=1, source_target_pairs={{1,0},{2,1},{3,2},{0,3},{5,4},{6,5},{7,6},{4,7},{9,8},{10,9},{11,1... | collective-permute-start | bytes 24584 | tf_op jit(solution)/shard_map/ppermute | solution.py:36
where the time goes:
time: 97.6 us; the launch traced here: 96.7 us
  other arithmetic  24.9 us (26%)
  starting transfers between devices  21.3 us (22%)
  waiting for transfers between devices  18.2 us (19%)
  matrix products  17.5 us (18%)
  local copies, waits for them, and re-layouts  13.6 us (14%)
  between operations  1.26 us (1%)
    ppermute x4, starting transfers between devices, extended(): after = lax.ppermute(initial, axis, down)  10.8 us
    all_to_all x1, waiting for transfers between devices, shards(): lax.all_to_all(single, ('gx', 'gy'), split_axis=2, concat_axis=1, tiled=T...  8.99 us
    unnamed x53, local copies, waits for them, and re-layouts  4.2 us
    all_to_all x1, waiting for transfers between devices, shards(): lax.all_to_all(spectral, ('gx', 'gy'), split_axis=0, concat_axis=1, tiled...  3.98 us
    ppermute x4, starting transfers between devices, extended(): before = lax.ppermute(last, axis, up)  3.34 us
    ppermute x4, waiting for transfers between devices, extended(): before = lax.ppermute(last, axis, up)  3.06 us
    add x1, other arithmetic, advect_fields(): return centre + TIME_STEP * (carried + DIFFUSION * spread)  2.93 us
    all_to_all x1, starting transfers between devices, shards(): lax.all_to_all(spectral, ('gx', 'gy'), split_axis=0, concat_axis=1, tiled...  2.81 us
  transfers between devices with their start and end apart: 12, of which 8 were waited for; matrix products, arithmetic and copies ran while one was open for 19% of the time, Pallas kernels for 0%

commit v1 on v0

v1 whole, which is shorter than its diff:
```python
import functools
import math

import jax
import jax.numpy as jnp
import ml_dtypes
import numpy as np
from jax import lax
from jax.experimental import pallas as pl
from jax.experimental.pallas import tpu as pltpu
from jax.sharding import PartitionSpec as P

BW = 4
LANES = 128

TIME_STEP = 0.2
DIFFUSION = 0.05
BUOYANCY = 0.5
GROWTH = 0.5
COLLISION = 0.05
CONDENSE = 0.002

VMEM = pl.BlockSpec(memory_space=pltpu.VMEM)
PARAMS = pltpu.CompilerParams(vmem_limit_bytes=24 * 2**20)
NT = (((1,), (1,)), ((), ()))
TN = (((0,), (0,)), ((), ()))
NN = (((1,), (0,)), ((), ()))

KINDS = [(sx, sy) for sx in (-1, 0, 1) for sy in (-1, 0, 1) if (sx, sy) != (0, 0)]


def halves(table):
    high = table.astype(np.float32).astype(ml_dtypes.bfloat16)
    low = (table - high.astype(np.float64)).astype(np.float32).astype(ml_dtypes.bfloat16)
    return high, low


def split(value):
    high = value.astype(jnp.bfloat16)
    return high, (value - high.astype(jnp.float32)).astype(jnp.bfloat16)


def dot3(left, right, dims=NN):
    (lh, ll), (rh, rl) = left, right
    dot = functools.partial(
        lax.dot_general, dimension_numbers=dims, preferred_element_type=jnp.float32
    )
    return dot(lh, rh) + (dot(ll, rh) + dot(lh, rl))


def real_basis(length):
    position = np.arange(length)[:, None]
    column = np.arange(length)
    wave = np.where(column <= length // 2, column, column - length // 2)
    angle = 2.0 * np.pi * ((position * wave[None, :]) % length) / length
    table = np.where(column[None, :] <= length // 2, np.cos(angle), np.sin(angle))
    table = table * np.sqrt(2.0 / length)
    table[:, 0] *= np.sqrt(0.5)
    if length % 2 == 0:
        table[:, length // 2] *= np.sqrt(0.5)
    return table, -4.0 * np.sin(np.pi * wave / length) ** 2


class Plan:
    def __init__(self, grid_x, grid_y, span_x, span_y, levels, slots):
        self.gx, self.gy = grid_x, grid_y
        self.sx, self.sy, self.nz = span_x, span_y, levels
        self.nd = grid_x * grid_y
        self.per = levels // self.nd
        self.x4 = LANES // span_y
        self.xg = span_x // self.x4
        self.main = self.per * self.xg
        self.rows1 = self.main + 2
        self.rows2 = self.main + 3
        self.tx, self.ty = grid_x * span_x, grid_y * span_y
        self.bx, self.by = span_x // BW, span_y // BW
        self.boxes = self.bx * self.by
        self.slots = slots

    def tables(self):
        nd, per, nz = self.nd, self.per, self.nz
        z = np.arange(nz)
        cosine = np.cos(np.pi / nz * (((2 * z[:, None] + 1) * z[None, :]) % (4 * nz)) / 2.0)
        mode = (np.arange(nd)[None, :] * per + np.arange(per)[:, None]).reshape(-1)
        forward = cosine.T[mode]
        weight = np.where(np.arange(nz) == 0, 1.0, 2.0) / nz
        backward = forward * weight[mode][:, None]
        qx, ex = real_basis(self.tx)
        qy, ey = real_basis(self.ty)
        q1 = qx.reshape(self.gx, self.xg, self.x4, self.tx)
        q1 = q1.transpose(3, 2, 1, 0).reshape(self.tx, self.tx)
        w = np.einsum("byk,pq->bpyqk", qy.reshape(self.gy, self.sy, self.ty), np.eye(self.x4))
        w = w.reshape(self.gy * LANES, self.x4 * self.ty)
        ez = -4.0 * np.sin(np.pi * z / (2 * nz)) ** 2
        return forward, backward, q1, w, ex, ey, ez


def neighbours(count):
    first = [(i, i ^ 1) for i in range(count)]
    second = [(i, (i + 1) % count if i % 2 else (i - 1) % count) for i in range(count)]
    return first, second


def edges_kernel(plan, vel, theta, vapour, xa, xb, ya, yb):
    odd_x = lax.axis_index("gx") % 2 == 1
    odd_y = lax.axis_index("gy") % 2 == 1
    fields = [(vel, i) for i in range(3)] + [(theta, None), (vapour, None)]
    for f, (ref, i) in enumerate(fields):
        at = (lambda x, ref=ref, i=i: ref[x] if i is None else ref[i, x])
        first, last = at(0), at(plan.sx - 1)
        xa[f] = jnp.where(odd_x, first, last)
        xb[f] = jnp.where(odd_x, last, first)
        for x in range(plan.sx):
            if i is None:
                south, north = ref[x, 0:1], ref[x, plan.sy - 1 : plan.sy]
            else:
                south, north = ref[i, x, 0:1], ref[i, x, plan.sy - 1 : plan.sy]
            ya[f, x : x + 1] = jnp.where(odd_y, south, north)
            yb[f, x : x + 1] = jnp.where(odd_y, north, south)


def edge_masks(plan):
    row = lax.broadcasted_iota(jnp.int32, (plan.sy, plan.nz), 0)
    lane = lax.broadcasted_iota(jnp.int32, (plan.sy, plan.nz), 1)
    return row == 0, row == plan.sy - 1, lane == 0, lane == plan.nz - 1


def coefficients(u, v, w):
    half = 0.5 * TIME_STEP
    side = TIME_STEP * DIFFUSION
    return (
        side - half * u, side + half * u,
        side - half * v, side + half * v,
        side - half * w, side + half * w,
    )


def advect(c, east, west, north_row, south_row, coef, masks, plan):
    row0, row_last, lane0, lane_last = masks
    north = jnp.where(row_last, north_row, pltpu.roll(c, plan.sy - 1, 0))
    south = jnp.where(row0, south_row, pltpu.roll(c, 1, 0))
    upper = jnp.where(lane_last, c, pltpu.roll(c, plan.nz - 1, 1))
    lower = jnp.where(lane0, c, pltpu.roll(c, 1, 1))
    ce, cw, cn, cs, cu, cl = coef
    return (
        (1.0 - 6.0 * TIME_STEP * DIFFUSION) * c
        + (ce * east + cw * west)
        + (cn * north + cs * south)
        + (cu * upper + cl * lower)
    )


def side_planes(xa, xb, f):
    odd = lax.axis_index("gx") % 2 == 1
    return jnp.where(odd, xa[f], xb[f]), jnp.where(odd, xb[f], xa[f])


def side_rows(ya, yb, f):
    odd = lax.axis_index("gy") % 2 == 1
    return jnp.where(odd, ya[f], yb[f]), jnp.where(odd, yb[f], ya[f])


def wind_kernel(plan, vel, theta, xa, xb, ya, yb, fh, fl, star, out):
    masks = edge_masks(plan)
    table = (fh[...], fl[...])
    west_of, east_of, south_of, north_of = [], [], [], []
    for f in range(3):
        west, east = side_planes(xa, xb, f)
        south, north = side_rows(ya, yb, f)
        west_of.append(west)
        east_of.append(east)
        south_of.append(south)
        north_of.append(north)
    row0, _, lane0, _ = masks
    last_u = None
    slab = []
    last_rows = []
    for x in range(plan.sx):
        coef = coefficients(vel[0, x], vel[1, x], vel[2, x])
        s = []
        for f in range(3):
            west = vel[f, x - 1] if x else west_of[f]
            east = vel[f, x + 1] if x < plan.sx - 1 else east_of[f]
            s.append(
                advect(
                    vel[f, x], east, west, north_of[f][x : x + 1], south_of[f][x : x + 1],
                    coef, masks, plan,
                )
            )
        s[2] = s[2] + (TIME_STEP * BUOYANCY) * theta[x]
        for f in range(3):
            star[f, x] = s[f]
        div = s[0] if last_u is None else s[0] - last_u
        div = div + (s[1] - jnp.where(row0, 0.0, pltpu.roll(s[1], 1, 0)))
        div = div + (s[2] - jnp.where(lane0, 0.0, pltpu.roll(s[2], 1, 1)))
        last_u = s[0]
        last_rows.append(s[1][plan.sy - 1 : plan.sy])
        slab.append(div)
        if len(slab) == plan.x4:
            g = x // plan.x4
            modes = dot3(table, split(jnp.concatenate(slab, axis=0)), NT)
            for j in range(plan.per):
                out[pl.ds(j * plan.xg + g, plan.nd, stride=plan.rows1), :] = modes[
                    j * plan.nd : (j + 1) * plan.nd
                ]
            slab = []
    tiled_plane = jnp.concatenate([-last_u] * plan.x4, axis=0)
    row = lax.broadcasted_iota(jnp.int32, (plan.sy, plan.nz), 0)
    tiled_rows = []
    for p in range(plan.x4):
        block = jnp.zeros((plan.sy, plan.nz), jnp.float32)
        for g in range(plan.xg):
            block = jnp.where(row % plan.xg == g, -last_rows[g * plan.x4 + p], block)
        tiled_rows.append(block)
    extra = dot3(table, split(jnp.concatenate([tiled_plane] + tiled_rows, axis=0)), NT)
    lane = lax.broadcasted_iota(jnp.int32, (plan.nd, LANES), 1)
    plane_sum = jnp.zeros((plan.nd, LANES), jnp.float32)
    row_sum = jnp.zeros((plan.nd, LANES), jnp.float32)
    for j in range(plan.per):
        part = extra[j * plan.nd : (j + 1) * plan.nd]
        plane_sum = jnp.where(lane // plan.sy == j, part[:, :LANES], plane_sum)
        row_sum = jnp.where(lane % plan.sy // plan.xg == j, part[:, LANES:], row_sum)
    out[pl.ds(plan.main, plan.nd, stride=plan.rows1), :] = plane_sum
    out[pl.ds(plan.main + 1, plan.nd, stride=plan.rows1), :] = row_sum


def solve_kernel(plan, r, inverse, leave, wh, wl, th, tl, qh, ql, qth, qtl, out):
    gx, gy, per, xg, x4 = plan.gx, plan.gy, plan.per, plan.xg, plan.x4
    lane = lax.broadcasted_iota(jnp.int32, (gx, LANES), 1)
    first_lanes = lane < plan.sy
    first_rows = lane % plan.sy == 0
    step1, step2 = gy * plan.rows1, gy * plan.rows2

    def take(b, q):
        return r[pl.ds(b * plan.rows1 + q, gx, stride=step1), :]

    blocks = [[take(b, q) for q in range(plan.main)] for b in range(gy)]
    for b in range(gy):
        plane = pltpu.roll(take(b, plan.main), 1, 0)
        for j in range(per):
            moved = plane if j == 0 else pltpu.roll(plane, LANES - j * plan.sy, 1)
            blocks[b][j * xg] = blocks[b][j * xg] + jnp.where(first_lanes, moved, 0.0)
        rows = take(b, plan.main + 1)
        for q in range(plan.main):
            moved = rows if q == 0 else pltpu.roll(rows, LANES - q, 1)
            nb = (b + 1) % gy
            blocks[nb][q] = blocks[nb][q] + jnp.where(first_rows, moved, 0.0)
    grid = jnp.concatenate([jnp.concatenate(column, axis=0) for column in blocks], axis=1)
    in_y = dot3(split(grid), (wh[...], wl[...]))
    height = xg * gx

    def swap(value, outer, inner):
        return jnp.concatenate(
            [
                jnp.concatenate(
                    [
                        value[o * height : (o + 1) * height, i * plan.ty : (i + 1) * plan.ty]
                        for o in range(outer)
                    ],
                    axis=1,
                )
                for i in range(inner)
            ],
            axis=0,
        )

    spectral = dot3((qh[...], ql[...]), split(swap(in_y, per, x4)))
    solved = spectral * inverse[...]
    in_x = dot3((qth[...], qtl[...]), split(solved))
    grid = dot3(split(swap(in_x, x4, per)), (th[...], tl[...]))
    planes = [jnp.zeros((gx, LANES), jnp.float32) for _ in range(gy)]
    rows = [jnp.zeros((gx, LANES), jnp.float32) for _ in range(gy)]
    for b in range(gy):
        for q in range(plan.main):
            block = grid[q * gx : (q + 1) * gx, b * LANES : (b + 1) * LANES]
            out[pl.ds(b * plan.rows2 + q, gx, stride=step2), :] = block
            moved = jnp.where(first_rows, block, 0.0)
            nb = (b - 1) % gy
            rows[nb] = rows[nb] + (moved if q == 0 else pltpu.roll(moved, q, 1))
            if q % xg == 0:
                j = q // xg
                moved = jnp.where(first_lanes, block, 0.0)
                planes[b] = planes[b] + (moved if j == 0 else pltpu.roll(moved, j * plan.sy, 1))
    for b in range(gy):
        out[pl.ds(b * plan.rows2 + plan.main, gx, stride=step2), :] = pltpu.roll(
            planes[b], gx - 1, 0
        )
        out[pl.ds(b * plan.rows2 + plan.main + 1, gx, stride=step2), :] = rows[b]
    out[pl.ds(plan.main + 2, plan.nd, stride=plan.rows2), :] = leave[...]


def project_kernel(plan, r, star, stay, bh, bl, place, vel_new, moments, scratch):
    nd, per, xg, x4, sy, sx = plan.nd, plan.per, plan.xg, plan.x4, plan.sy, plan.sx
    table = (bh[...], bl[...])
    lane = lax.broadcasted_iota(jnp.int32, (nd, LANES), 1)

    def take(q):
        return r[pl.ds(q, nd, stride=plan.rows2), :]

    planes, rows = take(plan.main), take(plan.main + 1)
    wide = jnp.concatenate(
        [
            jnp.concatenate([jnp.where(lane // sy == j, planes, 0.0) for j in range(per)], axis=0),
            jnp.concatenate(
                [jnp.where(lane % sy // xg == j, rows, 0.0) for j in range(per)], axis=0
            ),
        ],
        axis=1,
    )
    extra = dot3(split(wide), table, TN)
    beyond = extra[0:sy]
    for j in range(1, per):
        beyond = beyond + extra[j * sy : (j + 1) * sy]
    scratch[...] = extra[LANES:]
    row = lax.broadcasted_iota(jnp.int32, (sy, plan.nz), 0)
    level = lax.broadcasted_iota(jnp.int32, (sy, plan.nz), 1)
    pressure = []
    for g in range(xg):
        modes = jnp.concatenate([take(j * xg + g) for j in range(per)], axis=0)
        slab = dot3(split(modes), table, TN)
        pressure += [slab[p * sy : (p + 1) * sy] for p in range(x4)]
    pressure.append(beyond)
    for x in range(sx):
        here = pressure[x]
        g, p = x // x4, x % x4
        last = scratch[p * sy + g : p * sy + g + 1]
        for j in range(1, per):
            last = last + scratch[p * sy + j * xg + g : p * sy + j * xg + g + 1]
        north = jnp.where(row == sy - 1, last, pltpu.roll(here, sy - 1, 0))
        upper = jnp.where(level == plan.nz - 1, here, pltpu.roll(here, plan.nz - 1, 1))
        vel_new[0, x] = star[0, x] - (pressure[x + 1] - here)
        vel_new[1, x] = star[1, x] - (north - here)
        vel_new[2, x] = star[2, x] - (upper - here)
    came = jnp.sum(take(plan.main + 2), axis=0, keepdims=True)
    load = lax.broadcasted_iota(jnp.int32, (8, LANES), 0)
    at = lax.broadcasted_iota(jnp.int32, (8, LANES), 1)
    width = payload_width(plan)
    loads = jnp.where(at // width == load, came, 0.0)
    total = stay[...] + lax.dot_general(
        loads, place[...], NN, precision=lax.Precision.HIGHEST, preferred_element_type=jnp.float32
    )
    moments[...] = total[:3, : plan.boxes] * (1.0 / plan.slots)


def payload_width(plan):
    return 2 * plan.by + 2 * plan.bx + 4


def droplet_tables(plan):
    bx, by, boxes = plan.bx, plan.by, plan.boxes
    width = payload_width(plan)
    lane_of = {}
    kind_of = np.full((LANES,), -1)
    place = np.zeros((LANES, LANES), np.float32)
    for k, (sx, sy) in enumerate(KINDS):
        xs = range(bx) if sx == 0 else [0 if sx > 0 else bx - 1]
        ys = range(by) if sy == 0 else [0 if sy > 0 else by - 1]
        for x in xs:
            for y in ys:
                lane_of[k, x, y] = len(lane_of)
    assert len(lane_of) == width and 3 * width <= LANES
    for (k, x, y), at in lane_of.items():
        for load in range(3):
            kind_of[load * width + at] = k
            place[load * width + at, x * by + y] = 1.0
    here = np.zeros((9 * boxes, LANES), np.float32)
    away = np.zeros((3, 9 * boxes, LANES), np.float32)
    for dx in (-1, 0, 1):
        for dy in (-1, 0, 1):
            code = (dx + 1) * 3 + dy + 1
            for x in range(bx):
                for y in range(by):
                    line = code * boxes + x * by + y
                    sx = (x + dx) // bx
                    sy = (y + dy) // by
                    tx, ty = (x + dx) % bx, (y + dy) % by
                    if (sx, sy) == (0, 0):
                        here[line, tx * by + ty] = 1.0
                    else:
                        at = lane_of[KINDS.index((sx, sy)), tx, ty]
                        for load in range(3):
                            away[load, line, load * width + at] = 1.0
    return here, away, place, kind_of


def scalar_kernel(
    plan, vel, theta, vapour, xa, xb, ya, yb, drops, order, here, away, target,
    theta_new, vapour_new, stay, leave, moist,
):
    masks = edge_masks(plan)
    bx, by, boxes = plan.bx, plan.by, plan.boxes
    edges = []
    for f in (3, 4):
        west, east = side_planes(xa, xb, f)
        south, north = side_rows(ya, yb, f)
        edges.append((west, east, south, north))
    sums = []
    total = None
    for x in range(plan.sx):
        coef = coefficients(vel[0, x], vel[1, x], vel[2, x])
        for ref, new, (west, east, south, north) in (
            (theta, theta_new, edges[0]),
            (vapour, moist, edges[1]),
        ):
            moved = advect(
                ref[x],
                ref[x + 1] if x < plan.sx - 1 else east,
                ref[x - 1] if x else west,
                north[x : x + 1], south[x : x + 1], coef, masks, plan,
            )
            new[x] = moved
        total = moved if x % BW == 0 else total + moved
        if x % BW == BW - 1:
            sums.append(jnp.sum(total, axis=1, keepdims=True))
    exact = functools.partial(
        lax.dot_general, dimension_numbers=NN, precision=lax.Precision.HIGHEST,
        preferred_element_type=jnp.float32,
    )
    gather_y = (
        lax.broadcasted_iota(jnp.int32, (by, plan.sy), 1) // BW
        == lax.broadcasted_iota(jnp.int32, (by, plan.sy), 0)
    ).astype(jnp.float32)
    spread_y = (
        lax.broadcasted_iota(jnp.int32, (plan.sy, by), 0) // BW
        == lax.broadcasted_iota(jnp.int32, (plan.sy, by), 1)
    ).astype(jnp.float32)
    means = jnp.concatenate(
        [exact(gather_y, jnp.broadcast_to(s, (plan.sy, LANES))) for s in sums], axis=0
    ) * (1.0 / (BW * BW * plan.nz))
    softplus = jnp.maximum(means, 0.0) + jnp.log(1.0 + jnp.exp(-jnp.abs(means)))
    index = order[...]

    def gather(value):
        return jnp.take_along_axis(value, index, axis=1, mode="promise_in_bounds")

    radius_sq = gather(drops[0])
    live = gather(drops[1])
    code = gather(drops[2])
    grown_sq = radius_sq + GROWTH * softplus
    root = jnp.sqrt(grown_sq)
    mass = grown_sq * root
    lane = lax.broadcasted_iota(jnp.int32, (boxes, LANES), 1)
    own = lane < plan.slots
    condensed = jnp.sum(
        jnp.where(own, live * (mass - radius_sq * jnp.sqrt(radius_sq)), 0.0),
        axis=1, keepdims=True,
    )
    condensed = jnp.broadcast_to(condensed, (boxes, LANES))
    for big in range(bx):
        less = CONDENSE * exact(spread_y, condensed[big * by : (big + 1) * by])
        for x in range(big * BW, (big + 1) * BW):
            vapour_new[x] = moist[x] - less

    def partner(value):
        return pltpu.roll(value, LANES - plan.slots, 1)

    other_grown, other_root, other_mass = partner(grown_sq), partner(root), partner(mass)
    both = root + other_root
    rate = both * both * jnp.abs(grown_sq - other_grown) * partner(live)
    final = (mass + COLLISION * rate * other_mass) / (1.0 + COLLISION * rate)
    weight = jnp.where(own, live, 0.0)
    loads = (weight, weight * final, weight * final * final)
    parts = [[], [], []]
    for direction in range(9):
        chosen = code == float(direction)
        for k in range(3):
            parts[k].append(
                jnp.sum(jnp.where(chosen, loads[k], 0.0), axis=1, keepdims=True)
            )
    payload = jnp.zeros((1, LANES), jnp.float32)
    stays = jnp.zeros((8, LANES), jnp.float32)
    line = lax.broadcasted_iota(jnp.int32, (8, LANES), 0)
    for k in range(3):
        column = jnp.concatenate(parts[k], axis=0)
        payload = payload + jnp.sum(column * away[k], axis=0, keepdims=True)
        stays = jnp.where(line == k, jnp.sum(column * here[...], axis=0, keepdims=True), stays)
    stay[...] = stays
    leave[...] = payload * target[...]


def call(body, outs, args, flops, scratch=()):
    moved = sum(a.size * a.dtype.itemsize for a in args)
    moved += sum(math.prod(o) * 4 for o in outs)
    return pl.pallas_call(
        body,
        out_shape=[jax.ShapeDtypeStruct(o, jnp.float32) for o in outs],
        in_specs=[VMEM] * len(args),
        out_specs=[VMEM] * len(outs),
        scratch_shapes=list(scratch),
        compiler_params=PARAMS,
        cost_estimate=pl.CostEstimate(flops=flops, bytes_accessed=moved, transcendentals=0),
    )(*args)


def swap(block, axis):
    first, second = neighbours(lax.axis_size(axis))
    return (lambda a, b: (lax.ppermute(a, axis, first), lax.ppermute(b, axis, second)))(*block)


def exchange(chunks, plan, rows):
    flat = chunks.reshape(plan.nd, 1, rows * LANES)
    flat = lax.all_to_all(flat, ("gx", "gy"), split_axis=0, concat_axis=0, tiled=True)
    return flat.reshape(plan.nd * rows, LANES)


def shards(velocity, theta, vapour, radius_sq, multiplicity, counts, pairing, destination):
    span_x, span_y, levels = theta.shape
    slots = radius_sq.shape[0]
    plan = Plan(lax.axis_size("gx"), lax.axis_size("gy"), span_x, span_y, levels, slots)
    rank_x, rank_y = lax.axis_index("gx"), lax.axis_index("gy")
    rank = rank_x * plan.gy + rank_y
    forward, backward, q1, w, ex, ey, ez = plan.tables()
    here, away, place, kind_of = droplet_tables(plan)
    block = (span_x, span_y, levels)
    cells = math.prod(block)

    plane, rows = (5, span_y, levels), (5, span_x, levels)
    xa, xb, ya, yb = call(
        functools.partial(edges_kernel, plan),
        (plane, plane, rows, rows), (velocity, theta, vapour), cells,
    )
    xa, xb = swap((xa, xb), "gx")
    ya, yb = swap((ya, yb), "gy")

    box = jnp.arange(plan.boxes)
    source_x = rank_x * plan.bx + box // plan.by
    source_y = rank_y * plan.by + box % plan.by
    device, local = destination // plan.boxes, destination % plan.boxes
    target_x = device // plan.gy * plan.bx + local // plan.by
    target_y = device % plan.gy * plan.by + local % plan.by
    offset_x = (target_x - source_x[None, :] + 1) % (plan.bx * plan.gx)
    offset_y = (target_y - source_y[None, :] + 1) % (plan.by * plan.gy)
    live = jnp.where(jnp.arange(slots)[:, None] < counts[None, :], multiplicity, 0.0)
    drops = jnp.stack([radius_sq, live, (offset_x * 3 + offset_y).astype(jnp.float32)])
    drops = jnp.pad(jnp.swapaxes(drops, 1, 2), ((0, 0), (0, 0), (0, LANES - slots)))
    order = jnp.concatenate([pairing, jnp.roll(pairing, slots // 2, axis=1)], axis=1)
    every = jnp.arange(plan.nd)
    target = jnp.zeros((plan.nd, LANES), jnp.float32)
    for k, (sx, sy) in enumerate(KINDS):
        to = (rank_x + sx) % plan.gx * plan.gy + (rank_y + sy) % plan.gy
        target = target + ((every == to)[:, None] & (kind_of == k)[None, :]).astype(jnp.float32)

    star, chunks = call(
        functools.partial(wind_kernel, plan),
        ((3,) + block, (plan.nd * plan.rows1, LANES)),
        (velocity, theta, xa, xb, ya, yb) + halves(forward),
        100 * cells,
    )
    spectral = exchange(chunks, plan, plan.rows1)

    theta_new, vapour_new, stay, leave = call(
        functools.partial(scalar_kernel, plan),
        (block, block, (8, LANES), (plan.nd, LANES)),
        (velocity, theta, vapour, xa, xb, ya, yb, drops, order, here, away, target),
        100 * cells,
        (pltpu.VMEM(block, jnp.float32),),
    )

    modes = lax.dynamic_slice(jnp.asarray(ez, jnp.float32), (rank * plan.per,), (plan.per,))
    eigen = (
        jnp.asarray(ex, jnp.float32)[:, None, None]
        + jnp.asarray(ey, jnp.float32)[None, None, :]
        + modes[None, :, None]
    ).reshape(plan.tx, plan.per * plan.ty)
    inverse = jnp.where(eigen == 0.0, 0.0, 1.0 / jnp.where(eigen == 0.0, 1.0, eigen))
    (chunks,) = call(
        functools.partial(solve_kernel, plan),
        ((plan.nd * plan.rows2, LANES),),
        (spectral, inverse, leave) + halves(w) + halves(w.T) + halves(q1) + halves(q1.T),
        1000 * cells,
    )
    modal = exchange(chunks, plan, plan.rows2)

    velocity_new, moments = call(
        functools.partial(project_kernel, plan),
        ((3,) + block, (3, plan.boxes)),
        (modal, star, stay) + halves(backward) + (place,),
        100 * cells,
        (pltpu.VMEM((LANES, levels), jnp.float32),),
    )
    return (velocity_new, theta_new, vapour_new, moments)


def solution(mesh):
    placed = (
        P(None, "gx", "gy", None),
        P("gx", "gy", None),
        P("gx", "gy", None),
        P(None, ("gx", "gy")),
        P(None, ("gx", "gy")),
        P(("gx", "gy")),
        P(("gx", "gy"), None),
        P(None, ("gx", "gy")),
    )
    return jax.shard_map(
        shards,
        mesh=mesh,
        in_specs=placed,
        out_specs=(
            P(None, "gx", "gy", None),
            P("gx", "gy", None),
            P("gx", "gy", None),
            P(None, ("gx", "gy")),
        ),
        check_vma=False,
    )
```

time: 97.6 us -> 55.9 us (0.57)
  other arithmetic: 24.9 us -> 0.51 us
  matrix products: 17.5 us -> 0 us
  blocking collectives: 0 us -> 13.8 us
  waiting for transfers between devices: 18.2 us -> 7.06 us
  starting transfers between devices: 21.3 us -> 12.2 us
  Pallas kernels: 0 us -> 6.36 us
    dot_general x15 -> x0, matrix products: 17.5 us -> none  [the longest x1 2.77 us: shards(): jnp.einsum('mij,zm->ijz', returned, back_table, precision=HIGHEST)]
    all_to_all x0 -> x1, blocking collectives: none -> 13.8 us  [exchange(): lax.all_to_all(flat, ('gx', 'gy'), split_axis=0, concat_axis=0, tiled=True)]
    unnamed x53 -> x90, local copies, waits for them, and re-layouts: 4.2 us -> 13.2 us
    ppermute x10 -> x4, starting transfers between devices: 15.9 us -> 8.22 us  [the longest x2 6.22 us: swap(): lax.ppermute(b, axis, second)]
    all_to_all x2 -> x1, waiting for transfers between devices: 13 us -> 6.15 us  [exchange(): lax.all_to_all(flat, ('gx', 'gy'), split_axis=0, concat_axis=0, tiled=True)]
    pallas_call x0 -> x5, Pallas kernels: none -> 6.36 us  [call(): pl.pallas_call(body, out_shape=[jax.ShapeDtypeStruct(o, jnp.float32) for...]
    reduce_sum x7 -> x0, other arithmetic: 5.71 us -> none  [the longest x1 2.51 us: shards(): gained = jnp.sum(rate_tile * mass_grown[None, :, :], axis=1)]
    ppermute x10 -> x4, waiting for transfers between devices: 5.26 us -> 0.91 us  [the longest x2 0.91 us: swap(): lax.ppermute(b, axis, second)]
  transfers between devices with their start and end apart: 12 -> 5, of which waited for: 8 -> 2; matrix products, arithmetic and copies ran while one was open for 19% -> 3% of each run, Pallas kernels for 0% -> 3%
where the time goes in v1:
time: 55.9 us; the launch traced here: 55 us
  local copies, waits for them, and re-layouts  14.1 us (25%)
  blocking collectives  13.8 us (25%)
  starting transfers between devices  12.2 us (22%)
  waiting for transfers between devices  7.06 us (13%)
  Pallas kernels  6.36 us (11%)
  between operations  1.04 us (2%)
    all_to_all x1, blocking collectives, exchange(): lax.all_to_all(flat, ('gx', 'gy'), split_axis=0, concat_axis=0, tiled=True)  13.8 us
    unnamed x90, local copies, waits for them, and re-layouts  13.2 us
    pallas_call x5, Pallas kernels, call(): pl.pallas_call(body, out_shape=[jax.ShapeDtypeStruct(o, jnp.float32) for...  6.36 us
    ppermute x2, starting transfers between devices, swap(): lax.ppermute(b, axis, second)  6.22 us
    all_to_all x1, waiting for transfers between devices, exchange(): lax.all_to_all(flat, ('gx', 'gy'), split_axis=0, concat_axis=0, tiled=True)  6.15 us
    all_to_all x1, starting transfers between devices, exchange(): lax.all_to_all(flat, ('gx', 'gy'), split_axis=0, concat_axis=0, tiled=True)  3.94 us
    ppermute x2, starting transfers between devices, swap(): lax.ppermute(a, axis, first)  2.01 us
  transfers between devices with their start and end apart: 5, of which 2 were waited for; matrix products, arithmetic and copies ran while one was open for 3% of the time, Pallas kernels for 3%

profile of v1, /device:TPU:0, one launch (start us, length us, event | category | flops | bytes accessed | tf_op | source)
XLA Modules:
  0.0 55.0 jit_solution(10479334236785148465)
XLA Ops:
  0.6 1.1 %copy-done = f32[3,16,32,128]{3,2,1,0:T(8,128)S(1)} copy-done((f32[3,16,32,128]{3,2,1,0:T(8,128)S(1)}, f32[3,16,32,128]{3,2,1,0:T(8,128)}, u32[]{:S(2)}) %copy-start) | copy-done | bytes 786456
  1.8 0.9 %copy-done.2 = f32[16,32,128]{2,1,0:T(8,128)S(1)} copy-done((f32[16,32,128]{2,1,0:T(8,128)S(1)}, f32[16,32,128]{2,1,0:T(8,128)}, u32[]{:S(2)}) %copy-start.2) | copy-done | bytes 262168
  2.7 0.9 %copy-done.4 = f32[16,32,128]{2,1,0:T(8,128)S(1)} copy-done((f32[16,32,128]{2,1,0:T(8,128)S(1)}, f32[16,32,128]{2,1,0:T(8,128)}, u32[]{:S(2)}) %copy-start.4) | copy-done | bytes 262168
  3.7 0.1 shard_map.345
  3.7 0.5 collective-permute-start.2
  4.3 2.6 %collective-permute-start.3 = (f32[5,16,128]{2,1,0:T(8,128)S(1)}, f32[5,16,128]{2,1,0:T(8,128)S(1)}, u32[]{:S(2)}, u32[]{:S(2)}) collective-permute-start(f32[5,16,128]{2,1,0:T(8,128)S(1)} %get-tuple-element.19), channel_id=1, source_target_pairs={{0,3},{1,2},{2,1},{3,0},{4,7},{5,6},{6,5},{7,4},{8,11},{9,10},{10,... | collective-permute-start | bytes 122888 | tf_op jit(solution)/shard_map/ppermute | solution.py:497
  6.9 1.5 %collective-permute-start = (f32[5,32,128]{2,1,0:T(8,128)S(1)}, f32[5,32,128]{2,1,0:T(8,128)S(1)}, u32[]{:S(2)}, u32[]{:S(2)}) collective-permute-start(f32[5,32,128]{2,1,0:T(8,128)S(1)} %get-tuple-element.16), channel_id=1, source_target_pairs={{0,4},{4,0},{8,12},{12,8},{16,20},{20,16},{24,28},{28,24},{1,5},{5... | collective-permute-start | bytes 245768 | tf_op jit(solution)/shard_map/ppermute | solution.py:497
  8.4 3.6 %collective-permute-start.1 = (f32[5,32,128]{2,1,0:T(8,128)S(1)}, f32[5,32,128]{2,1,0:T(8,128)S(1)}, u32[]{:S(2)}, u32[]{:S(2)}) collective-permute-start(f32[5,32,128]{2,1,0:T(8,128)S(1)} %get-tuple-element.17), channel_id=1, source_target_pairs={{0,28},{4,8},{8,4},{12,16},{16,12},{20,24},{24,20},{28,0},{1,29},{... | collective-permute-start | bytes 245768 | tf_op jit(solution)/shard_map/ppermute | solution.py:497
  12.0 0.0 copy-start.3
  12.1 0.6 %copy-done.44 = f32[128]{0:T(128)S(1)} copy-done((f32[128]{0:T(128)S(1)}, f32[128]{0:T(128)}, u32[]{:S(2)}) %copy-start.44) | copy-done | bytes 536
  12.7 0.1 dynamic_slice.3
  12.8 0.1 broadcast_bitcast_fusion
  12.8 0.1 fusion.21
  13.0 0.1 select_bitcast_fusion
  13.1 0.0 copy-start.38
  13.1 0.0 copy-start.39
  13.1 0.0 copy-start.40
  13.1 0.0 copy-start.41
  13.1 0.0 copy-start.42
  13.1 0.0 copy-start.43
  13.1 0.1 fusion.9
  13.2 0.5 copy-done.36
  13.7 0.0 copy-done.37
  13.7 0.0 copy-done.38
  13.7 0.0 copy-done.39
  13.7 0.0 copy-done.40
  13.8 0.0 copy-done.41
  13.8 0.0 copy-done.42
  13.8 0.0 copy-done.43
  13.8 0.1 convert_add_fusion.target
  13.9 0.0 copy-done.33
  14.0 0.0 copy-start.27
  14.0 0.6 %pad.4.drops = f32[3,32,128]{2,1,0:T(8,128)} pad(f32[3,32,64]{2,1,0:T(8,128)S(1)} %maximum_bitcast_fusion, f32[]{:T(128)} %constant.207.clone.1), padding=0_0x0_0x0_64 | pad | bytes 73732 | tf_op jit(solution)/shard_map/jit(_pad)/pad | solution.py:535
  14.6 0.9 %collective-permute-done.1.xb = f32[5,32,128]{2,1,0:T(8,128)S(1)} collective-permute-done((f32[5,32,128]{2,1,0:T(8,128)S(1)}, f32[5,32,128]{2,1,0:T(8,128)S(1)}, u32[]{:S(2)}, u32[]{:S(2)}) %collective-permute-start.1) | collective-permute-done | bytes 81952 | tf_op jit(solution)/shard_map/ppermute | solution.py:497
  15.6 1.8 %shard_map.346 = (f32[3,16,32,128]{3,2,1,0:T(8,128)S(1)}, f32[576,128]{1,0:T(8,128)}) custom-call(f32[3,16,32,128]{3,2,1,0:T(8,128)S(1)} %copy-done.1, f32[16,32,128]{2,1,0:T(8,128)S(1)} %copy-done.3, f32[5,32,128]{2,1,0:T(8,128)S(1)} %collective-permute-done.xa, f32[5,32,128]{2,1,0:T(8,128)S(1)} %collective-permute-done.1.xb, ...), custom_call_target="tpu_custom_call" | custom-call | flops 6553600 | bytes 2441216 | tf_op jit(solution)/shard_map/pallas_call | solution.py:484
  17.3 3.9 %all-to-all-start = ((f32[32,1,2304]{2,1,0:T(1,128)}), f32[32,1,2304]{2,1,0:T(1,128)S(1)}, u32[]{:S(2)}, u32[]{:S(2)}) async-start(f32[32,1,2304]{2,1,0:T(1,128)} %bitcast), calls=%async_computation | async-start | bytes 589824 | tf_op jit(solution)/shard_map/all_to_all | solution.py:502
  21.3 0.0 copy-start.34
  21.3 0.1 pad_add_fusion.order
  21.4 0.6 %copy-done.34 = f32[128]{0:T(128)S(1)} copy-done((f32[128]{0:T(128)S(1)}, f32[128]{0:T(128)}, u32[]{:S(2)}) %copy-start.34) | copy-done | bytes 536
  21.9 0.1 broadcast_add_fusion
  22.0 0.0 copy-start.10
  22.1 0.1 compare_select_fusion.inverse
  22.2 0.5 copy-done.15
  22.7 0.0 copy-done.17
  22.7 0.3 copy-done.10
  23.1 0.1 copy-done.5
  23.1 0.0 copy-done.12
  23.2 0.9 %copy-done.18 = f32[288,128]{1,0:T(8,128)S(1)} copy-done((f32[288,128]{1,0:T(8,128)S(1)}, f32[288,128]{1,0:T(8,128)}, u32[]{:S(2)}) %copy-start.18) | copy-done | bytes 147480
  24.1 1.9 %shard_map.347 = (f32[16,32,128]{2,1,0:T(8,128)}, f32[16,32,128]{2,1,0:T(8,128)}, f32[8,128]{1,0:T(8,128)S(1)}, f32[32,128]{1,0:T(8,128)S(1)}) custom-call(f32[3,16,32,128]{3,2,1,0:T(8,128)S(1)} %copy-done.1, f32[16,32,128]{2,1,0:T(8,128)S(1)} %copy-done.3, f32[16,32,128]{2,1,0:T(8,128)S(1)} %copy-done.5, f32[5,32,128]{2,1,0:T(8,128)S(1)} %collective-permute-done.xa, ...), custom_call_target="tpu_custom_call" | custom-call | flops 6553600 | bytes 2772992 | tf_op jit(solution)/shard_map/pallas_call | solution.py:484
  25.9 0.6 %copy-done.28 = f32[8,128]{1,0:T(8,128)} copy-done((f32[8,128]{1,0:T(8,128)}, f32[8,128]{1,0:T(8,128)S(1)}, u32[]{:S(2)}) %copy-start.28) | copy-done | bytes 4120
  26.5 6.2 %all-to-all-done = f32[32,1,2304]{2,1,0:T(1,128)S(1)} async-done(((f32[32,1,2304]{2,1,0:T(1,128)}), f32[32,1,2304]{2,1,0:T(1,128)S(1)}, u32[]{:S(2)}, u32[]{:S(2)}) %all-to-all-start) | async-done | bytes 294944 | tf_op jit(solution)/shard_map/all_to_all | solution.py:502
  32.7 1.0 %copy-done.8 = bf16[512,512]{1,0:T(8,128)(2,1)S(1)} copy-done((bf16[512,512]{1,0:T(8,128)(2,1)S(1)}, bf16[512,512]{1,0:T(8,128)(2,1)}, u32[]{:S(2)}) %copy-start.8) | copy-done | bytes 524312
  33.7 1.0 %copy-done.9 = bf16[512,512]{1,0:T(8,128)(2,1)S(1)} copy-done((bf16[512,512]{1,0:T(8,128)(2,1)S(1)}, bf16[512,512]{1,0:T(8,128)(2,1)}, u32[]{:S(2)}) %copy-start.9) | copy-done | bytes 524312
  34.8 0.8 %copy-done.20 = bf16[128,128]{1,0:T(8,128)(2,1)S(1)} copy-done((bf16[128,128]{1,0:T(8,128)(2,1)S(1)}, bf16[128,128]{1,0:T(8,128)(2,1)}, u32[]{:S(2)}) %copy-start.20) | copy-done | bytes 32792
  35.5 0.8 %copy-done.21 = bf16[128,128]{1,0:T(8,128)(2,1)S(1)} copy-done((bf16[128,128]{1,0:T(8,128)(2,1)S(1)}, bf16[128,128]{1,0:T(8,128)(2,1)}, u32[]{:S(2)}) %copy-start.21) | copy-done | bytes 32792
  36.3 0.8 %copy-done.22 = bf16[128,128]{1,0:T(8,128)(2,1)S(1)} copy-done((bf16[128,128]{1,0:T(8,128)(2,1)S(1)}, bf16[128,128]{1,0:T(8,128)(2,1)}, u32[]{:S(2)}) %copy-start.22) | copy-done | bytes 32792
  37.1 0.8 %copy-done.23 = bf16[128,128]{1,0:T(8,128)(2,1)S(1)} copy-done((bf16[128,128]{1,0:T(8,128)(2,1)S(1)}, bf16[128,128]{1,0:T(8,128)(2,1)}, u32[]{:S(2)}) %copy-start.23) | copy-done | bytes 32792
  37.8 1.3 %shard_map.348 = f32[608,128]{1,0:T(8,128)S(1)} custom-call(f32[576,128]{1,0:T(8,128)S(1)} %bitcast.20, f32[128,512]{1,0:T(8,128)S(1)} %compare_select_fusion.inverse, f32[32,128]{1,0:T(8,128)S(1)} %get-tuple-element.21.leave, bf16[512,512]{1,0:T(8,128)(2,1)S(1)} %copy-done.9, bf16[512,512]{1,0:T(8,128)(2,1)S(1)} %copy-done.8, ...), custom_call_target="tpu_custom_call" | custom-call | flops 65536000 | bytes 3112960 | tf_op jit(solution)/shard_map/pallas_call | solution.py:484
  39.2 0.0 copy-start.19
  39.2 0.0 copy-start.24
  39.2 0.0 copy-start.25
  39.2 13.8 %all_to_all.10 = f32[32,1,2432]{2,1,0:T(1,128)S(1)} all-to-all(f32[32,1,2432]{2,1,0:T(1,128)S(1)} %bitcast.18), channel_id=1, replica_groups=mesh['gx'=8,'gy'=4] {'gx','gy'}, dimensions={0} | all-to-all | bytes 622592 | tf_op jit(solution)/shard_map/all_to_all | solution.py:502
  53.0 0.7 %copy-done.29 = f32[8,128]{1,0:T(8,128)S(1)} copy-done((f32[8,128]{1,0:T(8,128)S(1)}, f32[8,128]{1,0:T(8,128)}, u32[]{:S(2)}) %copy-start.29) | copy-done | bytes 4120
  53.7 1.3 %shard_map.349 = (f32[3,16,32,128]{3,2,1,0:T(8,128)}, f32[3,32]{1,0:T(4,128)}) custom-call(f32[608,128]{1,0:T(8,128)S(1)} %bitcast.19, f32[3,16,32,128]{3,2,1,0:T(8,128)S(1)} %get-tuple-element.22.star, f32[8,128]{1,0:T(8,128)S(1)} %copy-done.29, bf16[128,128]{1,0:T(8,128)(2,1)S(1)} %copy-done.25, bf16[128,128]{1,0:T(8,128)(2,1)S(1)} %copy-done.24, ...), custom_call_target="tpu_custom_call" | custom-call | flops 6553600 | bytes 2019712 | tf_op jit(solution)/shard_map/pallas_call | solution.py:484
  (59 shorter events, 0.2 us)
Async XLA Ops:
  0.6 1.1 %copy-start = (f32[3,16,32,128]{3,2,1,0:T(8,128)S(1)}, f32[3,16,32,128]{3,2,1,0:T(8,128)}, u32[]{:S(2)}) copy-start(f32[3,16,32,128]{3,2,1,0:T(8,128)} %vel.5) | copy-start | bytes 2359300
  1.8 0.9 %copy-start.2 = (f32[16,32,128]{2,1,0:T(8,128)S(1)}, f32[16,32,128]{2,1,0:T(8,128)}, u32[]{:S(2)}) copy-start(f32[16,32,128]{2,1,0:T(8,128)} %theta.5) | copy-start | bytes 786436
  2.7 0.9 %copy-start.4 = (f32[16,32,128]{2,1,0:T(8,128)S(1)}, f32[16,32,128]{2,1,0:T(8,128)}, u32[]{:S(2)}) copy-start(f32[16,32,128]{2,1,0:T(8,128)} %vapour.3) | copy-start | bytes 786436
  3.7 11.9 %copy-start.1 = (f32[3,16,32,128]{3,2,1,0:T(8,128)S(1)}, f32[3,16,32,128]{3,2,1,0:T(8,128)}, u32[]{:S(2)}) copy-start(f32[3,16,32,128]{3,2,1,0:T(8,128)} %vel.5) | copy-start | bytes 2359300
  3.7 10.9 %collective-permute-start.2 = (f32[5,16,128]{2,1,0:T(8,128)S(1)}, f32[5,16,128]{2,1,0:T(8,128)S(1)}, u32[]{:S(2)}, u32[]{:S(2)}) collective-permute-start(f32[5,16,128]{2,1,0:T(8,128)S(1)} %get-tuple-element.18), channel_id=1, source_target_pairs={{0,1},{1,0},{2,3},{3,2},{4,5},{5,4},{6,7},{7,6},{8,9},{9,8},{10,11... | collective-permute-start | bytes 122888 | tf_op jit(solution)/shard_map/ppermute | solution.py:497
  4.3 10.3 %collective-permute-start.3 = (f32[5,16,128]{2,1,0:T(8,128)S(1)}, f32[5,16,128]{2,1,0:T(8,128)S(1)}, u32[]{:S(2)}, u32[]{:S(2)}) collective-permute-start(f32[5,16,128]{2,1,0:T(8,128)S(1)} %get-tuple-element.19), channel_id=1, source_target_pairs={{0,3},{1,2},{2,1},{3,0},{4,7},{5,6},{6,5},{7,4},{8,11},{9,10},{10,... | collective-permute-start | bytes 122888 | tf_op jit(solution)/shard_map/ppermute | solution.py:497
  6.9 7.7 %collective-permute-start = (f32[5,32,128]{2,1,0:T(8,128)S(1)}, f32[5,32,128]{2,1,0:T(8,128)S(1)}, u32[]{:S(2)}, u32[]{:S(2)}) collective-permute-start(f32[5,32,128]{2,1,0:T(8,128)S(1)} %get-tuple-element.16), channel_id=1, source_target_pairs={{0,4},{4,0},{8,12},{12,8},{16,20},{20,16},{24,28},{28,24},{1,5},{5... | collective-permute-start | bytes 245768 | tf_op jit(solution)/shard_map/ppermute | solution.py:497
  8.4 7.1 %collective-permute-start.1 = (f32[5,32,128]{2,1,0:T(8,128)S(1)}, f32[5,32,128]{2,1,0:T(8,128)S(1)}, u32[]{:S(2)}, u32[]{:S(2)}) collective-permute-start(f32[5,32,128]{2,1,0:T(8,128)S(1)} %get-tuple-element.17), channel_id=1, source_target_pairs={{0,28},{4,8},{8,4},{12,16},{16,12},{20,24},{24,20},{28,0},{1,29},{... | collective-permute-start | bytes 245768 | tf_op jit(solution)/shard_map/ppermute | solution.py:497
  12.0 1.1 %copy-start.32 = (s32[64,32]{0,1:T(8,128)S(1)}, s32[64,32]{0,1:T(8,128)}, u32[]{:S(2)}) copy-start(s32[64,32]{0,1:T(8,128)} %param.41) | copy-start | bytes 24580
  12.0 1.0 %copy-start.31 = (f32[64,32]{0,1:T(8,128)S(1)}, f32[64,32]{0,1:T(8,128)}, u32[]{:S(2)}) copy-start(f32[64,32]{0,1:T(8,128)} %param.38) | copy-start | bytes 24580
  12.0 1.0 %copy-start.35 = (s32[32]{0:T(128)S(1)}, s32[32]{0:T(128)}, u32[]{:S(2)}) copy-start(s32[32]{0:T(128)} %param.39) | copy-start | bytes 388
  12.0 0.7 %copy-start.44 = (f32[128]{0:T(128)S(1)}, f32[128]{0:T(128)}, u32[]{:S(2)}) copy-start(f32[128]{0:T(128)} %constant.230.clone) | copy-start | bytes 1540
  12.0 0.8 %copy-start.30 = (s32[32,64]{1,0:T(8,128)S(1)}, s32[32,64]{1,0:T(8,128)}, u32[]{:S(2)}) copy-start(s32[32,64]{1,0:T(8,128)} %param.40) | copy-start | bytes 24580
  12.0 3.5 %copy-start.3 = (f32[16,32,128]{2,1,0:T(8,128)S(1)}, f32[16,32,128]{2,1,0:T(8,128)}, u32[]{:S(2)}) copy-start(f32[16,32,128]{2,1,0:T(8,128)} %theta.5) | copy-start | bytes 786436
  13.0 0.7 %copy-start.36 = (pred[128]{0:T(512)(128)(4,1)S(1)}, pred[128]{0:T(512)(128)(4,1)}, u32[]{:S(2)}) copy-start(pred[128]{0:T(512)(128)(4,1)} %constant.252) | copy-start | bytes 388
  13.0 0.7 %copy-start.37 = (pred[128]{0:T(512)(128)(4,1)S(1)}, pred[128]{0:T(512)(128)(4,1)}, u32[]{:S(2)}) copy-start(pred[128]{0:T(512)(128)(4,1)} %constant.251) | copy-start | bytes 388
  13.1 0.7 %copy-start.38 = (pred[128]{0:T(512)(128)(4,1)S(1)}, pred[128]{0:T(512)(128)(4,1)}, u32[]{:S(2)}) copy-start(pred[128]{0:T(512)(128)(4,1)} %constant.250) | copy-start | bytes 388
  13.1 0.7 %copy-start.39 = (pred[128]{0:T(512)(128)(4,1)S(1)}, pred[128]{0:T(512)(128)(4,1)}, u32[]{:S(2)}) copy-start(pred[128]{0:T(512)(128)(4,1)} %constant.249) | copy-start | bytes 388
  13.1 0.7 %copy-start.40 = (pred[128]{0:T(512)(128)(4,1)S(1)}, pred[128]{0:T(512)(128)(4,1)}, u32[]{:S(2)}) copy-start(pred[128]{0:T(512)(128)(4,1)} %constant.248) | copy-start | bytes 388
  13.1 0.7 %copy-start.41 = (pred[128]{0:T(512)(128)(4,1)S(1)}, pred[128]{0:T(512)(128)(4,1)}, u32[]{:S(2)}) copy-start(pred[128]{0:T(512)(128)(4,1)} %constant.247) | copy-start | bytes 388
  13.1 0.7 %copy-start.42 = (pred[128]{0:T(512)(128)(4,1)S(1)}, pred[128]{0:T(512)(128)(4,1)}, u32[]{:S(2)}) copy-start(pred[128]{0:T(512)(128)(4,1)} %constant.246) | copy-start | bytes 388
  13.1 0.7 %copy-start.43 = (pred[128]{0:T(512)(128)(4,1)S(1)}, pred[128]{0:T(512)(128)(4,1)}, u32[]{:S(2)}) copy-start(pred[128]{0:T(512)(128)(4,1)} %constant.245) | copy-start | bytes 388
  13.2 0.7 %copy-start.33 = (f32[64,32]{0,1:T(8,128)S(1)}, f32[64,32]{0,1:T(8,128)}, u32[]{:S(2)}) copy-start(f32[64,32]{0,1:T(8,128)} %param.37) | copy-start | bytes 24580
  14.0 1.6 %copy-start.26 = (bf16[128,128]{1,0:T(8,128)(2,1)S(1)}, bf16[128,128]{1,0:T(8,128)(2,1)}, u32[]{:S(2)}) copy-start(bf16[128,128]{1,0:T(8,128)(2,1)} %constant.227.clone.fl) | copy-start | bytes 98308
  14.0 1.6 %copy-start.27 = (bf16[128,128]{1,0:T(8,128)(2,1)S(1)}, bf16[128,128]{1,0:T(8,128)(2,1)}, u32[]{:S(2)}) copy-start(bf16[128,128]{1,0:T(8,128)(2,1)} %constant.226.clone.fh) | copy-start | bytes 98308
  14.6 2.7 %copy-start.14 = (f32[5,16,128]{2,1,0:T(8,128)}, f32[5,16,128]{2,1,0:T(8,128)S(1)}, u32[]{:S(2)}) copy-start(f32[5,16,128]{2,1,0:T(8,128)S(1)} %collective-permute-done.2.ya) | copy-start | bytes 122884
  14.6 2.7 %copy-start.16 = (f32[5,16,128]{2,1,0:T(8,128)}, f32[5,16,128]{2,1,0:T(8,128)S(1)}, u32[]{:S(2)}) copy-start(f32[5,16,128]{2,1,0:T(8,128)S(1)} %collective-permute-done.3.yb) | copy-start | bytes 122884
  15.6 1.8 %copy-start.11 = (f32[5,32,128]{2,1,0:T(8,128)}, f32[5,32,128]{2,1,0:T(8,128)S(1)}, u32[]{:S(2)}) copy-start(f32[5,32,128]{2,1,0:T(8,128)S(1)} %collective-permute-done.1.xb) | copy-start | bytes 245764
  17.3 15.3 %all-to-all-start = ((f32[32,1,2304]{2,1,0:T(1,128)}), f32[32,1,2304]{2,1,0:T(1,128)S(1)}, u32[]{:S(2)}, u32[]{:S(2)}) async-start(f32[32,1,2304]{2,1,0:T(1,128)} %bitcast), calls=%async_computation | async-start | bytes 589824 | tf_op jit(solution)/shard_map/all_to_all | solution.py:502
  21.3 0.7 %copy-start.34 = (f32[128]{0:T(128)S(1)}, f32[128]{0:T(128)}, u32[]{:S(2)}) copy-start(f32[128]{0:T(128)} %constant.231.clone) | copy-start | bytes 1540
  21.9 0.8 %copy-start.15 = (f32[5,16,128]{2,1,0:T(8,128)S(1)}, f32[5,16,128]{2,1,0:T(8,128)}, u32[]{:S(2)}) copy-start(f32[5,16,128]{2,1,0:T(8,128)} %copy-done.14) | copy-start | bytes 122884
  21.9 0.8 %copy-start.17 = (f32[5,16,128]{2,1,0:T(8,128)S(1)}, f32[5,16,128]{2,1,0:T(8,128)}, u32[]{:S(2)}) copy-start(f32[5,16,128]{2,1,0:T(8,128)} %copy-done.16) | copy-start | bytes 122884
  22.0 1.0 %copy-start.10 = (f32[3,288,128]{2,1,0:T(8,128)S(1)}, f32[3,288,128]{2,1,0:T(8,128)}, u32[]{:S(2)}) copy-start(f32[3,288,128]{2,1,0:T(8,128)} %constant.229.clone.away) | copy-start | bytes 1327108
  22.1 1.0 %copy-start.5 = (f32[16,32,128]{2,1,0:T(8,128)S(1)}, f32[16,32,128]{2,1,0:T(8,128)}, u32[]{:S(2)}) copy-start(f32[16,32,128]{2,1,0:T(8,128)} %vapour.3) | copy-start | bytes 786436
  22.1 1.0 %copy-start.12 = (f32[5,32,128]{2,1,0:T(8,128)S(1)}, f32[5,32,128]{2,1,0:T(8,128)}, u32[]{:S(2)}) copy-start(f32[5,32,128]{2,1,0:T(8,128)} %copy-done.11) | copy-start | bytes 245764
  22.1 1.0 %copy-start.13 = (f32[3,32,128]{2,1,0:T(8,128)S(1)}, f32[3,32,128]{2,1,0:T(8,128)}, u32[]{:S(2)}) copy-start(f32[3,32,128]{2,1,0:T(8,128)} %pad.4.drops) | copy-start | bytes 147460
  23.2 0.9 %copy-start.18 = (f32[288,128]{1,0:T(8,128)S(1)}, f32[288,128]{1,0:T(8,128)}, u32[]{:S(2)}) copy-start(f32[288,128]{1,0:T(8,128)} %constant.228.clone.here) | copy-start | bytes 442372
  24.1 8.6 %copy-start.6 = (bf16[512,512]{1,0:T(8,128)(2,1)S(1)}, bf16[512,512]{1,0:T(8,128)(2,1)}, u32[]{:S(2)}) copy-start(bf16[512,512]{1,0:T(8,128)(2,1)} %constant.235.clone.tl) | copy-start | bytes 1572868
  24.1 8.6 %copy-start.7 = (bf16[512,512]{1,0:T(8,128)(2,1)S(1)}, bf16[512,512]{1,0:T(8,128)(2,1)}, u32[]{:S(2)}) copy-start(bf16[512,512]{1,0:T(8,128)(2,1)} %constant.234.clone.th) | copy-start | bytes 1572868
  25.9 0.6 %copy-start.28 = (f32[8,128]{1,0:T(8,128)}, f32[8,128]{1,0:T(8,128)S(1)}, u32[]{:S(2)}) copy-start(f32[8,128]{1,0:T(8,128)S(1)} %get-tuple-element.23.stay) | copy-start | bytes 12292
  32.7 1.0 %copy-start.8 = (bf16[512,512]{1,0:T(8,128)(2,1)S(1)}, bf16[512,512]{1,0:T(8,128)(2,1)}, u32[]{:S(2)}) copy-start(bf16[512,512]{1,0:T(8,128)(2,1)} %constant.233.clone.wl) | copy-start | bytes 1572868
  33.7 1.0 %copy-start.9 = (bf16[512,512]{1,0:T(8,128)(2,1)S(1)}, bf16[512,512]{1,0:T(8,128)(2,1)}, u32[]{:S(2)}) copy-start(bf16[512,512]{1,0:T(8,128)(2,1)} %constant.232.clone.wh) | copy-start | bytes 1572868
  34.8 0.8 %copy-start.20 = (bf16[128,128]{1,0:T(8,128)(2,1)S(1)}, bf16[128,128]{1,0:T(8,128)(2,1)}, u32[]{:S(2)}) copy-start(bf16[128,128]{1,0:T(8,128)(2,1)} %constant.239.clone.qtl) | copy-start | bytes 98308
  35.5 0.8 %copy-start.21 = (bf16[128,128]{1,0:T(8,128)(2,1)S(1)}, bf16[128,128]{1,0:T(8,128)(2,1)}, u32[]{:S(2)}) copy-start(bf16[128,128]{1,0:T(8,128)(2,1)} %constant.238.clone.qth) | copy-start | bytes 98308
  36.3 0.8 %copy-start.22 = (bf16[128,128]{1,0:T(8,128)(2,1)S(1)}, bf16[128,128]{1,0:T(8,128)(2,1)}, u32[]{:S(2)}) copy-start(bf16[128,128]{1,0:T(8,128)(2,1)} %constant.237.clone.ql) | copy-start | bytes 98308
  37.0 0.8 %copy-start.23 = (bf16[128,128]{1,0:T(8,128)(2,1)S(1)}, bf16[128,128]{1,0:T(8,128)(2,1)}, u32[]{:S(2)}) copy-start(bf16[128,128]{1,0:T(8,128)(2,1)} %constant.236.clone.qh) | copy-start | bytes 98308
  39.2 13.9 %copy-start.19 = (f32[128,128]{1,0:T(8,128)S(1)}, f32[128,128]{1,0:T(8,128)}, u32[]{:S(2)}) copy-start(f32[128,128]{1,0:T(8,128)} %constant.242.clone.place) | copy-start | bytes 196612
  39.2 13.8 %copy-start.24 = (bf16[128,128]{1,0:T(8,128)(2,1)S(1)}, bf16[128,128]{1,0:T(8,128)(2,1)}, u32[]{:S(2)}) copy-start(bf16[128,128]{1,0:T(8,128)(2,1)} %constant.241.clone.bl) | copy-start | bytes 98308
  39.2 13.8 %copy-start.25 = (bf16[128,128]{1,0:T(8,128)(2,1)S(1)}, bf16[128,128]{1,0:T(8,128)(2,1)}, u32[]{:S(2)}) copy-start(bf16[128,128]{1,0:T(8,128)(2,1)} %constant.240.clone.bh) | copy-start | bytes 98308
  53.0 0.7 %copy-start.29 = (f32[8,128]{1,0:T(8,128)S(1)}, f32[8,128]{1,0:T(8,128)}, u32[]{:S(2)}) copy-start(f32[8,128]{1,0:T(8,128)} %copy-done.28) | copy-start | bytes 12292

commit v2 on v1

--- a/solution.py
+++ b/solution.py
@@ -13,6 +13,8 @@
 BW = 4
 LANES = 128
 
+EDGE_LIMIT = 55040 * 2**10
+
 TIME_STEP = 0.2
 DIFFUSION = 0.05
 BUOYANCY = 0.5
@@ -21,7 +23,7 @@
 CONDENSE = 0.002
 
 VMEM = pl.BlockSpec(memory_space=pltpu.VMEM)
-PARAMS = pltpu.CompilerParams(vmem_limit_bytes=24 * 2**20)
+HBM = pl.BlockSpec(memory_space=pltpu.HBM)
 NT = (((1,), (1,)), ((), ()))
 TN = (((0,), (0,)), ((), ()))
 NN = (((1,), (0,)), ((), ()))
@@ -89,10 +91,8 @@
         qy, ey = real_basis(self.ty)
         q1 = qx.reshape(self.gx, self.xg, self.x4, self.tx)
         q1 = q1.transpose(3, 2, 1, 0).reshape(self.tx, self.tx)
-        w = np.einsum("byk,pq->bpyqk", qy.reshape(self.gy, self.sy, self.ty), np.eye(self.x4))
-        w = w.reshape(self.gy * LANES, self.x4 * self.ty)
         ez = -4.0 * np.sin(np.pi * z / (2 * nz)) ** 2
-        return forward, backward, q1, w, ex, ey, ez
+        return forward, backward, q1, qy, ex, ey, ez
 
 
 def neighbours(count):
@@ -101,22 +101,43 @@
     return first, second
 
 
-def edges_kernel(plan, vel, theta, vapour, xa, xb, ya, yb):
-    odd_x = lax.axis_index("gx") % 2 == 1
+def copy_all(copies):
+    for copy in copies:
+        copy.start()
+    for copy in copies:
+        copy.wait()
+
+
+def plane_copies(vel, theta, vapour, x, out, sems):
+    return [
+        pltpu.make_async_copy(vel.at[:, x], out.at[0:3], sems.at[0]),
+        pltpu.make_async_copy(theta.at[x], out.at[3], sems.at[1]),
+        pltpu.make_async_copy(vapour.at[x], out.at[4], sems.at[2]),
+    ]
+
+
+def far_kernel(plan, vel, theta, vapour, xb, sems):
+    odd = lax.axis_index("gx") % 2
+    copy_all(plane_copies(vel, theta, vapour, (plan.sx - 1) * odd, xb, sems))
+
+
+def near_kernel(plan, vel, theta, vapour, after, xa, ya, yb, south, north, sems):
+    odd_x = lax.axis_index("gx") % 2
     odd_y = lax.axis_index("gy") % 2 == 1
-    fields = [(vel, i) for i in range(3)] + [(theta, None), (vapour, None)]
-    for f, (ref, i) in enumerate(fields):
-        at = (lambda x, ref=ref, i=i: ref[x] if i is None else ref[i, x])
-        first, last = at(0), at(plan.sx - 1)
-        xa[f] = jnp.where(odd_x, first, last)
-        xb[f] = jnp.where(odd_x, last, first)
-        for x in range(plan.sx):
-            if i is None:
-                south, north = ref[x, 0:1], ref[x, plan.sy - 1 : plan.sy]
-            else:
-                south, north = ref[i, x, 0:1], ref[i, x, plan.sy - 1 : plan.sy]
-            ya[f, x : x + 1] = jnp.where(odd_y, south, north)
-            yb[f, x : x + 1] = jnp.where(odd_y, north, south)
+    tile = south.shape[2]
+    copies = plane_copies(vel, theta, vapour, (plan.sx - 1) * (1 - odd_x), xa, sems.at[2])
+    for side, (out, y) in enumerate(((south, 0), (north, plan.sy - tile))):
+        copies += [
+            pltpu.make_async_copy(vel.at[:, :, y : y + tile], out.at[0:3], sems.at[side, 0]),
+            pltpu.make_async_copy(theta.at[:, y : y + tile], out.at[3], sems.at[side, 1]),
+            pltpu.make_async_copy(vapour.at[:, y : y + tile], out.at[4], sems.at[side, 2]),
+        ]
+    copy_all(copies)
+    for f in range(5):
+        low = jnp.concatenate([south[f, x, 0:1] for x in range(plan.sx)], axis=0)
+        high = jnp.concatenate([north[f, x, tile - 1 : tile] for x in range(plan.sx)], axis=0)
+        ya[f] = jnp.where(odd_y, low, high)
+        yb[f] = jnp.where(odd_y, high, low)
 
 
 def edge_masks(plan):
@@ -224,12 +245,22 @@
     out[pl.ds(plan.main + 1, plan.nd, stride=plan.rows1), :] = row_sum
 
 
-def solve_kernel(plan, r, inverse, leave, wh, wl, th, tl, qh, ql, qth, qtl, out):
+def solve_kernel(plan, r, inverse, leave, qy, qx, out, wide):
     gx, gy, per, xg, x4 = plan.gx, plan.gy, plan.per, plan.xg, plan.x4
     lane = lax.broadcasted_iota(jnp.int32, (gx, LANES), 1)
     first_lanes = lane < plan.sy
     first_rows = lane % plan.sy == 0
     step1, step2 = gy * plan.rows1, gy * plan.rows2
+
+    for part in range(2):
+        wide[part] = jnp.zeros(wide.shape[1:], wide.dtype)
+        for b in range(gy):
+            for p in range(x4):
+                at = b * LANES + p * plan.sy
+                wide[part, at : at + plan.sy, p * plan.ty : (p + 1) * plan.ty] = qy[
+                    part, b * plan.sy : (b + 1) * plan.sy
+                ]
+    table_y = (wide[0], wide[1])
 
     def take(b, q):
         return r[pl.ds(b * plan.rows1 + q, gx, stride=step1), :]
@@ -246,7 +277,7 @@
             nb = (b + 1) % gy
             blocks[nb][q] = blocks[nb][q] + jnp.where(first_rows, moved, 0.0)
     grid = jnp.concatenate([jnp.concatenate(column, axis=0) for column in blocks], axis=1)
-    in_y = dot3(split(grid), (wh[...], wl[...]))
+    in_y = dot3(split(grid), table_y)
     height = xg * gx
 
     def swap(value, outer, inner):
@@ -264,10 +295,10 @@
             axis=0,
         )
 
-    spectral = dot3((qh[...], ql[...]), split(swap(in_y, per, x4)))
+    spectral = dot3((qx[0], qx[1]), split(swap(in_y, per, x4)))
     solved = spectral * inverse[...]
-    in_x = dot3((qth[...], qtl[...]), split(solved))
-    grid = dot3(split(swap(in_x, x4, per)), (th[...], tl[...]))
+    in_x = dot3((qx[2], qx[3]), split(solved))
+    grid = dot3(split(swap(in_x, x4, per)), table_y, NT)
     planes = [jnp.zeros((gx, LANES), jnp.float32) for _ in range(gy)]
     rows = [jnp.zeros((gx, LANES), jnp.float32) for _ in range(gy)]
     for b in range(gy):
@@ -358,13 +389,12 @@
         for x in xs:
             for y in ys:
                 lane_of[k, x, y] = len(lane_of)
-    assert len(lane_of) == width and 3 * width <= LANES
+    assert len(lane_of) == width and max(3 * width, boxes + width) <= LANES
     for (k, x, y), at in lane_of.items():
         for load in range(3):
             kind_of[load * width + at] = k
             place[load * width + at, x * by + y] = 1.0
-    here = np.zeros((9 * boxes, LANES), np.float32)
-    away = np.zeros((3, 9 * boxes, LANES), np.float32)
+    goes = np.zeros((9 * boxes, LANES), np.float32)
     for dx in (-1, 0, 1):
         for dy in (-1, 0, 1):
             code = (dx + 1) * 3 + dy + 1
@@ -375,17 +405,21 @@
                     sy = (y + dy) // by
                     tx, ty = (x + dx) % bx, (y + dy) % by
                     if (sx, sy) == (0, 0):
-                        here[line, tx * by + ty] = 1.0
+                        goes[line, tx * by + ty] = 1.0
                     else:
-                        at = lane_of[KINDS.index((sx, sy)), tx, ty]
-                        for load in range(3):
-                            away[load, line, load * width + at] = 1.0
-    return here, away, place, kind_of
+                        goes[line, boxes + lane_of[KINDS.index((sx, sy)), tx, ty]] = 1.0
+    return goes, place, kind_of[None].astype(np.int32)
+
+
+def quotient(value, divisor):
+    if divisor & (divisor - 1) == 0:
+        return value >> (divisor.bit_length() - 1), value & (divisor - 1)
+    return lax.div(value, divisor), lax.rem(value, divisor)
 
 
 def scalar_kernel(
-    plan, vel, theta, vapour, xa, xb, ya, yb, drops, order, here, away, target,
-    theta_new, vapour_new, stay, leave, moist,
+    plan, vel, theta, vapour, xa, xb, ya, yb, radius, multiplicity, counts, pairing,
+    destination, goes, kind, theta_new, vapour_new, stay, leave, moist,
 ):
     masks = edge_masks(plan)
     bx, by, boxes = plan.bx, plan.by, plan.boxes
@@ -428,14 +462,33 @@
         [exact(gather_y, jnp.broadcast_to(s, (plan.sy, LANES))) for s in sums], axis=0
     ) * (1.0 / (BW * BW * plan.nz))
     softplus = jnp.maximum(means, 0.0) + jnp.log(1.0 + jnp.exp(-jnp.abs(means)))
-    index = order[...]
+    rank_x, rank_y = lax.axis_index("gx"), lax.axis_index("gy")
+    box = lax.broadcasted_iota(jnp.int32, (boxes, plan.slots), 0)
+    slot = lax.broadcasted_iota(jnp.int32, (boxes, plan.slots), 1)
+    device, local = quotient(destination[...], boxes)
+    device_x, device_y = quotient(device, plan.gy)
+    local_x, local_y = quotient(local, by)
+    source_x, source_y = quotient(box, by)
+    offset_x = (device_x - rank_x) * bx + local_x - source_x + (1 + bx * plan.gx)
+    offset_y = (device_y - rank_y) * by + local_y - source_y + (1 + by * plan.gy)
+    offset_x = quotient(offset_x, bx * plan.gx)[1]
+    offset_y = quotient(offset_y, by * plan.gy)[1]
+    code = (offset_x * 3 + offset_y).astype(jnp.float32)
+    line = lax.broadcasted_iota(jnp.int32, (boxes, boxes), 0)
+    used = jnp.where(
+        line == lax.broadcasted_iota(jnp.int32, (boxes, boxes), 1), counts[...], 0
+    )
+    used = jnp.sum(used, axis=1, keepdims=True)
+    live = jnp.where(slot < used, multiplicity[...], 0.0)
+    half = plan.slots // 2
+    order = pairing[...]
+    index = jnp.concatenate([order, order[:, half:], order[:, :half]], axis=1)
 
     def gather(value):
-        return jnp.take_along_axis(value, index, axis=1, mode="promise_in_bounds")
-
-    radius_sq = gather(drops[0])
-    live = gather(drops[1])
-    code = gather(drops[2])
+        twice = jnp.concatenate([value, value], axis=1)
+        return jnp.take_along_axis(twice, index, axis=1, mode="promise_in_bounds")
+
+    radius_sq, live, code = gather(radius[...]), gather(live), gather(code)
     grown_sq = radius_sq + GROWTH * softplus
     root = jnp.sqrt(grown_sq)
     mass = grown_sq * root
@@ -470,24 +523,36 @@
     payload = jnp.zeros((1, LANES), jnp.float32)
     stays = jnp.zeros((8, LANES), jnp.float32)
     line = lax.broadcasted_iota(jnp.int32, (8, LANES), 0)
+    lane = lax.broadcasted_iota(jnp.int32, (1, LANES), 1)
+    width = payload_width(plan)
+    leaving = (lane >= boxes) & (lane < boxes + width)
     for k in range(3):
         column = jnp.concatenate(parts[k], axis=0)
-        payload = payload + jnp.sum(column * away[k], axis=0, keepdims=True)
-        stays = jnp.where(line == k, jnp.sum(column * here[...], axis=0, keepdims=True), stays)
+        landed = jnp.sum(column * goes[...], axis=0, keepdims=True)
+        stays = jnp.where(line == k, landed, stays)
+        payload = payload + pltpu.roll(
+            jnp.where(leaving, landed, 0.0), (k * width - boxes) % LANES, 1
+        )
     stay[...] = stays
-    leave[...] = payload * target[...]
-
-
-def call(body, outs, args, flops, scratch=()):
+    owner = jnp.full((1, LANES), -1, jnp.int32)
+    for k, (sx, sy) in enumerate(KINDS):
+        to_x = lax.rem(rank_x + (sx + plan.gx), plan.gx)
+        to_y = lax.rem(rank_y + (sy + plan.gy), plan.gy)
+        owner = jnp.where(kind[...] == k, to_x * plan.gy + to_y, owner)
+    every = lax.broadcasted_iota(jnp.int32, (plan.nd, LANES), 0)
+    leave[...] = jnp.where(every == owner, payload, 0.0)
+
+
+def call(body, outs, args, flops, scratch=(), space=VMEM, limit=8 * 2**20):
     moved = sum(a.size * a.dtype.itemsize for a in args)
     moved += sum(math.prod(o) * 4 for o in outs)
     return pl.pallas_call(
         body,
         out_shape=[jax.ShapeDtypeStruct(o, jnp.float32) for o in outs],
-        in_specs=[VMEM] * len(args),
+        in_specs=[space] * len(args),
         out_specs=[VMEM] * len(outs),
         scratch_shapes=list(scratch),
-        compiler_params=PARAMS,
+        compiler_params=pltpu.CompilerParams(vmem_limit_bytes=limit),
         cost_estimate=pl.CostEstimate(flops=flops, bytes_accessed=moved, transcendentals=0),
     )(*args)
 
@@ -509,36 +574,24 @@
     plan = Plan(lax.axis_size("gx"), lax.axis_size("gy"), span_x, span_y, levels, slots)
     rank_x, rank_y = lax.axis_index("gx"), lax.axis_index("gy")
     rank = rank_x * plan.gy + rank_y
-    forward, backward, q1, w, ex, ey, ez = plan.tables()
-    here, away, place, kind_of = droplet_tables(plan)
+    forward, backward, q1, qy, ex, ey, ez = plan.tables()
+    goes, place, kind = droplet_tables(plan)
     block = (span_x, span_y, levels)
     cells = math.prod(block)
 
     plane, rows = (5, span_y, levels), (5, span_x, levels)
-    xa, xb, ya, yb = call(
-        functools.partial(edges_kernel, plan),
-        (plane, plane, rows, rows), (velocity, theta, vapour), cells,
+    fields = (velocity, theta, vapour)
+    (xb,) = call(
+        functools.partial(far_kernel, plan), (plane,), fields, cells,
+        [pltpu.SemaphoreType.DMA((3,))], HBM, EDGE_LIMIT,
+    )
+    xa, ya, yb = call(
+        functools.partial(near_kernel, plan), (plane, rows, rows), fields + (xb,), cells,
+        [pltpu.VMEM((5, span_x, 8, levels), jnp.float32)] * 2 + [pltpu.SemaphoreType.DMA((3, 3))],
+        HBM, EDGE_LIMIT,
     )
     xa, xb = swap((xa, xb), "gx")
     ya, yb = swap((ya, yb), "gy")
-
-    box = jnp.arange(plan.boxes)
-    source_x = rank_x * plan.bx + box // plan.by
-    source_y = rank_y * plan.by + box % plan.by
-    device, local = destination // plan.boxes, destination % plan.boxes
-    target_x = device // plan.gy * plan.bx + local // plan.by
-    target_y = device % plan.gy * plan.by + local % plan.by
-    offset_x = (target_x - source_x[None, :] + 1) % (plan.bx * plan.gx)
-    offset_y = (target_y - source_y[None, :] + 1) % (plan.by * plan.gy)
-    live = jnp.where(jnp.arange(slots)[:, None] < counts[None, :], multiplicity, 0.0)
-    drops = jnp.stack([radius_sq, live, (offset_x * 3 + offset_y).astype(jnp.float32)])
-    drops = jnp.pad(jnp.swapaxes(drops, 1, 2), ((0, 0), (0, 0), (0, LANES - slots)))
-    order = jnp.concatenate([pairing, jnp.roll(pairing, slots // 2, axis=1)], axis=1)
-    every = jnp.arange(plan.nd)
-    target = jnp.zeros((plan.nd, LANES), jnp.float32)
-    for k, (sx, sy) in enumerate(KINDS):
-        to = (rank_x + sx) % plan.gx * plan.gy + (rank_y + sy) % plan.gy
-        target = target + ((every == to)[:, None] & (kind_of == k)[None, :]).astype(jnp.float32)
 
     star, chunks = call(
         functools.partial(wind_kernel, plan),
@@ -551,7 +604,8 @@
     theta_new, vapour_new, stay, leave = call(
         functools.partial(scalar_kernel, plan),
         (block, block, (8, LANES), (plan.nd, LANES)),
-        (velocity, theta, vapour, xa, xb, ya, yb, drops, order, here, away, target),
+        fields + (xa, xb, ya, yb, radius_sq.T, multiplicity.T, counts[None], pairing)
+        + (destination.T, goes, kind),
         100 * cells,
         (pltpu.VMEM(block, jnp.float32),),
     )
@@ -566,8 +620,9 @@
     (chunks,) = call(
         functools.partial(solve_kernel, plan),
         ((plan.nd * plan.rows2, LANES),),
-        (spectral, inverse, leave) + halves(w) + halves(w.T) + halves(q1) + halves(q1.T),
+        (spectral, inverse, leave, np.stack(halves(qy)), np.stack(halves(q1) + halves(q1.T))),
         1000 * cells,
+        [pltpu.VMEM((2, plan.gy * LANES, plan.x4 * plan.ty), jnp.bfloat16)],
     )
     modal = exchange(chunks, plan, plan.rows2)
 

time: 55.9 us -> 47 us (0.84); the launches traced: 55 us -> 46.7 us
  local copies, waits for them, and re-layouts: 14.1 us -> 1.79 us
  waiting for transfers between devices: 7.06 us -> 10.1 us
  Pallas kernels: 6.36 us -> 8.8 us
  starting transfers between devices: 12.2 us -> 11.2 us
    unnamed x90 -> x40, local copies, waits for them, and re-layouts: 13.2 us -> 1.6 us
    pallas_call x5 -> x6, Pallas kernels: 6.36 us -> 8.8 us  [call(): pl.pallas_call(body, out_shape=[jax.ShapeDtypeStruct(o, jnp.float32) for...]
    all_to_all x1, waiting for transfers between devices: 6.15 us -> 8.14 us  [exchange(): lax.all_to_all(flat, ('gx', 'gy'), split_axis=0, concat_axis=0, tiled=True)]
    ppermute x2, starting transfers between devices: 2.01 us -> 0.14 us  [swap(): lax.ppermute(a, axis, first)]
    ppermute x2, starting transfers between devices: 6.22 us -> 7.68 us  [swap(): lax.ppermute(b, axis, second)]
    ppermute x2, waiting for transfers between devices: 0.01 us -> 0.85 us  [swap(): lax.ppermute(a, axis, first)]
    pad x1 -> x0, local copies, waits for them, and re-layouts: 0.63 us -> none  [shards(): jnp.pad(jnp.swapaxes(drops, 1, 2), ((0, 0), (0, 0), (0, LANES - slots)))]
    all_to_all x1, starting transfers between devices: 3.94 us -> 3.35 us  [exchange(): lax.all_to_all(flat, ('gx', 'gy'), split_axis=0, concat_axis=0, tiled=True)]
  transfers between devices with their start and end apart: 5 -> 5, of which waited for: 2 -> 3; matrix products, arithmetic and copies ran while one was open for 3% -> 1% of each run, Pallas kernels for 3% -> 7%
where the time goes in v2:
time: 47 us; the launch traced here: 46.7 us
  blocking collectives  13.8 us (29%)
  starting transfers between devices  11.2 us (24%)
  waiting for transfers between devices  10.1 us (21%)
  Pallas kernels  8.8 us (19%)
  local copies, waits for them, and re-layouts  1.79 us (4%)
  between operations  0.88 us (2%)
    all_to_all x1, blocking collectives, exchange(): lax.all_to_all(flat, ('gx', 'gy'), split_axis=0, concat_axis=0, tiled=True)  13.8 us
    pallas_call x6, Pallas kernels, call(): pl.pallas_call(body, out_shape=[jax.ShapeDtypeStruct(o, jnp.float32) for...  8.8 us
    all_to_all x1, waiting for transfers between devices, exchange(): lax.all_to_all(flat, ('gx', 'gy'), split_axis=0, concat_axis=0, tiled=True)  8.14 us
    ppermute x2, starting transfers between devices, swap(): lax.ppermute(b, axis, second)  7.68 us
    all_to_all x1, starting transfers between devices, exchange(): lax.all_to_all(flat, ('gx', 'gy'), split_axis=0, concat_axis=0, tiled=True)  3.35 us
    unnamed x40, local copies, waits for them, and re-layouts  1.6 us
    ppermute x2, waiting for transfers between devices, swap(): lax.ppermute(b, axis, second)  1.13 us
  transfers between devices with their start and end apart: 5, of which 3 were waited for; matrix products, arithmetic and copies ran while one was open for 1% of the time, Pallas kernels for 7%

profile of v2, /device:TPU:0, one launch (start us, length us, event | category | flops | bytes accessed | tf_op | source)
XLA Modules:
  0.0 46.7 jit_solution(17540215855238156625)
XLA Ops:
  0.6 0.8 %shard_map.219.after = f32[5,32,128]{2,1,0:T(8,128)S(1)} custom-call(f32[3,16,32,128]{3,2,1,0:T(8,128)} %vel.7, f32[16,32,128]{2,1,0:T(8,128)} %theta.7, f32[16,32,128]{2,1,0:T(8,128)} %vapour.5), custom_call_target="tpu_custom_call" | custom-call | flops 65536 | bytes 1392640 | tf_op jit(solution)/shard_map/pallas_call | solution.py:549
  1.5 0.0 copy-start.3
  1.5 0.0 copy-start
  1.5 0.0 copy-start.1
  1.5 6.0 %collective-permute-start.1 = (f32[5,32,128]{2,1,0:T(8,128)S(1)}, f32[5,32,128]{2,1,0:T(8,128)S(1)}, u32[]{:S(2)}, u32[]{:S(2)}) collective-permute-start(f32[5,32,128]{2,1,0:T(8,128)S(1)} %shard_map.219.after), channel_id=1, source_target_pairs={{0,28},{4,8},{8,4},{12,16},{16,12},{20,24},{24,20},{28,0},{1,29},{... | collective-permute-start | bytes 245768 | tf_op jit(solution)/shard_map/ppermute | solution.py:562
  7.6 0.0 copy-done.3
  7.6 0.0 copy-start.10
  7.6 0.0 copy-start.11
  7.6 1.3 %shard_map.220 = (f32[5,32,128]{2,1,0:T(8,128)S(1)}, f32[5,16,128]{2,1,0:T(8,128)S(1)}, f32[5,16,128]{2,1,0:T(8,128)S(1)}) custom-call(f32[3,16,32,128]{3,2,1,0:T(8,128)} %vel.7, f32[16,32,128]{2,1,0:T(8,128)} %theta.7, f32[16,32,128]{2,1,0:T(8,128)} %vapour.5, f32[5,32,128]{2,1,0:T(8,128)} %copy-done.3), custom_call_target="tpu_custom_call" | custom-call | flops 65536 | bytes 1556480 | tf_op jit(solution)/shard_map/pallas_call | solution.py:549
  8.9 0.1 collective-permute-start
  9.0 0.1 collective-permute-start.2
  9.0 1.6 %collective-permute-start.3 = (f32[5,16,128]{2,1,0:T(8,128)S(1)}, f32[5,16,128]{2,1,0:T(8,128)S(1)}, u32[]{:S(2)}, u32[]{:S(2)}) collective-permute-start(f32[5,16,128]{2,1,0:T(8,128)S(1)} %get-tuple-element.17), channel_id=1, source_target_pairs={{0,3},{1,2},{2,1},{3,0},{4,7},{5,6},{6,5},{7,4},{8,11},{9,10},{10,... | collective-permute-start | bytes 122888 | tf_op jit(solution)/shard_map/ppermute | solution.py:562
  10.7 0.0 copy-start.19
  10.7 0.7 %copy-done.19 = f32[128]{0:T(128)S(1)} copy-done((f32[128]{0:T(128)S(1)}, f32[128]{0:T(128)}, u32[]{:S(2)}) %copy-start.19) | copy-done | bytes 536
  11.3 0.1 dynamic_slice.3
  11.4 0.0 collective-permute-done.2.ya
  11.4 1.1 %collective-permute-done.3.yb = f32[5,16,128]{2,1,0:T(8,128)S(1)} collective-permute-done((f32[5,16,128]{2,1,0:T(8,128)S(1)}, f32[5,16,128]{2,1,0:T(8,128)S(1)}, u32[]{:S(2)}, u32[]{:S(2)}) %collective-permute-start.3) | collective-permute-done | bytes 40992 | tf_op jit(solution)/shard_map/ppermute | solution.py:562
  12.5 0.0 collective-permute-done.1.xb
  12.5 0.9 %collective-permute-done.xa = f32[5,32,128]{2,1,0:T(8,128)S(1)} collective-permute-done((f32[5,32,128]{2,1,0:T(8,128)S(1)}, f32[5,32,128]{2,1,0:T(8,128)S(1)}, u32[]{:S(2)}, u32[]{:S(2)}) %collective-permute-start) | collective-permute-done | bytes 81952 | tf_op jit(solution)/shard_map/ppermute | solution.py:562
  13.4 0.0 copy-done
  13.4 0.0 copy-done.1
  13.4 0.0 copy-done.10
  13.4 0.0 copy-done.11
  13.4 1.8 %shard_map.221 = (f32[3,16,32,128]{3,2,1,0:T(8,128)S(1)}, f32[576,128]{1,0:T(8,128)}) custom-call(f32[3,16,32,128]{3,2,1,0:T(8,128)S(1)} %copy-done, f32[16,32,128]{2,1,0:T(8,128)S(1)} %copy-done.1, f32[5,32,128]{2,1,0:T(8,128)S(1)} %collective-permute-done.xa, f32[5,32,128]{2,1,0:T(8,128)S(1)} %collective-permute-done.1.xb, ...), custom_call_target="tpu_custom_call" | custom-call | flops 6553600 | bytes 2441216 | tf_op jit(solution)/shard_map/pallas_call | solution.py:549
  15.2 0.0 copy-start.18
  15.2 3.4 %all-to-all-start = ((f32[32,1,2304]{2,1,0:T(1,128)}), f32[32,1,2304]{2,1,0:T(1,128)S(1)}, u32[]{:S(2)}, u32[]{:S(2)}) async-start(f32[32,1,2304]{2,1,0:T(1,128)} %bitcast), calls=%async_computation | async-start | bytes 589824 | tf_op jit(solution)/shard_map/all_to_all | solution.py:567
  18.5 0.1 broadcast_bitcast_fusion
  18.6 0.0 copy-done.18
  18.6 0.1 broadcast_add_fusion
  18.8 0.0 copy-start.2
  18.8 0.0 copy-start.4
  18.8 0.0 copy-start.12
  18.8 0.0 copy-start.13
  18.8 0.0 copy-start.14
  18.8 0.0 copy-start.15
  18.8 0.1 compare_select_fusion.inverse
  18.9 0.0 copy-start.16
  18.9 0.0 copy-start.17
  18.9 0.8 %copy-done.2 = f32[16,32,128]{2,1,0:T(8,128)S(1)} copy-done((f32[16,32,128]{2,1,0:T(8,128)S(1)}, f32[16,32,128]{2,1,0:T(8,128)}, u32[]{:S(2)}) %copy-start.2) | copy-done | bytes 262168
  19.7 0.0 copy-done.4
  19.7 0.0 copy-done.12
  19.7 0.0 copy-done.13
  19.7 0.0 copy-done.14
  19.8 0.0 copy-done.15
  19.8 0.0 copy-done.16
  19.8 0.0 copy-done.17
  19.8 0.0 copy-start.5
  19.8 0.0 copy-start.7
  19.8 2.0 %shard_map.222 = (f32[16,32,128]{2,1,0:T(8,128)}, f32[16,32,128]{2,1,0:T(8,128)}, f32[8,128]{1,0:T(8,128)S(1)}, f32[32,128]{1,0:T(8,128)S(1)}) custom-call(f32[3,16,32,128]{3,2,1,0:T(8,128)S(1)} %copy-done, f32[16,32,128]{2,1,0:T(8,128)S(1)} %copy-done.1, f32[16,32,128]{2,1,0:T(8,128)S(1)} %copy-done.2, f32[5,32,128]{2,1,0:T(8,128)S(1)} %collective-permute-done.xa, ...), custom_call_target="tpu_custom_call" | custom-call | flops 6553600 | bytes 2282112 | tf_op jit(solution)/shard_map/pallas_call | solution.py:549
  21.8 8.1 %all-to-all-done = f32[32,1,2304]{2,1,0:T(1,128)S(1)} async-done(((f32[32,1,2304]{2,1,0:T(1,128)}), f32[32,1,2304]{2,1,0:T(1,128)S(1)}, u32[]{:S(2)}, u32[]{:S(2)}) %all-to-all-start) | async-done | bytes 294944 | tf_op jit(solution)/shard_map/all_to_all | solution.py:567
  29.9 0.0 copy-done.5
  29.9 0.0 copy-done.7
  29.9 1.6 %shard_map.223 = f32[608,128]{1,0:T(8,128)S(1)} custom-call(f32[576,128]{1,0:T(8,128)S(1)} %bitcast.17, f32[128,512]{1,0:T(8,128)S(1)} %compare_select_fusion.inverse, f32[32,128]{1,0:T(8,128)S(1)} %get-tuple-element.19.leave, bf16[2,128,128]{2,1,0:T(8,128)(2,1)S(1)} %copy-done.7, bf16[4,128,128]{2,1,0:T(8,128)(2,1)S(1)} %copy-done.5), custom_call_target="tpu_custom_call" | custom-call | flops 65536000 | bytes 1081344 | tf_op jit(solution)/shard_map/pallas_call | solution.py:549
  31.5 0.0 copy-start.6
  31.5 0.0 copy-start.8
  31.5 0.0 copy-start.9
  31.5 13.8 %all_to_all.10 = f32[32,1,2432]{2,1,0:T(1,128)S(1)} all-to-all(f32[32,1,2432]{2,1,0:T(1,128)S(1)} %bitcast.16), channel_id=1, replica_groups=mesh['gx'=8,'gy'=4] {'gx','gy'}, dimensions={0} | all-to-all | bytes 622592 | tf_op jit(solution)/shard_map/all_to_all | solution.py:567
  45.4 0.0 copy-done.6
  45.4 0.0 copy-done.8
  45.4 0.0 copy-done.9
  45.4 1.3 %shard_map.224 = (f32[3,16,32,128]{3,2,1,0:T(8,128)}, f32[3,32]{1,0:T(4,128)}) custom-call(f32[608,128]{1,0:T(8,128)S(1)} %bitcast.15, f32[3,16,32,128]{3,2,1,0:T(8,128)S(1)} %get-tuple-element.20.star, f32[8,128]{1,0:T(8,128)S(1)} %get-tuple-element.21.stay, bf16[128,128]{1,0:T(8,128)(2,1)S(1)} %copy-done.9, bf16[128,128]{1,0:T(8,128)(2,1)S(1)} %copy-done.8, ...), custom_call_target="tpu_custom_call" | custom-call | flops 6553600 | bytes 2019712 | tf_op jit(solution)/shard_map/pallas_call | solution.py:549
  (1 shorter events, 0.0 us)
Async XLA Ops:
  1.5 6.1 %copy-start.3 = (f32[5,32,128]{2,1,0:T(8,128)}, f32[5,32,128]{2,1,0:T(8,128)S(1)}, u32[]{:S(2)}) copy-start(f32[5,32,128]{2,1,0:T(8,128)S(1)} %shard_map.219.after) | copy-start | bytes 245764
  1.5 11.9 %copy-start = (f32[3,16,32,128]{3,2,1,0:T(8,128)S(1)}, f32[3,16,32,128]{3,2,1,0:T(8,128)}, u32[]{:S(2)}) copy-start(f32[3,16,32,128]{3,2,1,0:T(8,128)} %vel.7) | copy-start | bytes 2359300
  1.5 11.9 %copy-start.1 = (f32[16,32,128]{2,1,0:T(8,128)S(1)}, f32[16,32,128]{2,1,0:T(8,128)}, u32[]{:S(2)}) copy-start(f32[16,32,128]{2,1,0:T(8,128)} %theta.7) | copy-start | bytes 786436
  1.5 11.0 %collective-permute-start.1 = (f32[5,32,128]{2,1,0:T(8,128)S(1)}, f32[5,32,128]{2,1,0:T(8,128)S(1)}, u32[]{:S(2)}, u32[]{:S(2)}) collective-permute-start(f32[5,32,128]{2,1,0:T(8,128)S(1)} %shard_map.219.after), channel_id=1, source_target_pairs={{0,28},{4,8},{8,4},{12,16},{16,12},{20,24},{24,20},{28,0},{1,29},{... | collective-permute-start | bytes 245768 | tf_op jit(solution)/shard_map/ppermute | solution.py:562
  7.6 5.8 %copy-start.10 = (bf16[128,128]{1,0:T(8,128)(2,1)S(1)}, bf16[128,128]{1,0:T(8,128)(2,1)}, u32[]{:S(2)}) copy-start(bf16[128,128]{1,0:T(8,128)(2,1)} %constant.44.clone.fl) | copy-start | bytes 98308
  7.6 5.8 %copy-start.11 = (bf16[128,128]{1,0:T(8,128)(2,1)S(1)}, bf16[128,128]{1,0:T(8,128)(2,1)}, u32[]{:S(2)}) copy-start(bf16[128,128]{1,0:T(8,128)(2,1)} %constant.43.clone.fh) | copy-start | bytes 98308
  8.9 4.5 %collective-permute-start = (f32[5,32,128]{2,1,0:T(8,128)S(1)}, f32[5,32,128]{2,1,0:T(8,128)S(1)}, u32[]{:S(2)}, u32[]{:S(2)}) collective-permute-start(f32[5,32,128]{2,1,0:T(8,128)S(1)} %get-tuple-element.15), channel_id=1, source_target_pairs={{0,4},{4,0},{8,12},{12,8},{16,20},{20,16},{24,28},{28,24},{1,5},{5... | collective-permute-start | bytes 245768 | tf_op jit(solution)/shard_map/ppermute | solution.py:562
  9.0 2.4 %collective-permute-start.2 = (f32[5,16,128]{2,1,0:T(8,128)S(1)}, f32[5,16,128]{2,1,0:T(8,128)S(1)}, u32[]{:S(2)}, u32[]{:S(2)}) collective-permute-start(f32[5,16,128]{2,1,0:T(8,128)S(1)} %get-tuple-element.16), channel_id=1, source_target_pairs={{0,1},{1,0},{2,3},{3,2},{4,5},{5,4},{6,7},{7,6},{8,9},{9,8},{10,11... | collective-permute-start | bytes 122888 | tf_op jit(solution)/shard_map/ppermute | solution.py:562
  9.0 3.5 %collective-permute-start.3 = (f32[5,16,128]{2,1,0:T(8,128)S(1)}, f32[5,16,128]{2,1,0:T(8,128)S(1)}, u32[]{:S(2)}, u32[]{:S(2)}) collective-permute-start(f32[5,16,128]{2,1,0:T(8,128)S(1)} %get-tuple-element.17), channel_id=1, source_target_pairs={{0,3},{1,2},{2,1},{3,0},{4,7},{5,6},{6,5},{7,4},{8,11},{9,10},{10,... | collective-permute-start | bytes 122888 | tf_op jit(solution)/shard_map/ppermute | solution.py:562
  10.7 0.7 %copy-start.19 = (f32[128]{0:T(128)S(1)}, f32[128]{0:T(128)}, u32[]{:S(2)}) copy-start(f32[128]{0:T(128)} %constant.47.clone) | copy-start | bytes 1540
  15.2 3.4 %copy-start.18 = (f32[128]{0:T(128)S(1)}, f32[128]{0:T(128)}, u32[]{:S(2)}) copy-start(f32[128]{0:T(128)} %constant.48.clone) | copy-start | bytes 1540
  15.2 14.8 %all-to-all-start = ((f32[32,1,2304]{2,1,0:T(1,128)}), f32[32,1,2304]{2,1,0:T(1,128)S(1)}, u32[]{:S(2)}, u32[]{:S(2)}) async-start(f32[32,1,2304]{2,1,0:T(1,128)} %bitcast), calls=%async_computation | async-start | bytes 589824 | tf_op jit(solution)/shard_map/all_to_all | solution.py:567
  18.8 1.0 %copy-start.2 = (f32[16,32,128]{2,1,0:T(8,128)S(1)}, f32[16,32,128]{2,1,0:T(8,128)}, u32[]{:S(2)}) copy-start(f32[16,32,128]{2,1,0:T(8,128)} %vapour.5) | copy-start | bytes 786436
  18.8 1.0 %copy-start.4 = (f32[288,128]{1,0:T(8,128)S(1)}, f32[288,128]{1,0:T(8,128)}, u32[]{:S(2)}) copy-start(f32[288,128]{1,0:T(8,128)} %constant.45.clone.goes) | copy-start | bytes 442372
  18.8 1.0 %copy-start.12 = (f32[64,32]{0,1:T(8,128)S(1)}, f32[64,32]{0,1:T(8,128)}, u32[]{:S(2)}) copy-start(f32[64,32]{0,1:T(8,128)} %param.23) | copy-start | bytes 24580
  18.8 1.0 %copy-start.13 = (f32[64,32]{0,1:T(8,128)S(1)}, f32[64,32]{0,1:T(8,128)}, u32[]{:S(2)}) copy-start(f32[64,32]{0,1:T(8,128)} %param.24) | copy-start | bytes 24580
  18.8 1.0 %copy-start.14 = (s32[32,64]{1,0:T(8,128)S(1)}, s32[32,64]{1,0:T(8,128)}, u32[]{:S(2)}) copy-start(s32[32,64]{1,0:T(8,128)} %pairing.1) | copy-start | bytes 24580
  18.8 0.9 %copy-start.15 = (s32[64,32]{0,1:T(8,128)S(1)}, s32[64,32]{0,1:T(8,128)}, u32[]{:S(2)}) copy-start(s32[64,32]{0,1:T(8,128)} %param.27) | copy-start | bytes 24580
  18.9 0.9 %copy-start.16 = (s32[32]{0:T(128)S(1)}, s32[32]{0:T(128)}, u32[]{:S(2)}) copy-start(s32[32]{0:T(128)} %param.25) | copy-start | bytes 388
  18.9 0.9 %copy-start.17 = (s32[1,128]{1,0:T(1,128)S(1)}, s32[1,128]{1,0:T(1,128)}, u32[]{:S(2)}) copy-start(s32[1,128]{1,0:T(1,128)} %constant.46.clone.kind) | copy-start | bytes 1540
  19.8 10.2 %copy-start.5 = (bf16[4,128,128]{2,1,0:T(8,128)(2,1)S(1)}, bf16[4,128,128]{2,1,0:T(8,128)(2,1)}, u32[]{:S(2)}) copy-start(bf16[4,128,128]{2,1,0:T(8,128)(2,1)} %constant.50.clone.qx) | copy-start | bytes 393220
  19.8 10.2 %copy-start.7 = (bf16[2,128,128]{2,1,0:T(8,128)(2,1)S(1)}, bf16[2,128,128]{2,1,0:T(8,128)(2,1)}, u32[]{:S(2)}) copy-start(bf16[2,128,128]{2,1,0:T(8,128)(2,1)} %constant.49.clone.qy) | copy-start | bytes 196612
  31.5 13.9 %copy-start.6 = (f32[128,128]{1,0:T(8,128)S(1)}, f32[128,128]{1,0:T(8,128)}, u32[]{:S(2)}) copy-start(f32[128,128]{1,0:T(8,128)} %constant.53.clone.place) | copy-start | bytes 196612
  31.5 13.8 %copy-start.8 = (bf16[128,128]{1,0:T(8,128)(2,1)S(1)}, bf16[128,128]{1,0:T(8,128)(2,1)}, u32[]{:S(2)}) copy-start(bf16[128,128]{1,0:T(8,128)(2,1)} %constant.52.clone.bl) | copy-start | bytes 98308
  31.5 13.8 %copy-start.9 = (bf16[128,128]{1,0:T(8,128)(2,1)S(1)}, bf16[128,128]{1,0:T(8,128)(2,1)}, u32[]{:S(2)}) copy-start(bf16[128,128]{1,0:T(8,128)(2,1)} %constant.51.clone.bh) | copy-start | bytes 98308

commit v3 on v2

--- a/solution.py
+++ b/solution.py
@@ -13,8 +13,6 @@
 BW = 4
 LANES = 128
 
-EDGE_LIMIT = 55040 * 2**10
-
 TIME_STEP = 0.2
 DIFFUSION = 0.05
 BUOYANCY = 0.5
@@ -37,17 +35,38 @@
     return high, low
 
 
-def split(value):
+def on_left(table):
+    high, low = halves(table)
+    return np.block([[high, high], [low, np.zeros_like(low)]])
+
+
+def on_right(table):
+    high, low = halves(table)
+    return np.block([[high, low], [high, np.zeros_like(low)]])
+
+
+def split(value, axis):
     high = value.astype(jnp.bfloat16)
-    return high, (value - high.astype(jnp.float32)).astype(jnp.bfloat16)
-
-
-def dot3(left, right, dims=NN):
-    (lh, ll), (rh, rl) = left, right
-    dot = functools.partial(
-        lax.dot_general, dimension_numbers=dims, preferred_element_type=jnp.float32
-    )
-    return dot(lh, rh) + (dot(ll, rh) + dot(lh, rl))
+    low = (value - high.astype(jnp.float32)).astype(jnp.bfloat16)
+    return jnp.concatenate([high, low], axis=axis)
+
+
+def from_left(table, value, turned=False):
+    out = lax.dot_general(
+        table, split(value, 1 if turned else 0), NT if turned else NN,
+        preferred_element_type=jnp.float32,
+    )
+    rows = out.shape[0] // 2
+    return out[:rows] + out[rows:]
+
+
+def from_right(value, table, turned=False):
+    out = lax.dot_general(
+        split(value, 0 if turned else 1), table, TN if turned else NN,
+        preferred_element_type=jnp.float32,
+    )
+    columns = out.shape[1] // 2
+    return out[:, :columns] + out[:, columns:]
 
 
 def real_basis(length):
@@ -108,36 +127,29 @@
         copy.wait()
 
 
-def plane_copies(vel, theta, vapour, x, out, sems):
-    return [
-        pltpu.make_async_copy(vel.at[:, x], out.at[0:3], sems.at[0]),
-        pltpu.make_async_copy(theta.at[x], out.at[3], sems.at[1]),
-        pltpu.make_async_copy(vapour.at[x], out.at[4], sems.at[2]),
-    ]
-
-
-def far_kernel(plan, vel, theta, vapour, xb, sems):
+def planes_kernel(plan, vel, theta, vapour, xb, xa, sems):
     odd = lax.axis_index("gx") % 2
-    copy_all(plane_copies(vel, theta, vapour, (plan.sx - 1) * odd, xb, sems))
-
-
-def near_kernel(plan, vel, theta, vapour, after, xa, ya, yb, south, north, sems):
-    odd_x = lax.axis_index("gx") % 2
-    odd_y = lax.axis_index("gy") % 2 == 1
-    tile = south.shape[2]
-    copies = plane_copies(vel, theta, vapour, (plan.sx - 1) * (1 - odd_x), xa, sems.at[2])
-    for side, (out, y) in enumerate(((south, 0), (north, plan.sy - tile))):
+    copies = []
+    for side, (out, x) in enumerate(((xb, odd), (xa, 1 - odd))):
+        x = x * (plan.sx - 1)
         copies += [
-            pltpu.make_async_copy(vel.at[:, :, y : y + tile], out.at[0:3], sems.at[side, 0]),
-            pltpu.make_async_copy(theta.at[:, y : y + tile], out.at[3], sems.at[side, 1]),
-            pltpu.make_async_copy(vapour.at[:, y : y + tile], out.at[4], sems.at[side, 2]),
+            pltpu.make_async_copy(vel.at[:, x], out.at[0:3], sems.at[side, 0]),
+            pltpu.make_async_copy(theta.at[x], out.at[3], sems.at[side, 1]),
+            pltpu.make_async_copy(vapour.at[x], out.at[4], sems.at[side, 2]),
         ]
-    copy_all(copies)
-    for f in range(5):
-        low = jnp.concatenate([south[f, x, 0:1] for x in range(plan.sx)], axis=0)
-        high = jnp.concatenate([north[f, x, tile - 1 : tile] for x in range(plan.sx)], axis=0)
-        ya[f] = jnp.where(odd_y, low, high)
-        yb[f] = jnp.where(odd_y, high, low)
+    for copy in copies:
+        copy.start()
+    for copy in copies:
+        copy.wait()
+
+
+def rows_kernel(plan, vel, theta, vapour, after, yb, ya):
+    odd = lax.axis_index("gy") % 2 == 1
+    for f, ref in enumerate((vel.at[0], vel.at[1], vel.at[2], theta, vapour)):
+        for x in range(plan.sx):
+            low, high = ref[x, 0:1], ref[x, plan.sy - 1 :]
+            ya[f, x : x + 1] = jnp.where(odd, low, high)
+            yb[f, x : x + 1] = jnp.where(odd, high, low)
 
 
 def edge_masks(plan):
@@ -181,59 +193,96 @@
     return jnp.where(odd, ya[f], yb[f]), jnp.where(odd, yb[f], ya[f])
 
 
-def wind_kernel(plan, vel, theta, xa, xb, ya, yb, fh, fl, star, out):
+def before(value, axis):
+    at = lax.broadcasted_iota(jnp.int32, value.shape, axis)
+    return jnp.where(at == 0, 0.0, pltpu.roll(value, 1, axis))
+
+
+def inner_kernel(plan, vel, theta, div, along_x, along_y):
     masks = edge_masks(plan)
-    table = (fh[...], fl[...])
-    west_of, east_of, south_of, north_of = [], [], [], []
-    for f in range(3):
-        west, east = side_planes(xa, xb, f)
-        south, north = side_rows(ya, yb, f)
-        west_of.append(west)
-        east_of.append(east)
-        south_of.append(south)
-        north_of.append(north)
-    row0, _, lane0, _ = masks
+    zero = jnp.zeros((plan.sy, plan.nz), jnp.float32)
+    zero_row = jnp.zeros((1, plan.nz), jnp.float32)
+    last = plan.sx - 1
     last_u = None
-    slab = []
-    last_rows = []
     for x in range(plan.sx):
         coef = coefficients(vel[0, x], vel[1, x], vel[2, x])
-        s = []
-        for f in range(3):
-            west = vel[f, x - 1] if x else west_of[f]
-            east = vel[f, x + 1] if x < plan.sx - 1 else east_of[f]
-            s.append(
-                advect(
-                    vel[f, x], east, west, north_of[f][x : x + 1], south_of[f][x : x + 1],
-                    coef, masks, plan,
-                )
+        u, v, w = (
+            advect(
+                vel[f, x],
+                vel[f, x + 1] if x < last else zero,
+                vel[f, x - 1] if x else zero,
+                zero_row, zero_row, coef, masks, plan,
             )
-        s[2] = s[2] + (TIME_STEP * BUOYANCY) * theta[x]
-        for f in range(3):
-            star[f, x] = s[f]
-        div = s[0] if last_u is None else s[0] - last_u
-        div = div + (s[1] - jnp.where(row0, 0.0, pltpu.roll(s[1], 1, 0)))
-        div = div + (s[2] - jnp.where(lane0, 0.0, pltpu.roll(s[2], 1, 1)))
-        last_u = s[0]
-        last_rows.append(s[1][plan.sy - 1 : plan.sy])
-        slab.append(div)
-        if len(slab) == plan.x4:
-            g = x // plan.x4
-            modes = dot3(table, split(jnp.concatenate(slab, axis=0)), NT)
-            for j in range(plan.per):
-                out[pl.ds(j * plan.xg + g, plan.nd, stride=plan.rows1), :] = modes[
-                    j * plan.nd : (j + 1) * plan.nd
-                ]
-            slab = []
+            for f in range(3)
+        )
+        w = w + (TIME_STEP * BUOYANCY) * theta[x]
+        total = (u if last_u is None else u - last_u) + (v - before(v, 0)) + (w - before(w, 1))
+        div[x] = total
+        last_u = u
+        along_y[0, x : x + 1] = v[plan.sy - 1 : plan.sy]
+        along_y[1, x : x + 1] = coef[3][0:1]
+        along_y[2, x : x + 1] = coef[2][plan.sy - 1 : plan.sy]
+        if x == 0:
+            along_x[1] = coef[1]
+        if x == last:
+            along_x[0] = u
+            along_x[2] = coef[0]
+
+
+def spread_kernel(plan, div, along_x, along_y, xb, yb, xa, ya, forward, out):
+    sides = [side_planes(xa, xb, f) for f in range(3)]
+    ends = [side_rows(ya, yb, f) for f in range(3)]
+    west_u, west_v, west_w = (along_x[1] * west for west, _ in sides)
+    east_u, east_v, east_w = (along_x[2] * east for _, east in sides)
+    south_u, south_v, south_w = (along_y[1] * south for south, _ in ends)
+    north_u, north_v, north_w = (along_y[2] * north for _, north in ends)
+    first_row = south_u - before(south_u, 0) + south_v + south_w - before(south_w, 1)
+    last_row = north_u - before(north_u, 0) + north_v + north_w - before(north_w, 1)
+    row = lax.broadcasted_iota(jnp.int32, (plan.sy, plan.nz), 0)
+    last = plan.sx - 1
+    slab = []
+    for x in range(plan.sx):
+        at = slice(x, x + 1)
+        total = div[x] + jnp.where(
+            row == 0,
+            first_row[at],
+            jnp.where(
+                row == 1, -south_v[at], jnp.where(row == plan.sy - 1, last_row[at], 0.0)
+            ),
+        )
+        if x == 0:
+            total = total + west_u + (west_v - before(west_v, 0)) + (west_w - before(west_w, 1))
+        if x == 1:
+            total = total - west_u
+        if x == last:
+            total = total + east_u + (east_v - before(east_v, 0)) + (east_w - before(east_w, 1))
+        slab.append(total)
+    last_u = along_x[0] + east_u + jnp.where(
+        row == 0, south_u[last:], jnp.where(row == plan.sy - 1, north_u[last:], 0.0)
+    )
+    column = lax.broadcasted_iota(jnp.int32, (plan.sx, plan.nz), 0)
+    last_v = along_y[0] + north_v + jnp.where(
+        column == 0,
+        west_v[plan.sy - 1 :],
+        jnp.where(column == last, east_v[plan.sy - 1 :], 0.0),
+    )
     tiled_plane = jnp.concatenate([-last_u] * plan.x4, axis=0)
-    row = lax.broadcasted_iota(jnp.int32, (plan.sy, plan.nz), 0)
     tiled_rows = []
     for p in range(plan.x4):
         block = jnp.zeros((plan.sy, plan.nz), jnp.float32)
         for g in range(plan.xg):
-            block = jnp.where(row % plan.xg == g, -last_rows[g * plan.x4 + p], block)
+            at = g * plan.x4 + p
+            block = jnp.where(row % plan.xg == g, -last_v[at : at + 1], block)
         tiled_rows.append(block)
-    extra = dot3(table, split(jnp.concatenate([tiled_plane] + tiled_rows, axis=0)), NT)
+    modes = from_left(
+        forward[...], jnp.concatenate(slab + [tiled_plane] + tiled_rows, axis=0), turned=True
+    )
+    for g in range(plan.xg):
+        for j in range(plan.per):
+            out[pl.ds(j * plan.xg + g, plan.nd, stride=plan.rows1), :] = modes[
+                j * plan.nd : (j + 1) * plan.nd, g * LANES : (g + 1) * LANES
+            ]
+    extra = modes[:, plan.xg * LANES :]
     lane = lax.broadcasted_iota(jnp.int32, (plan.nd, LANES), 1)
     plane_sum = jnp.zeros((plan.nd, LANES), jnp.float32)
     row_sum = jnp.zeros((plan.nd, LANES), jnp.float32)
@@ -245,22 +294,34 @@
     out[pl.ds(plan.main + 1, plan.nd, stride=plan.rows1), :] = row_sum
 
 
-def solve_kernel(plan, r, inverse, leave, qy, qx, out, wide):
+def regroup(parts, plan):
+    group = lax.broadcasted_iota(jnp.int32, parts[0].shape, 1) // plan.sy
+    parts = list(parts)
+    distance = plan.x4 // 2
+    while distance:
+        lower = group & distance == 0
+        step = distance * plan.sy
+        for i in range(plan.x4):
+            if not i & distance:
+                one, two = parts[i], parts[i + distance]
+                parts[i] = jnp.where(lower, one, pltpu.roll(two, step, 1))
+                parts[i + distance] = jnp.where(lower, pltpu.roll(one, LANES - step, 1), two)
+        distance //= 2
+    return parts
+
+
+def solve_kernel(plan, r, leave, eigen_x, eigen_yz, tables, out):
+    wide_x, wide_y = 2 * plan.tx, 2 * plan.ty
+    fy, by = tables[0, :wide_y, :wide_y], tables[1, :wide_y, :wide_y]
+    fx, bx = tables[2, :wide_x, :wide_x], tables[3, :wide_x, :wide_x]
+    rank = lax.axis_index("gx") * plan.gy + lax.axis_index("gy")
+    eigen = eigen_x[...] + eigen_yz[pl.ds(rank, 1), :]
+    inverse = jnp.where(eigen == 0.0, 0.0, 1.0 / jnp.where(eigen == 0.0, 1.0, eigen))
     gx, gy, per, xg, x4 = plan.gx, plan.gy, plan.per, plan.xg, plan.x4
     lane = lax.broadcasted_iota(jnp.int32, (gx, LANES), 1)
     first_lanes = lane < plan.sy
     first_rows = lane % plan.sy == 0
     step1, step2 = gy * plan.rows1, gy * plan.rows2
-
-    for part in range(2):
-        wide[part] = jnp.zeros(wide.shape[1:], wide.dtype)
-        for b in range(gy):
-            for p in range(x4):
-                at = b * LANES + p * plan.sy
-                wide[part, at : at + plan.sy, p * plan.ty : (p + 1) * plan.ty] = qy[
-                    part, b * plan.sy : (b + 1) * plan.sy
-                ]
-    table_y = (wide[0], wide[1])
 
     def take(b, q):
         return r[pl.ds(b * plan.rows1 + q, gx, stride=step1), :]
@@ -276,34 +337,52 @@
             moved = rows if q == 0 else pltpu.roll(rows, LANES - q, 1)
             nb = (b + 1) % gy
             blocks[nb][q] = blocks[nb][q] + jnp.where(first_rows, moved, 0.0)
-    grid = jnp.concatenate([jnp.concatenate(column, axis=0) for column in blocks], axis=1)
-    in_y = dot3(split(grid), table_y)
+    turned = [
+        [regroup([blocks[h + i][q] for i in range(x4)], plan) for h in range(0, gy, x4)]
+        for q in range(plan.main)
+    ]
+    grid = jnp.concatenate(
+        [
+            jnp.concatenate([part[p] for part in turned[q]], axis=1)
+            for p in range(x4)
+            for q in range(plan.main)
+        ],
+        axis=0,
+    )
+    in_y = from_right(grid, fy)
     height = xg * gx
 
-    def swap(value, outer, inner):
-        return jnp.concatenate(
-            [
-                jnp.concatenate(
-                    [
-                        value[o * height : (o + 1) * height, i * plan.ty : (i + 1) * plan.ty]
-                        for o in range(outer)
-                    ],
-                    axis=1,
-                )
-                for i in range(inner)
-            ],
-            axis=0,
-        )
-
-    spectral = dot3((qx[0], qx[1]), split(swap(in_y, per, x4)))
-    solved = spectral * inverse[...]
-    in_x = dot3((qx[2], qx[3]), split(solved))
-    grid = dot3(split(swap(in_x, x4, per)), table_y, NT)
+    def piece(value, row, column):
+        return value[row * height : (row + 1) * height, column * plan.ty : (column + 1) * plan.ty]
+
+    in_y = jnp.concatenate(
+        [
+            jnp.concatenate([piece(in_y, p * per + j, 0) for p in range(x4)], axis=0)
+            for j in range(per)
+        ],
+        axis=1,
+    )
+    solved = from_left(fx, in_y) * inverse
+    in_x = from_left(bx, solved)
+    in_x = jnp.concatenate([piece(in_x, p, j) for p in range(x4) for j in range(per)], axis=0)
+    grid = from_right(in_x, by)
+    blocks = [[None] * plan.main for _ in range(gy)]
+    for q in range(plan.main):
+        for h in range(0, gy, x4):
+            parts = [
+                grid[
+                    (p * plan.main + q) * gx : (p * plan.main + q + 1) * gx,
+                    h * plan.sy : h * plan.sy + LANES,
+                ]
+                for p in range(x4)
+            ]
+            for i, part in enumerate(regroup(parts, plan)):
+                blocks[h + i][q] = part
     planes = [jnp.zeros((gx, LANES), jnp.float32) for _ in range(gy)]
     rows = [jnp.zeros((gx, LANES), jnp.float32) for _ in range(gy)]
     for b in range(gy):
         for q in range(plan.main):
-            block = grid[q * gx : (q + 1) * gx, b * LANES : (b + 1) * LANES]
+            block = blocks[b][q]
             out[pl.ds(b * plan.rows2 + q, gx, stride=step2), :] = block
             moved = jnp.where(first_rows, block, 0.0)
             nb = (b - 1) % gy
@@ -320,9 +399,8 @@
     out[pl.ds(plan.main + 2, plan.nd, stride=plan.rows2), :] = leave[...]
 
 
-def project_kernel(plan, r, star, stay, bh, bl, place, vel_new, moments, scratch):
+def project_kernel(plan, r, star, stay, backward, place, vel_new, moments, scratch):
     nd, per, xg, x4, sy, sx = plan.nd, plan.per, plan.xg, plan.x4, plan.sy, plan.sx
-    table = (bh[...], bl[...])
     lane = lax.broadcasted_iota(jnp.int32, (nd, LANES), 1)
 
     def take(q):
@@ -338,18 +416,18 @@
         ],
         axis=1,
     )
-    extra = dot3(split(wide), table, TN)
+    modes = [
+        jnp.concatenate([take(j * xg + g) for j in range(per)], axis=0) for g in range(xg)
+    ]
+    cells = from_right(jnp.concatenate(modes + [wide], axis=1), backward[...], turned=True)
+    extra = cells[xg * LANES :]
     beyond = extra[0:sy]
     for j in range(1, per):
         beyond = beyond + extra[j * sy : (j + 1) * sy]
     scratch[...] = extra[LANES:]
     row = lax.broadcasted_iota(jnp.int32, (sy, plan.nz), 0)
     level = lax.broadcasted_iota(jnp.int32, (sy, plan.nz), 1)
-    pressure = []
-    for g in range(xg):
-        modes = jnp.concatenate([take(j * xg + g) for j in range(per)], axis=0)
-        slab = dot3(split(modes), table, TN)
-        pressure += [slab[p * sy : (p + 1) * sy] for p in range(x4)]
+    pressure = [cells[x * sy : (x + 1) * sy] for x in range(sx)]
     pressure.append(beyond)
     for x in range(sx):
         here = pressure[x]
@@ -418,13 +496,13 @@
 
 
 def scalar_kernel(
-    plan, vel, theta, vapour, xa, xb, ya, yb, radius, multiplicity, counts, pairing,
-    destination, goes, kind, theta_new, vapour_new, stay, leave, moist,
+    plan, vel, theta, vapour, xb, yb, xa, ya, radius, multiplicity, counts, pairing,
+    destination, goes, kind, star, theta_new, vapour_new, stay, leave, moist,
 ):
     masks = edge_masks(plan)
     bx, by, boxes = plan.bx, plan.by, plan.boxes
     edges = []
-    for f in (3, 4):
+    for f in range(5):
         west, east = side_planes(xa, xb, f)
         south, north = side_rows(ya, yb, f)
         edges.append((west, east, south, north))
@@ -432,16 +510,17 @@
     total = None
     for x in range(plan.sx):
         coef = coefficients(vel[0, x], vel[1, x], vel[2, x])
-        for ref, new, (west, east, south, north) in (
-            (theta, theta_new, edges[0]),
-            (vapour, moist, edges[1]),
-        ):
+        for f, (west, east, south, north) in enumerate(edges):
+            ref = (vel.at[0], vel.at[1], vel.at[2], theta, vapour)[f]
+            new = (star.at[0], star.at[1], star.at[2], theta_new, moist)[f]
             moved = advect(
                 ref[x],
                 ref[x + 1] if x < plan.sx - 1 else east,
                 ref[x - 1] if x else west,
                 north[x : x + 1], south[x : x + 1], coef, masks, plan,
             )
+            if f == 2:
+                moved = moved + (TIME_STEP * BUOYANCY) * theta[x]
             new[x] = moved
         total = moved if x % BW == 0 else total + moved
         if x % BW == BW - 1:
@@ -543,7 +622,7 @@
     leave[...] = jnp.where(every == owner, payload, 0.0)
 
 
-def call(body, outs, args, flops, scratch=(), space=VMEM, limit=8 * 2**20):
+def call(body, outs, args, flops, scratch=(), space=VMEM):
     moved = sum(a.size * a.dtype.itemsize for a in args)
     moved += sum(math.prod(o) * 4 for o in outs)
     return pl.pallas_call(
@@ -552,14 +631,9 @@
         in_specs=[space] * len(args),
         out_specs=[VMEM] * len(outs),
         scratch_shapes=list(scratch),
-        compiler_params=pltpu.CompilerParams(vmem_limit_bytes=limit),
+        compiler_params=pltpu.CompilerParams(vmem_limit_bytes=16 * 2**20),
         cost_estimate=pl.CostEstimate(flops=flops, bytes_accessed=moved, transcendentals=0),
     )(*args)
-
-
-def swap(block, axis):
-    first, second = neighbours(lax.axis_size(axis))
-    return (lambda a, b: (lax.ppermute(a, axis, first), lax.ppermute(b, axis, second)))(*block)
 
 
 def exchange(chunks, plan, rows):
@@ -572,8 +646,6 @@
     span_x, span_y, levels = theta.shape
     slots = radius_sq.shape[0]
     plan = Plan(lax.axis_size("gx"), lax.axis_size("gy"), span_x, span_y, levels, slots)
-    rank_x, rank_y = lax.axis_index("gx"), lax.axis_index("gy")
-    rank = rank_x * plan.gy + rank_y
     forward, backward, q1, qy, ex, ey, ez = plan.tables()
     goes, place, kind = droplet_tables(plan)
     block = (span_x, span_y, levels)
@@ -581,55 +653,53 @@
 
     plane, rows = (5, span_y, levels), (5, span_x, levels)
     fields = (velocity, theta, vapour)
-    (xb,) = call(
-        functools.partial(far_kernel, plan), (plane,), fields, cells,
-        [pltpu.SemaphoreType.DMA((3,))], HBM, EDGE_LIMIT,
-    )
-    xa, ya, yb = call(
-        functools.partial(near_kernel, plan), (plane, rows, rows), fields + (xb,), cells,
-        [pltpu.VMEM((5, span_x, 8, levels), jnp.float32)] * 2 + [pltpu.SemaphoreType.DMA((3, 3))],
-        HBM, EDGE_LIMIT,
-    )
-    xa, xb = swap((xa, xb), "gx")
-    ya, yb = swap((ya, yb), "gy")
-
-    star, chunks = call(
-        functools.partial(wind_kernel, plan),
-        ((3,) + block, (plan.nd * plan.rows1, LANES)),
-        (velocity, theta, xa, xb, ya, yb) + halves(forward),
-        100 * cells,
+    placed = [pltpu.with_memory_space_constraint(f, pltpu.HBM) for f in fields]
+    xb, xa = call(
+        functools.partial(planes_kernel, plan), (plane, plane), placed, cells,
+        [pltpu.SemaphoreType.DMA((2, 3))], HBM,
+    )
+    yb, ya = call(functools.partial(rows_kernel, plan), (rows, rows), (*fields, xa), cells)
+    ways_x, ways_y = neighbours(plan.gx), neighbours(plan.gy)
+    xb, xa = lax.ppermute(xb, "gx", ways_x[1]), lax.ppermute(xa, "gx", ways_x[0])
+    yb, ya = lax.ppermute(yb, "gy", ways_y[1]), lax.ppermute(ya, "gy", ways_y[0])
+    halo = (xb, yb, xa, ya)
+
+    inner = call(
+        functools.partial(inner_kernel, plan),
+        (block, (3, span_y, levels), (3, span_x, levels)), (velocity, theta), 100 * cells,
+    )
+    (chunks,) = call(
+        functools.partial(spread_kernel, plan), ((plan.nd * plan.rows1, LANES),),
+        (*inner, *halo, on_left(forward)), 100 * cells,
     )
     spectral = exchange(chunks, plan, plan.rows1)
 
-    theta_new, vapour_new, stay, leave = call(
+    tables = [on_right(qy), on_right(qy.T), on_left(q1), on_left(q1.T)]
+    most = max(t.shape[0] for t in tables)
+    tables = np.stack([np.pad(t, (0, most - t.shape[0])) for t in tables])
+    eigen_x = ex.astype(np.float32)[:, None]
+    eigen_yz = (ez.reshape(plan.nd, plan.per, 1) + ey).reshape(plan.nd, -1).astype(np.float32)
+    star, theta_new, vapour_new, stay, leave = call(
         functools.partial(scalar_kernel, plan),
-        (block, block, (8, LANES), (plan.nd, LANES)),
-        fields + (xa, xb, ya, yb, radius_sq.T, multiplicity.T, counts[None], pairing)
+        ((3,) + block, block, block, (8, LANES), (plan.nd, LANES)),
+        fields + halo + (radius_sq.T, multiplicity.T, counts[None], pairing)
         + (destination.T, goes, kind),
         100 * cells,
         (pltpu.VMEM(block, jnp.float32),),
     )
 
-    modes = lax.dynamic_slice(jnp.asarray(ez, jnp.float32), (rank * plan.per,), (plan.per,))
-    eigen = (
-        jnp.asarray(ex, jnp.float32)[:, None, None]
-        + jnp.asarray(ey, jnp.float32)[None, None, :]
-        + modes[None, :, None]
-    ).reshape(plan.tx, plan.per * plan.ty)
-    inverse = jnp.where(eigen == 0.0, 0.0, 1.0 / jnp.where(eigen == 0.0, 1.0, eigen))
     (chunks,) = call(
         functools.partial(solve_kernel, plan),
         ((plan.nd * plan.rows2, LANES),),
-        (spectral, inverse, leave, np.stack(halves(qy)), np.stack(halves(q1) + halves(q1.T))),
+        (spectral, leave, eigen_x, eigen_yz, tables),
         1000 * cells,
-        [pltpu.VMEM((2, plan.gy * LANES, plan.x4 * plan.ty), jnp.bfloat16)],
     )
     modal = exchange(chunks, plan, plan.rows2)
 
     velocity_new, moments = call(
         functools.partial(project_kernel, plan),
         ((3,) + block, (3, plan.boxes)),
-        (modal, star, stay) + halves(backward) + (place,),
+        (modal, star, stay, on_right(backward), place),
         100 * cells,
         (pltpu.VMEM((LANES, levels), jnp.float32),),
     )

time: 47 us -> 45.6 us (0.970)
  local copies, waits for them, and re-layouts: 1.79 us -> 0.67 us
  starting transfers between devices: 11.2 us -> 11.8 us
  waiting for transfers between devices: 10.1 us -> 9.53 us
    unnamed x40 -> x32, local copies, waits for them, and re-layouts: 1.6 us -> 0.67 us
    ppermute x4, waiting for transfers between devices: 1.98 us -> 1.25 us  [the longest x1 0.76 us: shards(): lax.ppermute(yb, 'gy', ways_y[1])]
    all_to_all x1, starting transfers between devices: 3.35 us -> 4.03 us  [exchange(): lax.all_to_all(flat, ('gx', 'gy'), split_axis=0, concat_axis=0, tiled=True)]
    pallas_call x6 -> x7, Pallas kernels: 8.8 us -> 8.65 us  [call(): pl.pallas_call(body, out_shape=[jax.ShapeDtypeStruct(o, jnp.float32) for...]
  transfers between devices with their start and end apart: 5 -> 5, of which waited for: 3 -> 3; matrix products, arithmetic and copies ran while one was open for 1% -> 0% of each run, Pallas kernels for 7% -> 9%
where the time goes in v3:
time: 45.6 us; the launch traced here: 45.2 us
  blocking collectives  13.8 us (30%)
  starting transfers between devices  11.8 us (26%)
  waiting for transfers between devices  9.53 us (21%)
  Pallas kernels  8.65 us (19%)
  between operations  0.79 us (2%)
  local copies, waits for them, and re-layouts  0.67 us (1%)
    all_to_all x1, blocking collectives, exchange(): lax.all_to_all(flat, ('gx', 'gy'), split_axis=0, concat_axis=0, tiled=True)  13.8 us
    pallas_call x7, Pallas kernels, call(): pl.pallas_call(body, out_shape=[jax.ShapeDtypeStruct(o, jnp.float32) for...  8.65 us
    all_to_all x1, waiting for transfers between devices, exchange(): lax.all_to_all(flat, ('gx', 'gy'), split_axis=0, concat_axis=0, tiled=True)  8.28 us
    ppermute x1, starting transfers between devices, shards(): lax.ppermute(xb, 'gx', ways_x[1])  6.04 us
    all_to_all x1, starting transfers between devices, exchange(): lax.all_to_all(flat, ('gx', 'gy'), split_axis=0, concat_axis=0, tiled=True)  4.03 us
    ppermute x1, starting transfers between devices, shards(): lax.ppermute(ya, 'gy', ways_y[0])  0.96 us
  transfers between devices with their start and end apart: 5, of which 3 were waited for; matrix products, arithmetic and copies ran while one was open for 0% of the time, Pallas kernels for 9%

profile of v3, /device:TPU:0, one launch (start us, length us, event | category | flops | bytes accessed | tf_op | source)
XLA Modules:
  0.0 45.2 jit_solution(7302994076229325321)
XLA Ops:
  0.6 0.0 copy-start.1
  0.6 0.0 copy-start
  0.7 0.0 copy-start.2
  0.7 1.0 %shard_map.184 = (f32[5,32,128]{2,1,0:T(8,128)S(1)}, f32[5,32,128]{2,1,0:T(8,128)S(1)}) custom-call(f32[3,16,32,128]{3,2,1,0:T(8,128)} %vel.7, f32[16,32,128]{2,1,0:T(8,128)} %theta.7, f32[16,32,128]{2,1,0:T(8,128)} %vapour.5), custom_call_target="tpu_custom_call" | custom-call | flops 65536 | bytes 1474560 | tf_op jit(solution)/shard_map/pallas_call | solution.py:628
  1.7 6.0 %collective-permute-start = (f32[5,32,128]{2,1,0:T(8,128)S(1)}, f32[5,32,128]{2,1,0:T(8,128)S(1)}, u32[]{:S(2)}, u32[]{:S(2)}) collective-permute-start(f32[5,32,128]{2,1,0:T(8,128)S(1)} %get-tuple-element.21), channel_id=1, source_target_pairs={{0,28},{4,8},{8,4},{12,16},{16,12},{20,24},{24,20},{28,0},{1,29},{... | collective-permute-start | bytes 245768 | tf_op jit(solution)/shard_map/ppermute | solution.py:663
  7.7 0.0 collective-permute-start.2
  7.7 0.0 copy-done.1
  7.7 0.0 copy-done
  7.7 0.0 copy-done.2
  7.8 0.1 shard_map.185
  7.8 0.7 %collective-permute-start.1 = (f32[5,16,128]{2,1,0:T(8,128)S(1)}, f32[5,16,128]{2,1,0:T(8,128)S(1)}, u32[]{:S(2)}, u32[]{:S(2)}) collective-permute-start(f32[5,16,128]{2,1,0:T(8,128)S(1)} %get-tuple-element.23), channel_id=1, source_target_pairs={{0,3},{1,2},{2,1},{3,0},{4,7},{5,6},{6,5},{7,4},{8,11},{9,10},{10,... | collective-permute-start | bytes 122888 | tf_op jit(solution)/shard_map/ppermute | solution.py:664
  8.6 0.0 copy-start.6
  8.6 1.0 %collective-permute-start.3 = (f32[5,16,128]{2,1,0:T(8,128)S(1)}, f32[5,16,128]{2,1,0:T(8,128)S(1)}, u32[]{:S(2)}, u32[]{:S(2)}) collective-permute-start(f32[5,16,128]{2,1,0:T(8,128)S(1)} %get-tuple-element.24), channel_id=1, source_target_pairs={{0,1},{1,0},{2,3},{3,2},{4,5},{5,4},{6,7},{7,6},{8,9},{9,8},{10,11... | collective-permute-start | bytes 122888 | tf_op jit(solution)/shard_map/ppermute | solution.py:664
  9.5 1.4 %shard_map.183 = (f32[16,32,128]{2,1,0:T(8,128)S(1)}, f32[3,32,128]{2,1,0:T(8,128)S(1)}, f32[3,16,128]{2,1,0:T(8,128)S(1)}) custom-call(f32[3,16,32,128]{3,2,1,0:T(8,128)S(1)} %copy-done, f32[16,32,128]{2,1,0:T(8,128)S(1)} %copy-done.1), custom_call_target="tpu_custom_call" | custom-call | flops 6553600 | bytes 1384448 | tf_op jit(solution)/shard_map/pallas_call | solution.py:628
  10.9 0.8 %collective-permute-done.1.yb = f32[5,16,128]{2,1,0:T(8,128)S(1)} collective-permute-done((f32[5,16,128]{2,1,0:T(8,128)S(1)}, f32[5,16,128]{2,1,0:T(8,128)S(1)}, u32[]{:S(2)}, u32[]{:S(2)}) %collective-permute-start.1) | collective-permute-done | bytes 40992 | tf_op jit(solution)/shard_map/ppermute | solution.py:664
  11.7 0.0 collective-permute-done.3.ya
  11.7 0.0 collective-permute-done.xb
  11.7 0.5 %collective-permute-done.2.xa = f32[5,32,128]{2,1,0:T(8,128)S(1)} collective-permute-done((f32[5,32,128]{2,1,0:T(8,128)S(1)}, f32[5,32,128]{2,1,0:T(8,128)S(1)}, u32[]{:S(2)}, u32[]{:S(2)}) %collective-permute-start.2) | collective-permute-done | bytes 81952 | tf_op jit(solution)/shard_map/ppermute | solution.py:663
  12.2 0.0 copy-done.6
  12.2 1.1 %shard_map.186 = f32[576,128]{1,0:T(8,128)} custom-call(f32[16,32,128]{2,1,0:T(8,128)S(1)} %get-tuple-element.18.div, f32[3,32,128]{2,1,0:T(8,128)S(1)} %get-tuple-element.19.along_x, f32[3,16,128]{2,1,0:T(8,128)S(1)} %get-tuple-element.20.along_y, f32[5,32,128]{2,1,0:T(8,128)S(1)} %collective-permute-done.xb, f32[5,16,128]{2,1,0:T(8,128)S(1)} %collective-permute-done.1.yb, ...), custom_call_target="tpu_custom_call" | custom-call | flops 6553600 | bytes 1007616 | tf_op jit(solution)/shard_map/pallas_call | solution.py:628
  13.3 0.0 copy-start.4
  13.3 0.0 copy-start.10
  13.3 0.0 copy-start.11
  13.3 0.0 copy-start.12
  13.3 0.0 copy-start.13
  13.3 4.0 %all-to-all-start = ((f32[32,1,2304]{2,1,0:T(1,128)}), f32[32,1,2304]{2,1,0:T(1,128)S(1)}, u32[]{:S(2)}, u32[]{:S(2)}) async-start(f32[32,1,2304]{2,1,0:T(1,128)} %bitcast), calls=%async_computation | async-start | bytes 589824 | tf_op jit(solution)/shard_map/all_to_all | solution.py:641
  17.3 0.0 copy-start.14
  17.4 0.0 copy-start.15
  17.4 0.0 copy-done.4
  17.4 0.0 copy-done.10
  17.4 0.0 copy-done.11
  17.4 0.0 copy-done.12
  17.4 0.0 copy-done.13
  17.4 0.6 %copy-done.14 = s32[32]{0:T(128)S(1)} copy-done((s32[32]{0:T(128)S(1)}, s32[32]{0:T(128)}, u32[]{:S(2)}) %copy-start.14) | copy-done | bytes 152
  18.0 0.0 copy-done.15
  18.0 0.0 copy-start.3
  18.0 0.0 copy-start.8
  18.0 0.0 copy-start.9
  18.0 2.4 %shard_map.187 = (f32[3,16,32,128]{3,2,1,0:T(8,128)S(1)}, f32[16,32,128]{2,1,0:T(8,128)}, f32[16,32,128]{2,1,0:T(8,128)}, f32[8,128]{1,0:T(8,128)S(1)}, f32[32,128]{1,0:T(8,128)S(1)}) custom-call(f32[3,16,32,128]{3,2,1,0:T(8,128)S(1)} %copy-done, f32[16,32,128]{2,1,0:T(8,128)S(1)} %copy-done.1, f32[16,32,128]{2,1,0:T(8,128)S(1)} %copy-done.2, ...), custom_call_target="tpu_custom_call" | custom-call | flops 6553600 | bytes 3068544 | tf_op jit(solution)/shard_map/pallas_call | solution.py:628
  20.5 8.3 %all-to-all-done = f32[32,1,2304]{2,1,0:T(1,128)S(1)} async-done(((f32[32,1,2304]{2,1,0:T(1,128)}), f32[32,1,2304]{2,1,0:T(1,128)S(1)}, u32[]{:S(2)}, u32[]{:S(2)}) %all-to-all-start) | async-done | bytes 294944 | tf_op jit(solution)/shard_map/all_to_all | solution.py:641
  28.7 0.0 copy-done.3
  28.7 0.0 copy-done.8
  28.7 0.0 copy-done.9
  28.8 1.4 %shard_map.188 = f32[608,128]{1,0:T(8,128)S(1)} custom-call(f32[576,128]{1,0:T(8,128)S(1)} %bitcast.10, f32[32,128]{1,0:T(8,128)S(1)} %get-tuple-element.25.leave, f32[128,1]{1,0:T(8,128)S(1)} %copy-done.9, f32[32,512]{1,0:T(8,128)S(1)} %copy-done.8, bf16[4,256,256]{2,1,0:T(8,128)(2,1)S(1)} %copy-done.3), custom_call_target="tpu_custom_call" | custom-call | flops 65536000 | bytes 1212928 | tf_op jit(solution)/shard_map/pallas_call | solution.py:628
  30.1 0.0 copy-start.5
  30.1 0.0 copy-start.7
  30.1 13.8 %all_to_all.10 = f32[32,1,2432]{2,1,0:T(1,128)S(1)} all-to-all(f32[32,1,2432]{2,1,0:T(1,128)S(1)} %bitcast.9), channel_id=1, replica_groups=mesh['gx'=8,'gy'=4] {'gx','gy'}, dimensions={0} | all-to-all | bytes 622592 | tf_op jit(solution)/shard_map/all_to_all | solution.py:641
  43.9 0.0 copy-done.5
  43.9 0.0 copy-done.7
  43.9 1.3 %shard_map.189 = (f32[3,16,32,128]{3,2,1,0:T(8,128)}, f32[3,32]{1,0:T(4,128)}) custom-call(f32[608,128]{1,0:T(8,128)S(1)} %bitcast.8, f32[3,16,32,128]{3,2,1,0:T(8,128)S(1)} %get-tuple-element.26.star, f32[8,128]{1,0:T(8,128)S(1)} %get-tuple-element.27.stay, bf16[256,256]{1,0:T(8,128)(2,1)S(1)} %copy-done.5, f32[128,128]{1,0:T(8,128)S(1)} %copy-done.7), custom_call_target="tpu_custom_call" | custom-call | flops 6553600 | bytes 2085248 | tf_op jit(solution)/shard_map/pallas_call | solution.py:628
Async XLA Ops:
  0.6 7.1 %copy-start.1 = (f32[16,32,128]{2,1,0:T(8,128)S(1)}, f32[16,32,128]{2,1,0:T(8,128)}, u32[]{:S(2)}) copy-start(f32[16,32,128]{2,1,0:T(8,128)} %theta.7) | copy-start | bytes 786436
  0.6 7.1 %copy-start = (f32[3,16,32,128]{3,2,1,0:T(8,128)S(1)}, f32[3,16,32,128]{3,2,1,0:T(8,128)}, u32[]{:S(2)}) copy-start(f32[3,16,32,128]{3,2,1,0:T(8,128)} %vel.7) | copy-start | bytes 2359300
  0.7 7.1 %copy-start.2 = (f32[16,32,128]{2,1,0:T(8,128)S(1)}, f32[16,32,128]{2,1,0:T(8,128)}, u32[]{:S(2)}) copy-start(f32[16,32,128]{2,1,0:T(8,128)} %vapour.5) | copy-start | bytes 786436
  1.7 10.0 %collective-permute-start = (f32[5,32,128]{2,1,0:T(8,128)S(1)}, f32[5,32,128]{2,1,0:T(8,128)S(1)}, u32[]{:S(2)}, u32[]{:S(2)}) collective-permute-start(f32[5,32,128]{2,1,0:T(8,128)S(1)} %get-tuple-element.21), channel_id=1, source_target_pairs={{0,28},{4,8},{8,4},{12,16},{16,12},{20,24},{24,20},{28,0},{1,29},{... | collective-permute-start | bytes 245768 | tf_op jit(solution)/shard_map/ppermute | solution.py:663
  7.7 4.4 %collective-permute-start.2 = (f32[5,32,128]{2,1,0:T(8,128)S(1)}, f32[5,32,128]{2,1,0:T(8,128)S(1)}, u32[]{:S(2)}, u32[]{:S(2)}) collective-permute-start(f32[5,32,128]{2,1,0:T(8,128)S(1)} %get-tuple-element.22.after), channel_id=1, source_target_pairs={{0,4},{4,0},{8,12},{12,8},{16,20},{20,16},{24,28},{28,24},{1,5},{5... | collective-permute-start | bytes 245768 | tf_op jit(solution)/shard_map/ppermute | solution.py:663
  7.8 3.9 %collective-permute-start.1 = (f32[5,16,128]{2,1,0:T(8,128)S(1)}, f32[5,16,128]{2,1,0:T(8,128)S(1)}, u32[]{:S(2)}, u32[]{:S(2)}) collective-permute-start(f32[5,16,128]{2,1,0:T(8,128)S(1)} %get-tuple-element.23), channel_id=1, source_target_pairs={{0,3},{1,2},{2,1},{3,0},{4,7},{5,6},{6,5},{7,4},{8,11},{9,10},{10,... | collective-permute-start | bytes 122888 | tf_op jit(solution)/shard_map/ppermute | solution.py:664
  8.6 3.6 %copy-start.6 = (bf16[256,256]{1,0:T(8,128)(2,1)S(1)}, bf16[256,256]{1,0:T(8,128)(2,1)}, u32[]{:S(2)}) copy-start(bf16[256,256]{1,0:T(8,128)(2,1)} %constant.16.clone.forward) | copy-start | bytes 393220
  8.6 3.1 %collective-permute-start.3 = (f32[5,16,128]{2,1,0:T(8,128)S(1)}, f32[5,16,128]{2,1,0:T(8,128)S(1)}, u32[]{:S(2)}, u32[]{:S(2)}) collective-permute-start(f32[5,16,128]{2,1,0:T(8,128)S(1)} %get-tuple-element.24), channel_id=1, source_target_pairs={{0,1},{1,0},{2,3},{3,2},{4,5},{5,4},{6,7},{7,6},{8,9},{9,8},{10,11... | collective-permute-start | bytes 122888 | tf_op jit(solution)/shard_map/ppermute | solution.py:664
  13.3 4.1 %copy-start.4 = (f32[288,128]{1,0:T(8,128)S(1)}, f32[288,128]{1,0:T(8,128)}, u32[]{:S(2)}) copy-start(f32[288,128]{1,0:T(8,128)} %constant.17.clone.goes) | copy-start | bytes 442372
  13.3 4.1 %copy-start.10 = (f32[64,32]{0,1:T(8,128)S(1)}, f32[64,32]{0,1:T(8,128)}, u32[]{:S(2)}) copy-start(f32[64,32]{0,1:T(8,128)} %param.19) | copy-start | bytes 24580
  13.3 4.1 %copy-start.11 = (f32[64,32]{0,1:T(8,128)S(1)}, f32[64,32]{0,1:T(8,128)}, u32[]{:S(2)}) copy-start(f32[64,32]{0,1:T(8,128)} %param.20) | copy-start | bytes 24580
  13.3 4.1 %copy-start.12 = (s32[32,64]{1,0:T(8,128)S(1)}, s32[32,64]{1,0:T(8,128)}, u32[]{:S(2)}) copy-start(s32[32,64]{1,0:T(8,128)} %pairing.1) | copy-start | bytes 24580
  13.3 4.1 %copy-start.13 = (s32[64,32]{0,1:T(8,128)S(1)}, s32[64,32]{0,1:T(8,128)}, u32[]{:S(2)}) copy-start(s32[64,32]{0,1:T(8,128)} %param.23) | copy-start | bytes 24580
  13.3 15.4 %all-to-all-start = ((f32[32,1,2304]{2,1,0:T(1,128)}), f32[32,1,2304]{2,1,0:T(1,128)S(1)}, u32[]{:S(2)}, u32[]{:S(2)}) async-start(f32[32,1,2304]{2,1,0:T(1,128)} %bitcast), calls=%async_computation | async-start | bytes 589824 | tf_op jit(solution)/shard_map/all_to_all | solution.py:641
  17.3 0.7 %copy-start.14 = (s32[32]{0:T(128)S(1)}, s32[32]{0:T(128)}, u32[]{:S(2)}) copy-start(s32[32]{0:T(128)} %param.21) | copy-start | bytes 388
  17.4 0.7 %copy-start.15 = (s32[1,128]{1,0:T(1,128)S(1)}, s32[1,128]{1,0:T(1,128)}, u32[]{:S(2)}) copy-start(s32[1,128]{1,0:T(1,128)} %constant.18.clone.kind) | copy-start | bytes 1540
  18.0 10.7 %copy-start.3 = (bf16[4,256,256]{2,1,0:T(8,128)(2,1)S(1)}, bf16[4,256,256]{2,1,0:T(8,128)(2,1)}, u32[]{:S(2)}) copy-start(bf16[4,256,256]{2,1,0:T(8,128)(2,1)} %constant.21.clone.tables) | copy-start | bytes 1572868
  18.0 10.7 %copy-start.8 = (f32[32,512]{1,0:T(8,128)S(1)}, f32[32,512]{1,0:T(8,128)}, u32[]{:S(2)}) copy-start(f32[32,512]{1,0:T(8,128)} %constant.20.clone.eigen_yz) | copy-start | bytes 196612
  18.0 10.7 %copy-start.9 = (f32[128,1]{1,0:T(8,128)S(1)}, f32[128,1]{1,0:T(8,128)}, u32[]{:S(2)}) copy-start(f32[128,1]{1,0:T(8,128)} %constant.19.clone.eigen_x) | copy-start | bytes 1540
  30.1 13.8 %copy-start.5 = (bf16[256,256]{1,0:T(8,128)(2,1)S(1)}, bf16[256,256]{1,0:T(8,128)(2,1)}, u32[]{:S(2)}) copy-start(bf16[256,256]{1,0:T(8,128)(2,1)} %constant.22.clone.backward) | copy-start | bytes 393220
  30.1 13.8 %copy-start.7 = (f32[128,128]{1,0:T(8,128)S(1)}, f32[128,128]{1,0:T(8,128)}, u32[]{:S(2)}) copy-start(f32[128,128]{1,0:T(8,128)} %constant.23.clone.place) | copy-start | bytes 196612

commit v4 on v3

--- a/solution.py
+++ b/solution.py
@@ -37,12 +37,12 @@
 
 def on_left(table):
     high, low = halves(table)
-    return np.block([[high, high], [low, np.zeros_like(low)]])
+    return np.block([[high, high], [low, low]])
 
 
 def on_right(table):
     high, low = halves(table)
-    return np.block([[high, low], [high, np.zeros_like(low)]])
+    return np.block([[high, low], [high, low]])
 
 
 def split(value, axis):
@@ -92,11 +92,14 @@
         self.xg = span_x // self.x4
         self.main = self.per * self.xg
         self.rows1 = self.main + 2
-        self.rows2 = self.main + 3
+        self.rows2 = self.main + 1
         self.tx, self.ty = grid_x * span_x, grid_y * span_y
         self.bx, self.by = span_x // BW, span_y // BW
         self.boxes = self.bx * self.by
         self.slots = slots
+        self.width = 2 * self.by + 2 * self.bx + 4
+        self.edge = 3 * self.width
+        assert max(self.edge + 3 * self.per + 1, self.boxes + self.width) <= LANES
 
     def tables(self):
         nd, per, nz = self.nd, self.per, self.nz
@@ -362,7 +365,8 @@
         ],
         axis=1,
     )
-    solved = from_left(fx, in_y) * inverse
+    spectrum = from_left(fx, in_y)
+    solved = spectrum * inverse
     in_x = from_left(bx, solved)
     in_x = jnp.concatenate([piece(in_x, p, j) for p in range(x4) for j in range(per)], axis=0)
     grid = from_right(in_x, by)
@@ -378,86 +382,90 @@
             ]
             for i, part in enumerate(regroup(parts, plan)):
                 blocks[h + i][q] = part
-    planes = [jnp.zeros((gx, LANES), jnp.float32) for _ in range(gy)]
-    rows = [jnp.zeros((gx, LANES), jnp.float32) for _ in range(gy)]
+    scale = 1.0 / (plan.nz * math.sqrt(plan.tx * plan.ty))
+    mean = jnp.where(rank == 0, spectrum[0:1, 0:1] * scale, 0.0)
+    mean = jnp.where(lane == plan.edge + 3 * per, mean, 0.0)
+
+    def moved(block, source, target):
+        return pltpu.roll(jnp.where(lane == source, block, 0.0), (target - source) % LANES, 1)
+
     for b in range(gy):
         for q in range(plan.main):
-            block = blocks[b][q]
-            out[pl.ds(b * plan.rows2 + q, gx, stride=step2), :] = block
-            moved = jnp.where(first_rows, block, 0.0)
-            nb = (b - 1) % gy
-            rows[nb] = rows[nb] + (moved if q == 0 else pltpu.roll(moved, q, 1))
-            if q % xg == 0:
-                j = q // xg
-                moved = jnp.where(first_lanes, block, 0.0)
-                planes[b] = planes[b] + (moved if j == 0 else pltpu.roll(moved, j * plan.sy, 1))
-    for b in range(gy):
-        out[pl.ds(b * plan.rows2 + plan.main, gx, stride=step2), :] = pltpu.roll(
-            planes[b], gx - 1, 0
+            out[pl.ds(b * plan.rows2 + q, gx, stride=step2), :] = blocks[b][q]
+        along_x = jnp.zeros((gx, LANES), jnp.float32)
+        row = leave[pl.ds(b, gx, stride=gy), :] + mean
+        for j in range(per):
+            here = blocks[b][j * xg]
+            along_x = along_x + moved(here, 0, plan.edge + j)
+            along_x = along_x + moved(here, plan.sy - 1, plan.edge + 2 * per + j)
+            row = row + moved(blocks[(b + 1) % gy][j * xg], 0, plan.edge + per + j)
+        out[pl.ds(b * plan.rows2 + plan.main, gx, stride=step2), :] = row + pltpu.roll(
+            along_x, gx - 1, 0
         )
-        out[pl.ds(b * plan.rows2 + plan.main + 1, gx, stride=step2), :] = rows[b]
-    out[pl.ds(plan.main + 2, plan.nd, stride=plan.rows2), :] = leave[...]
-
-
-def project_kernel(plan, r, star, stay, backward, place, vel_new, moments, scratch):
-    nd, per, xg, x4, sy, sx = plan.nd, plan.per, plan.xg, plan.x4, plan.sy, plan.sx
-    lane = lax.broadcasted_iota(jnp.int32, (nd, LANES), 1)
+
+
+def project_kernel(plan, r, star, stay, backward, place, vel_new, moments):
+    nd, per, xg, sy, sx = plan.nd, plan.per, plan.xg, plan.sy, plan.sx
+    lane = lax.broadcasted_iota(jnp.int32, (nd, LANES), 1) - plan.edge
 
     def take(q):
         return r[pl.ds(q, nd, stride=plan.rows2), :]
 
-    planes, rows = take(plan.main), take(plan.main + 1)
-    wide = jnp.concatenate(
-        [
-            jnp.concatenate([jnp.where(lane // sy == j, planes, 0.0) for j in range(per)], axis=0),
-            jnp.concatenate(
-                [jnp.where(lane % sy // xg == j, rows, 0.0) for j in range(per)], axis=0
-            ),
-        ],
-        axis=1,
-    )
+    row = take(plan.main)
+    beyond = (lane >= 0) & (lane < 3 * per)
+    beyond = [jnp.where(beyond & (lane % per == j), row, 0.0) for j in range(per)]
     modes = [
         jnp.concatenate([take(j * xg + g) for j in range(per)], axis=0) for g in range(xg)
     ]
-    cells = from_right(jnp.concatenate(modes + [wide], axis=1), backward[...], turned=True)
-    extra = cells[xg * LANES :]
-    beyond = extra[0:sy]
-    for j in range(1, per):
-        beyond = beyond + extra[j * sy : (j + 1) * sy]
-    scratch[...] = extra[LANES:]
-    row = lax.broadcasted_iota(jnp.int32, (sy, plan.nz), 0)
-    level = lax.broadcasted_iota(jnp.int32, (sy, plan.nz), 1)
+    modes.append(jnp.concatenate(beyond, axis=0))
+    cells = from_right(jnp.concatenate(modes, axis=1), backward[...], turned=True)
+
+    def cell(k):
+        at = xg * LANES + plan.edge + k * per
+        return functools.reduce(jnp.add, [cells[at + j : at + j + 1] for j in range(per)])
+
+    east_first, north_first, east_last = cell(0), cell(1), cell(2)
+    came = jnp.sum(row, axis=0, keepdims=True)
+    mean = came[:, plan.edge + 3 * per : plan.edge + 3 * per + 1]
     pressure = [cells[x * sy : (x + 1) * sy] for x in range(sx)]
-    pressure.append(beyond)
+    y = lax.broadcasted_iota(jnp.int32, (sy, plan.nz), 0)
+    z = lax.broadcasted_iota(jnp.int32, (sy, plan.nz), 1)
+    ends = slice(sy - 8, sy)
+    u_before = None
     for x in range(sx):
         here = pressure[x]
-        g, p = x // x4, x % x4
-        last = scratch[p * sy + g : p * sy + g + 1]
-        for j in range(1, per):
-            last = last + scratch[p * sy + j * xg + g : p * sy + j * xg + g + 1]
-        north = jnp.where(row == sy - 1, last, pltpu.roll(here, sy - 1, 0))
-        upper = jnp.where(level == plan.nz - 1, here, pltpu.roll(here, plan.nz - 1, 1))
-        vel_new[0, x] = star[0, x] - (pressure[x + 1] - here)
-        vel_new[1, x] = star[1, x] - (north - here)
-        vel_new[2, x] = star[2, x] - (upper - here)
-    came = jnp.sum(take(plan.main + 2), axis=0, keepdims=True)
+        upper = jnp.where(z == plan.nz - 1, here, pltpu.roll(here, plan.nz - 1, 1))
+        w = star[2, x] - (upper - here)
+        along_z = w - before(w, 1)
+        v = star[1, x] - (pltpu.roll(here, sy - 1, 0) - here)
+        if x < sx - 1:
+            u = star[0, x] - (pressure[x + 1] - here)
+        else:
+            u = u_before - (v - pltpu.roll(v, 1, 0)) - along_z + mean
+            u = jnp.where(y == 0, star[0, x] - (east_first - here), u)
+            u = jnp.where(y == sy - 1, star[0, x] - (east_last - here), u)
+        if x == 0:
+            v_last = star[1, x, ends] - (north_first - here[ends])
+        else:
+            v_last = pltpu.roll(v[ends], 1, 0) - (u[ends] - u_before[ends]) - along_z[ends] + mean
+        v_last = jnp.where(y[ends] == sy - 1, v_last, v[ends])
+        vel_new[0, x] = u
+        vel_new[1, x, : sy - 8] = v[: sy - 8]
+        vel_new[1, x, sy - 8 :] = v_last
+        vel_new[2, x] = w
+        u_before = u
     load = lax.broadcasted_iota(jnp.int32, (8, LANES), 0)
     at = lax.broadcasted_iota(jnp.int32, (8, LANES), 1)
-    width = payload_width(plan)
-    loads = jnp.where(at // width == load, came, 0.0)
+    loads = jnp.where(at // plan.width == load, came, 0.0)
     total = stay[...] + lax.dot_general(
         loads, place[...], NN, precision=lax.Precision.HIGHEST, preferred_element_type=jnp.float32
     )
     moments[...] = total[:3, : plan.boxes] * (1.0 / plan.slots)
 
 
-def payload_width(plan):
-    return 2 * plan.by + 2 * plan.bx + 4
-
-
 def droplet_tables(plan):
     bx, by, boxes = plan.bx, plan.by, plan.boxes
-    width = payload_width(plan)
+    width = plan.width
     lane_of = {}
     kind_of = np.full((LANES,), -1)
     place = np.zeros((LANES, LANES), np.float32)
@@ -467,7 +475,7 @@
         for x in xs:
             for y in ys:
                 lane_of[k, x, y] = len(lane_of)
-    assert len(lane_of) == width and max(3 * width, boxes + width) <= LANES
+    assert len(lane_of) == width
     for (k, x, y), at in lane_of.items():
         for load in range(3):
             kind_of[load * width + at] = k
@@ -603,7 +611,7 @@
     stays = jnp.zeros((8, LANES), jnp.float32)
     line = lax.broadcasted_iota(jnp.int32, (8, LANES), 0)
     lane = lax.broadcasted_iota(jnp.int32, (1, LANES), 1)
-    width = payload_width(plan)
+    width = plan.width
     leaving = (lane >= boxes) & (lane < boxes + width)
     for k in range(3):
         column = jnp.concatenate(parts[k], axis=0)
@@ -701,7 +709,6 @@
         ((3,) + block, (3, plan.boxes)),
         (modal, star, stay, on_right(backward), place),
         100 * cells,
-        (pltpu.VMEM((LANES, levels), jnp.float32),),
     )
     return (velocity_new, theta_new, vapour_new, moments)
 

time: 45.6 us -> 45 us (0.987)
  blocking collectives: 13.8 us -> 13.2 us
    all_to_all x1, blocking collectives: 13.8 us -> 13.2 us  [exchange(): lax.all_to_all(flat, ('gx', 'gy'), split_axis=0, concat_axis=0, tiled=True)]
where the time goes in v4:
time: 45 us; the launch traced here: 44.7 us
  blocking collectives  13.2 us (29%)
  starting transfers between devices  11.8 us (26%)
  waiting for transfers between devices  9.53 us (21%)
  Pallas kernels  8.72 us (19%)
  between operations  0.79 us (2%)
  local copies, waits for them, and re-layouts  0.67 us (1%)
    all_to_all x1, blocking collectives, exchange(): lax.all_to_all(flat, ('gx', 'gy'), split_axis=0, concat_axis=0, tiled=True)  13.2 us
    pallas_call x7, Pallas kernels, call(): pl.pallas_call(body, out_shape=[jax.ShapeDtypeStruct(o, jnp.float32) for...  8.72 us
    all_to_all x1, waiting for transfers between devices, exchange(): lax.all_to_all(flat, ('gx', 'gy'), split_axis=0, concat_axis=0, tiled=True)  8.28 us
    ppermute x1, starting transfers between devices, shards(): lax.ppermute(xb, 'gx', ways_x[1])  6.04 us
    all_to_all x1, starting transfers between devices, exchange(): lax.all_to_all(flat, ('gx', 'gy'), split_axis=0, concat_axis=0, tiled=True)  4.03 us
    ppermute x1, starting transfers between devices, shards(): lax.ppermute(ya, 'gy', ways_y[0])  0.96 us
  transfers between devices with their start and end apart: 5, of which 3 were waited for; matrix products, arithmetic and copies ran while one was open for 0% of the time, Pallas kernels for 9%

profile of v4, /device:TPU:0, one launch (start us, length us, event | category | flops | bytes accessed | tf_op | source)
XLA Modules:
  0.0 44.7 jit_solution(16995633894772405767)
XLA Ops:
  0.6 0.0 copy-start.1
  0.6 0.0 copy-start
  0.7 0.0 copy-start.2
  0.7 1.0 %shard_map.184 = (f32[5,32,128]{2,1,0:T(8,128)S(1)}, f32[5,32,128]{2,1,0:T(8,128)S(1)}) custom-call(f32[3,16,32,128]{3,2,1,0:T(8,128)} %vel.7, f32[16,32,128]{2,1,0:T(8,128)} %theta.7, f32[16,32,128]{2,1,0:T(8,128)} %vapour.5), custom_call_target="tpu_custom_call" | custom-call | flops 65536 | bytes 1474560 | tf_op jit(solution)/shard_map/pallas_call | solution.py:636
  1.7 6.0 %collective-permute-start = (f32[5,32,128]{2,1,0:T(8,128)S(1)}, f32[5,32,128]{2,1,0:T(8,128)S(1)}, u32[]{:S(2)}, u32[]{:S(2)}) collective-permute-start(f32[5,32,128]{2,1,0:T(8,128)S(1)} %get-tuple-element.21), channel_id=1, source_target_pairs={{0,28},{4,8},{8,4},{12,16},{16,12},{20,24},{24,20},{28,0},{1,29},{... | collective-permute-start | bytes 245768 | tf_op jit(solution)/shard_map/ppermute | solution.py:671
  7.7 0.0 collective-permute-start.2
  7.7 0.0 copy-done.1
  7.7 0.0 copy-done
  7.7 0.0 copy-done.2
  7.8 0.1 shard_map.185
  7.8 0.7 %collective-permute-start.1 = (f32[5,16,128]{2,1,0:T(8,128)S(1)}, f32[5,16,128]{2,1,0:T(8,128)S(1)}, u32[]{:S(2)}, u32[]{:S(2)}) collective-permute-start(f32[5,16,128]{2,1,0:T(8,128)S(1)} %get-tuple-element.23), channel_id=1, source_target_pairs={{0,3},{1,2},{2,1},{3,0},{4,7},{5,6},{6,5},{7,4},{8,11},{9,10},{10,... | collective-permute-start | bytes 122888 | tf_op jit(solution)/shard_map/ppermute | solution.py:672
  8.6 0.0 copy-start.6
  8.6 1.0 %collective-permute-start.3 = (f32[5,16,128]{2,1,0:T(8,128)S(1)}, f32[5,16,128]{2,1,0:T(8,128)S(1)}, u32[]{:S(2)}, u32[]{:S(2)}) collective-permute-start(f32[5,16,128]{2,1,0:T(8,128)S(1)} %get-tuple-element.24), channel_id=1, source_target_pairs={{0,1},{1,0},{2,3},{3,2},{4,5},{5,4},{6,7},{7,6},{8,9},{9,8},{10,11... | collective-permute-start | bytes 122888 | tf_op jit(solution)/shard_map/ppermute | solution.py:672
  9.5 1.4 %shard_map.183 = (f32[16,32,128]{2,1,0:T(8,128)S(1)}, f32[3,32,128]{2,1,0:T(8,128)S(1)}, f32[3,16,128]{2,1,0:T(8,128)S(1)}) custom-call(f32[3,16,32,128]{3,2,1,0:T(8,128)S(1)} %copy-done, f32[16,32,128]{2,1,0:T(8,128)S(1)} %copy-done.1), custom_call_target="tpu_custom_call" | custom-call | flops 6553600 | bytes 1384448 | tf_op jit(solution)/shard_map/pallas_call | solution.py:636
  10.9 0.8 %collective-permute-done.1.yb = f32[5,16,128]{2,1,0:T(8,128)S(1)} collective-permute-done((f32[5,16,128]{2,1,0:T(8,128)S(1)}, f32[5,16,128]{2,1,0:T(8,128)S(1)}, u32[]{:S(2)}, u32[]{:S(2)}) %collective-permute-start.1) | collective-permute-done | bytes 40992 | tf_op jit(solution)/shard_map/ppermute | solution.py:672
  11.7 0.0 collective-permute-done.3.ya
  11.7 0.0 collective-permute-done.xb
  11.7 0.5 %collective-permute-done.2.xa = f32[5,32,128]{2,1,0:T(8,128)S(1)} collective-permute-done((f32[5,32,128]{2,1,0:T(8,128)S(1)}, f32[5,32,128]{2,1,0:T(8,128)S(1)}, u32[]{:S(2)}, u32[]{:S(2)}) %collective-permute-start.2) | collective-permute-done | bytes 81952 | tf_op jit(solution)/shard_map/ppermute | solution.py:671
  12.2 0.0 copy-done.6
  12.2 1.1 %shard_map.186 = f32[576,128]{1,0:T(8,128)} custom-call(f32[16,32,128]{2,1,0:T(8,128)S(1)} %get-tuple-element.18.div, f32[3,32,128]{2,1,0:T(8,128)S(1)} %get-tuple-element.19.along_x, f32[3,16,128]{2,1,0:T(8,128)S(1)} %get-tuple-element.20.along_y, f32[5,32,128]{2,1,0:T(8,128)S(1)} %collective-permute-done.xb, f32[5,16,128]{2,1,0:T(8,128)S(1)} %collective-permute-done.1.yb, ...), custom_call_target="tpu_custom_call" | custom-call | flops 6553600 | bytes 1007616 | tf_op jit(solution)/shard_map/pallas_call | solution.py:636
  13.3 0.0 copy-start.4
  13.3 0.0 copy-start.10
  13.3 0.0 copy-start.11
  13.3 0.0 copy-start.12
  13.3 0.0 copy-start.13
  13.3 4.0 %all-to-all-start = ((f32[32,1,2304]{2,1,0:T(1,128)}), f32[32,1,2304]{2,1,0:T(1,128)S(1)}, u32[]{:S(2)}, u32[]{:S(2)}) async-start(f32[32,1,2304]{2,1,0:T(1,128)} %bitcast), calls=%async_computation | async-start | bytes 589824 | tf_op jit(solution)/shard_map/all_to_all | solution.py:649
  17.3 0.0 copy-start.14
  17.4 0.0 copy-start.15
  17.4 0.0 copy-done.4
  17.4 0.0 copy-done.10
  17.4 0.0 copy-done.11
  17.4 0.0 copy-done.12
  17.4 0.0 copy-done.13
  17.4 0.6 %copy-done.14 = s32[32]{0:T(128)S(1)} copy-done((s32[32]{0:T(128)S(1)}, s32[32]{0:T(128)}, u32[]{:S(2)}) %copy-start.14) | copy-done | bytes 152
  18.0 0.0 copy-done.15
  18.0 0.0 copy-start.3
  18.0 0.0 copy-start.8
  18.0 0.0 copy-start.9
  18.0 2.4 %shard_map.187 = (f32[3,16,32,128]{3,2,1,0:T(8,128)S(1)}, f32[16,32,128]{2,1,0:T(8,128)}, f32[16,32,128]{2,1,0:T(8,128)}, f32[8,128]{1,0:T(8,128)S(1)}, f32[32,128]{1,0:T(8,128)S(1)}) custom-call(f32[3,16,32,128]{3,2,1,0:T(8,128)S(1)} %copy-done, f32[16,32,128]{2,1,0:T(8,128)S(1)} %copy-done.1, f32[16,32,128]{2,1,0:T(8,128)S(1)} %copy-done.2, ...), custom_call_target="tpu_custom_call" | custom-call | flops 6553600 | bytes 3068544 | tf_op jit(solution)/shard_map/pallas_call | solution.py:636
  20.5 8.3 %all-to-all-done = f32[32,1,2304]{2,1,0:T(1,128)S(1)} async-done(((f32[32,1,2304]{2,1,0:T(1,128)}), f32[32,1,2304]{2,1,0:T(1,128)S(1)}, u32[]{:S(2)}, u32[]{:S(2)}) %all-to-all-start) | async-done | bytes 294944 | tf_op jit(solution)/shard_map/all_to_all | solution.py:649
  28.7 0.0 copy-done.3
  28.7 0.0 copy-done.8
  28.7 0.0 copy-done.9
  28.8 1.3 %shard_map.188 = f32[544,128]{1,0:T(8,128)S(1)} custom-call(f32[576,128]{1,0:T(8,128)S(1)} %bitcast.8, f32[32,128]{1,0:T(8,128)S(1)} %get-tuple-element.25.leave, f32[128,1]{1,0:T(8,128)S(1)} %copy-done.9, f32[32,512]{1,0:T(8,128)S(1)} %copy-done.8, bf16[4,256,256]{2,1,0:T(8,128)(2,1)S(1)} %copy-done.3), custom_call_target="tpu_custom_call" | custom-call | flops 65536000 | bytes 1180160 | tf_op jit(solution)/shard_map/pallas_call | solution.py:636
  30.1 0.0 copy-start.5
  30.1 0.0 copy-start.7
  30.1 13.2 %all_to_all.10 = f32[32,1,2176]{2,1,0:T(1,128)S(1)} all-to-all(f32[32,1,2176]{2,1,0:T(1,128)S(1)} %bitcast.10), channel_id=1, replica_groups=mesh['gx'=8,'gy'=4] {'gx','gy'}, dimensions={0} | all-to-all | bytes 557056 | tf_op jit(solution)/shard_map/all_to_all | solution.py:649
  43.3 0.0 copy-done.5
  43.3 0.0 copy-done.7
  43.3 1.4 %shard_map.189 = (f32[3,16,32,128]{3,2,1,0:T(8,128)}, f32[3,32]{1,0:T(4,128)}) custom-call(f32[544,128]{1,0:T(8,128)S(1)} %bitcast.9, f32[3,16,32,128]{3,2,1,0:T(8,128)S(1)} %get-tuple-element.26.star, f32[8,128]{1,0:T(8,128)S(1)} %get-tuple-element.27.stay, bf16[256,256]{1,0:T(8,128)(2,1)S(1)} %copy-done.5, f32[128,128]{1,0:T(8,128)S(1)} %copy-done.7), custom_call_target="tpu_custom_call" | custom-call | flops 6553600 | bytes 2052480 | tf_op jit(solution)/shard_map/pallas_call | solution.py:636
Async XLA Ops:
  0.6 7.1 %copy-start.1 = (f32[16,32,128]{2,1,0:T(8,128)S(1)}, f32[16,32,128]{2,1,0:T(8,128)}, u32[]{:S(2)}) copy-start(f32[16,32,128]{2,1,0:T(8,128)} %theta.7) | copy-start | bytes 786436
  0.6 7.1 %copy-start = (f32[3,16,32,128]{3,2,1,0:T(8,128)S(1)}, f32[3,16,32,128]{3,2,1,0:T(8,128)}, u32[]{:S(2)}) copy-start(f32[3,16,32,128]{3,2,1,0:T(8,128)} %vel.7) | copy-start | bytes 2359300
  0.7 7.1 %copy-start.2 = (f32[16,32,128]{2,1,0:T(8,128)S(1)}, f32[16,32,128]{2,1,0:T(8,128)}, u32[]{:S(2)}) copy-start(f32[16,32,128]{2,1,0:T(8,128)} %vapour.5) | copy-start | bytes 786436
  1.7 10.0 %collective-permute-start = (f32[5,32,128]{2,1,0:T(8,128)S(1)}, f32[5,32,128]{2,1,0:T(8,128)S(1)}, u32[]{:S(2)}, u32[]{:S(2)}) collective-permute-start(f32[5,32,128]{2,1,0:T(8,128)S(1)} %get-tuple-element.21), channel_id=1, source_target_pairs={{0,28},{4,8},{8,4},{12,16},{16,12},{20,24},{24,20},{28,0},{1,29},{... | collective-permute-start | bytes 245768 | tf_op jit(solution)/shard_map/ppermute | solution.py:671
  7.7 4.4 %collective-permute-start.2 = (f32[5,32,128]{2,1,0:T(8,128)S(1)}, f32[5,32,128]{2,1,0:T(8,128)S(1)}, u32[]{:S(2)}, u32[]{:S(2)}) collective-permute-start(f32[5,32,128]{2,1,0:T(8,128)S(1)} %get-tuple-element.22.after), channel_id=1, source_target_pairs={{0,4},{4,0},{8,12},{12,8},{16,20},{20,16},{24,28},{28,24},{1,5},{5... | collective-permute-start | bytes 245768 | tf_op jit(solution)/shard_map/ppermute | solution.py:671
  7.8 3.9 %collective-permute-start.1 = (f32[5,16,128]{2,1,0:T(8,128)S(1)}, f32[5,16,128]{2,1,0:T(8,128)S(1)}, u32[]{:S(2)}, u32[]{:S(2)}) collective-permute-start(f32[5,16,128]{2,1,0:T(8,128)S(1)} %get-tuple-element.23), channel_id=1, source_target_pairs={{0,3},{1,2},{2,1},{3,0},{4,7},{5,6},{6,5},{7,4},{8,11},{9,10},{10,... | collective-permute-start | bytes 122888 | tf_op jit(solution)/shard_map/ppermute | solution.py:672
  8.6 3.6 %copy-start.6 = (bf16[256,256]{1,0:T(8,128)(2,1)S(1)}, bf16[256,256]{1,0:T(8,128)(2,1)}, u32[]{:S(2)}) copy-start(bf16[256,256]{1,0:T(8,128)(2,1)} %constant.16.clone.forward) | copy-start | bytes 393220
  8.6 3.1 %collective-permute-start.3 = (f32[5,16,128]{2,1,0:T(8,128)S(1)}, f32[5,16,128]{2,1,0:T(8,128)S(1)}, u32[]{:S(2)}, u32[]{:S(2)}) collective-permute-start(f32[5,16,128]{2,1,0:T(8,128)S(1)} %get-tuple-element.24), channel_id=1, source_target_pairs={{0,1},{1,0},{2,3},{3,2},{4,5},{5,4},{6,7},{7,6},{8,9},{9,8},{10,11... | collective-permute-start | bytes 122888 | tf_op jit(solution)/shard_map/ppermute | solution.py:672
  13.3 4.1 %copy-start.4 = (f32[288,128]{1,0:T(8,128)S(1)}, f32[288,128]{1,0:T(8,128)}, u32[]{:S(2)}) copy-start(f32[288,128]{1,0:T(8,128)} %constant.17.clone.goes) | copy-start | bytes 442372
  13.3 4.1 %copy-start.10 = (f32[64,32]{0,1:T(8,128)S(1)}, f32[64,32]{0,1:T(8,128)}, u32[]{:S(2)}) copy-start(f32[64,32]{0,1:T(8,128)} %param.19) | copy-start | bytes 24580
  13.3 4.1 %copy-start.11 = (f32[64,32]{0,1:T(8,128)S(1)}, f32[64,32]{0,1:T(8,128)}, u32[]{:S(2)}) copy-start(f32[64,32]{0,1:T(8,128)} %param.20) | copy-start | bytes 24580
  13.3 4.1 %copy-start.12 = (s32[32,64]{1,0:T(8,128)S(1)}, s32[32,64]{1,0:T(8,128)}, u32[]{:S(2)}) copy-start(s32[32,64]{1,0:T(8,128)} %pairing.1) | copy-start | bytes 24580
  13.3 4.1 %copy-start.13 = (s32[64,32]{0,1:T(8,128)S(1)}, s32[64,32]{0,1:T(8,128)}, u32[]{:S(2)}) copy-start(s32[64,32]{0,1:T(8,128)} %param.23) | copy-start | bytes 24580
  13.3 15.4 %all-to-all-start = ((f32[32,1,2304]{2,1,0:T(1,128)}), f32[32,1,2304]{2,1,0:T(1,128)S(1)}, u32[]{:S(2)}, u32[]{:S(2)}) async-start(f32[32,1,2304]{2,1,0:T(1,128)} %bitcast), calls=%async_computation | async-start | bytes 589824 | tf_op jit(solution)/shard_map/all_to_all | solution.py:649
  17.3 0.7 %copy-start.14 = (s32[32]{0:T(128)S(1)}, s32[32]{0:T(128)}, u32[]{:S(2)}) copy-start(s32[32]{0:T(128)} %param.21) | copy-start | bytes 388
  17.4 0.7 %copy-start.15 = (s32[1,128]{1,0:T(1,128)S(1)}, s32[1,128]{1,0:T(1,128)}, u32[]{:S(2)}) copy-start(s32[1,128]{1,0:T(1,128)} %constant.18.clone.kind) | copy-start | bytes 1540
  18.0 10.7 %copy-start.3 = (bf16[4,256,256]{2,1,0:T(8,128)(2,1)S(1)}, bf16[4,256,256]{2,1,0:T(8,128)(2,1)}, u32[]{:S(2)}) copy-start(bf16[4,256,256]{2,1,0:T(8,128)(2,1)} %constant.21.clone.tables) | copy-start | bytes 1572868
  18.0 10.7 %copy-start.8 = (f32[32,512]{1,0:T(8,128)S(1)}, f32[32,512]{1,0:T(8,128)}, u32[]{:S(2)}) copy-start(f32[32,512]{1,0:T(8,128)} %constant.20.clone.eigen_yz) | copy-start | bytes 196612
  18.0 10.7 %copy-start.9 = (f32[128,1]{1,0:T(8,128)S(1)}, f32[128,1]{1,0:T(8,128)}, u32[]{:S(2)}) copy-start(f32[128,1]{1,0:T(8,128)} %constant.19.clone.eigen_x) | copy-start | bytes 1540
  30.1 13.2 %copy-start.5 = (bf16[256,256]{1,0:T(8,128)(2,1)S(1)}, bf16[256,256]{1,0:T(8,128)(2,1)}, u32[]{:S(2)}) copy-start(bf16[256,256]{1,0:T(8,128)(2,1)} %constant.22.clone.backward) | copy-start | bytes 393220
  30.1 13.2 %copy-start.7 = (f32[128,128]{1,0:T(8,128)S(1)}, f32[128,128]{1,0:T(8,128)}, u32[]{:S(2)}) copy-start(f32[128,128]{1,0:T(8,128)} %constant.23.clone.place) | copy-start | bytes 196612

commit v5 on v4

--- a/solution.py
+++ b/solution.py
@@ -32,17 +32,17 @@
 def halves(table):
     high = table.astype(np.float32).astype(ml_dtypes.bfloat16)
     low = (table - high.astype(np.float64)).astype(np.float32).astype(ml_dtypes.bfloat16)
-    return high, low
-
-
-def on_left(table):
-    high, low = halves(table)
-    return np.block([[high, high], [low, low]])
-
-
-def on_right(table):
-    high, low = halves(table)
-    return np.block([[high, low], [high, low]])
+    return np.concatenate([high, low], axis=0)
+
+
+def on_left(pair):
+    return jnp.concatenate([pair, pair], axis=1)
+
+
+def on_right(pair):
+    size = pair.shape[0] // 2
+    once = jnp.concatenate([pair[:size], pair[size:]], axis=1)
+    return jnp.concatenate([once, once], axis=0)
 
 
 def split(value, axis):
@@ -91,7 +91,7 @@
         self.x4 = LANES // span_y
         self.xg = span_x // self.x4
         self.main = self.per * self.xg
-        self.rows1 = self.main + 2
+        self.rows1 = self.main + 1
         self.rows2 = self.main + 1
         self.tx, self.ty = grid_x * span_x, grid_y * span_y
         self.bx, self.by = span_x // BW, span_y // BW
@@ -134,8 +134,10 @@
     odd = lax.axis_index("gx") % 2
     copies = []
     for side, (out, x) in enumerate(((xb, odd), (xa, 1 - odd))):
+        second = 1 + x * (plan.sx - 3)
         x = x * (plan.sx - 1)
         copies += [
+            pltpu.make_async_copy(vel.at[0, second], out.at[5], sems.at[side, 3]),
             pltpu.make_async_copy(vel.at[:, x], out.at[0:3], sems.at[side, 0]),
             pltpu.make_async_copy(theta.at[x], out.at[3], sems.at[side, 1]),
             pltpu.make_async_copy(vapour.at[x], out.at[4], sems.at[side, 2]),
@@ -153,6 +155,10 @@
             low, high = ref[x, 0:1], ref[x, plan.sy - 1 :]
             ya[f, x : x + 1] = jnp.where(odd, low, high)
             yb[f, x : x + 1] = jnp.where(odd, high, low)
+    for x in range(plan.sx):
+        low, high = vel[1, x, 1:2], vel[1, x, plan.sy - 2 : plan.sy - 1]
+        ya[5, x : x + 1] = jnp.where(odd, low, high)
+        yb[5, x : x + 1] = jnp.where(odd, high, low)
 
 
 def edge_masks(plan):
@@ -175,7 +181,11 @@
     row0, row_last, lane0, lane_last = masks
     north = jnp.where(row_last, north_row, pltpu.roll(c, plan.sy - 1, 0))
     south = jnp.where(row0, south_row, pltpu.roll(c, 1, 0))
-    upper = jnp.where(lane_last, c, pltpu.roll(c, plan.nz - 1, 1))
+    return weigh(c, east, west, north, south, coef, lane0, lane_last)
+
+
+def weigh(c, east, west, north, south, coef, lane0, lane_last):
+    upper = jnp.where(lane_last, c, pltpu.roll(c, c.shape[1] - 1, 1))
     lower = jnp.where(lane0, c, pltpu.roll(c, 1, 1))
     ce, cw, cn, cs, cu, cl = coef
     return (
@@ -225,8 +235,10 @@
         along_y[0, x : x + 1] = v[plan.sy - 1 : plan.sy]
         along_y[1, x : x + 1] = coef[3][0:1]
         along_y[2, x : x + 1] = coef[2][plan.sy - 1 : plan.sy]
+        along_y[3, x : x + 1] = vel[1, x, 0:1]
         if x == 0:
             along_x[1] = coef[1]
+            along_x[3] = vel[0, x]
         if x == last:
             along_x[0] = u
             along_x[2] = coef[0]
@@ -242,7 +254,27 @@
     first_row = south_u - before(south_u, 0) + south_v + south_w - before(south_w, 1)
     last_row = north_u - before(north_u, 0) + north_v + north_w - before(north_w, 1)
     row = lax.broadcasted_iota(jnp.int32, (plan.sy, plan.nz), 0)
+    column = lax.broadcasted_iota(jnp.int32, (plan.sx, plan.nz), 0)
+    level = lax.broadcasted_iota(jnp.int32, (plan.sx, plan.nz), 1)
     last = plan.sx - 1
+    west = [side[0] for side in sides]
+    none = jnp.zeros((1, plan.nz), jnp.float32)
+    west_star = advect(
+        west[0], along_x[3], side_planes(xa, xb, 5)[0], none, none, coefficients(*west),
+        edge_masks(plan), plan,
+    )
+    south = [end[0] for end in ends]
+    south_star = weigh(
+        south[1],
+        jnp.where(column == last, 0.0, pltpu.roll(south[1], plan.sx - 1, 0)),
+        before(south[1], 0),
+        along_y[3],
+        side_rows(ya, yb, 5)[0],
+        coefficients(*south),
+        level == 0,
+        level == plan.nz - 1,
+    )
+    first_row = first_row - south_star
     slab = []
     for x in range(plan.sx):
         at = slice(x, x + 1)
@@ -254,31 +286,20 @@
             ),
         )
         if x == 0:
-            total = total + west_u + (west_v - before(west_v, 0)) + (west_w - before(west_w, 1))
+            total = total - west_star + west_u + (west_v - before(west_v, 0)) + (west_w - before(west_w, 1))
         if x == 1:
             total = total - west_u
         if x == last:
             total = total + east_u + (east_v - before(east_v, 0)) + (east_w - before(east_w, 1))
         slab.append(total)
-    last_u = along_x[0] + east_u + jnp.where(
-        row == 0, south_u[last:], jnp.where(row == plan.sy - 1, north_u[last:], 0.0)
-    )
-    column = lax.broadcasted_iota(jnp.int32, (plan.sx, plan.nz), 0)
-    last_v = along_y[0] + north_v + jnp.where(
-        column == 0,
-        west_v[plan.sy - 1 :],
-        jnp.where(column == last, east_v[plan.sy - 1 :], 0.0),
-    )
-    tiled_plane = jnp.concatenate([-last_u] * plan.x4, axis=0)
-    tiled_rows = []
-    for p in range(plan.x4):
-        block = jnp.zeros((plan.sy, plan.nz), jnp.float32)
-        for g in range(plan.xg):
-            at = g * plan.x4 + p
-            block = jnp.where(row % plan.xg == g, -last_v[at : at + 1], block)
-        tiled_rows.append(block)
+    corners = (
+        south_u[last:], north_u[last:], west_v[plan.sy - 1 :], east_v[plan.sy - 1 :]
+    )
+    block = jnp.zeros((plan.sy, plan.nz), jnp.float32)
+    for k, corner in enumerate(corners):
+        block = jnp.where(row == k, -corner, block)
     modes = from_left(
-        forward[...], jnp.concatenate(slab + [tiled_plane] + tiled_rows, axis=0), turned=True
+        on_left(forward[...]), jnp.concatenate(slab + [block] * plan.x4, axis=0), turned=True
     )
     for g in range(plan.xg):
         for j in range(plan.per):
@@ -287,14 +308,11 @@
             ]
     extra = modes[:, plan.xg * LANES :]
     lane = lax.broadcasted_iota(jnp.int32, (plan.nd, LANES), 1)
-    plane_sum = jnp.zeros((plan.nd, LANES), jnp.float32)
-    row_sum = jnp.zeros((plan.nd, LANES), jnp.float32)
+    total = jnp.zeros((plan.nd, LANES), jnp.float32)
     for j in range(plan.per):
         part = extra[j * plan.nd : (j + 1) * plan.nd]
-        plane_sum = jnp.where(lane // plan.sy == j, part[:, :LANES], plane_sum)
-        row_sum = jnp.where(lane % plan.sy // plan.xg == j, part[:, LANES:], row_sum)
-    out[pl.ds(plan.main, plan.nd, stride=plan.rows1), :] = plane_sum
-    out[pl.ds(plan.main + 1, plan.nd, stride=plan.rows1), :] = row_sum
+        total = jnp.where(lane // plan.sy == j, part, total)
+    out[pl.ds(plan.main, plan.nd, stride=plan.rows1), :] = total
 
 
 def regroup(parts, plan):
@@ -315,31 +333,33 @@
 
 def solve_kernel(plan, r, leave, eigen_x, eigen_yz, tables, out):
     wide_x, wide_y = 2 * plan.tx, 2 * plan.ty
-    fy, by = tables[0, :wide_y, :wide_y], tables[1, :wide_y, :wide_y]
-    fx, bx = tables[2, :wide_x, :wide_x], tables[3, :wide_x, :wide_x]
+    fy, by = (on_right(tables[i, :wide_y, : plan.ty]) for i in (0, 1))
+    fx, bx = (on_left(tables[i, :wide_x, : plan.tx]) for i in (2, 3))
     rank = lax.axis_index("gx") * plan.gy + lax.axis_index("gy")
     eigen = eigen_x[...] + eigen_yz[pl.ds(rank, 1), :]
     inverse = jnp.where(eigen == 0.0, 0.0, 1.0 / jnp.where(eigen == 0.0, 1.0, eigen))
     gx, gy, per, xg, x4 = plan.gx, plan.gy, plan.per, plan.xg, plan.x4
     lane = lax.broadcasted_iota(jnp.int32, (gx, LANES), 1)
-    first_lanes = lane < plan.sy
-    first_rows = lane % plan.sy == 0
     step1, step2 = gy * plan.rows1, gy * plan.rows2
 
     def take(b, q):
         return r[pl.ds(b * plan.rows1 + q, gx, stride=step1), :]
 
+    def moved(block, source, target):
+        return pltpu.roll(jnp.where(lane == source, block, 0.0), (target - source) % LANES, 1)
+
     blocks = [[take(b, q) for q in range(plan.main)] for b in range(gy)]
     for b in range(gy):
-        plane = pltpu.roll(take(b, plan.main), 1, 0)
+        here = take(b, plan.main)
+        ahead = pltpu.roll(here, 1, 0)
+        nb = (b + 1) % gy
         for j in range(per):
-            moved = plane if j == 0 else pltpu.roll(plane, LANES - j * plan.sy, 1)
-            blocks[b][j * xg] = blocks[b][j * xg] + jnp.where(first_lanes, moved, 0.0)
-        rows = take(b, plan.main + 1)
-        for q in range(plan.main):
-            moved = rows if q == 0 else pltpu.roll(rows, LANES - q, 1)
-            nb = (b + 1) % gy
-            blocks[nb][q] = blocks[nb][q] + jnp.where(first_rows, moved, 0.0)
+            at, first, final = j * plan.sy, j * xg, j * xg + xg - 1
+            blocks[b][first] = blocks[b][first] + (
+                moved(ahead, at, 0) + moved(ahead, at + 1, plan.sy - 1)
+            )
+            blocks[nb][first] = blocks[nb][first] + moved(here, at + 2, 0)
+            blocks[nb][final] = blocks[nb][final] + moved(here, at + 3, (x4 - 1) * plan.sy)
     turned = [
         [regroup([blocks[h + i][q] for i in range(x4)], plan) for h in range(0, gy, x4)]
         for q in range(plan.main)
@@ -386,9 +406,6 @@
     mean = jnp.where(rank == 0, spectrum[0:1, 0:1] * scale, 0.0)
     mean = jnp.where(lane == plan.edge + 3 * per, mean, 0.0)
 
-    def moved(block, source, target):
-        return pltpu.roll(jnp.where(lane == source, block, 0.0), (target - source) % LANES, 1)
-
     for b in range(gy):
         for q in range(plan.main):
             out[pl.ds(b * plan.rows2 + q, gx, stride=step2), :] = blocks[b][q]
@@ -418,7 +435,7 @@
         jnp.concatenate([take(j * xg + g) for j in range(per)], axis=0) for g in range(xg)
     ]
     modes.append(jnp.concatenate(beyond, axis=0))
-    cells = from_right(jnp.concatenate(modes, axis=1), backward[...], turned=True)
+    cells = from_right(jnp.concatenate(modes, axis=1), on_right(backward[...]), turned=True)
 
     def cell(k):
         at = xg * LANES + plan.edge + k * per
@@ -659,12 +676,12 @@
     block = (span_x, span_y, levels)
     cells = math.prod(block)
 
-    plane, rows = (5, span_y, levels), (5, span_x, levels)
+    plane, rows = (6, span_y, levels), (6, span_x, levels)
     fields = (velocity, theta, vapour)
     placed = [pltpu.with_memory_space_constraint(f, pltpu.HBM) for f in fields]
     xb, xa = call(
         functools.partial(planes_kernel, plan), (plane, plane), placed, cells,
-        [pltpu.SemaphoreType.DMA((2, 3))], HBM,
+        [pltpu.SemaphoreType.DMA((2, 4))], HBM,
     )
     yb, ya = call(functools.partial(rows_kernel, plan), (rows, rows), (*fields, xa), cells)
     ways_x, ways_y = neighbours(plan.gx), neighbours(plan.gy)
@@ -674,17 +691,19 @@
 
     inner = call(
         functools.partial(inner_kernel, plan),
-        (block, (3, span_y, levels), (3, span_x, levels)), (velocity, theta), 100 * cells,
+        (block, (4, span_y, levels), (4, span_x, levels)), (velocity, theta), 100 * cells,
     )
     (chunks,) = call(
         functools.partial(spread_kernel, plan), ((plan.nd * plan.rows1, LANES),),
-        (*inner, *halo, on_left(forward)), 100 * cells,
+        (*inner, *halo, halves(forward)), 100 * cells,
     )
     spectral = exchange(chunks, plan, plan.rows1)
 
-    tables = [on_right(qy), on_right(qy.T), on_left(q1), on_left(q1.T)]
-    most = max(t.shape[0] for t in tables)
-    tables = np.stack([np.pad(t, (0, most - t.shape[0])) for t in tables])
+    tables = [halves(qy), halves(qy.T), halves(q1), halves(q1.T)]
+    rows, columns = (max(t.shape[i] for t in tables) for i in (0, 1))
+    tables = np.stack(
+        [np.pad(t, ((0, rows - t.shape[0]), (0, columns - t.shape[1]))) for t in tables]
+    )
     eigen_x = ex.astype(np.float32)[:, None]
     eigen_yz = (ez.reshape(plan.nd, plan.per, 1) + ey).reshape(plan.nd, -1).astype(np.float32)
     star, theta_new, vapour_new, stay, leave = call(
@@ -707,7 +726,7 @@
     velocity_new, moments = call(
         functools.partial(project_kernel, plan),
         ((3,) + block, (3, plan.boxes)),
-        (modal, star, stay, on_right(backward), place),
+        (modal, star, stay, halves(backward), place),
         100 * cells,
     )
     return (velocity_new, theta_new, vapour_new, moments)

time: 45 us -> 44.9 us (level)
  no operation moved by 1% of the time
where the time goes in v5:
time: 44.9 us; the launch traced here: 44.6 us
  blocking collectives  13.2 us (29%)
  starting transfers between devices  11.5 us (26%)
  waiting for transfers between devices  9.68 us (22%)
  Pallas kernels  8.78 us (20%)
  between operations  0.79 us (2%)
  local copies, waits for them, and re-layouts  0.67 us (1%)
    all_to_all x1, blocking collectives, exchange(): lax.all_to_all(flat, ('gx', 'gy'), split_axis=0, concat_axis=0, tiled=True)  13.2 us
    pallas_call x7, Pallas kernels, call(): pl.pallas_call(body, out_shape=[jax.ShapeDtypeStruct(o, jnp.float32) for...  8.78 us
    all_to_all x1, waiting for transfers between devices, exchange(): lax.all_to_all(flat, ('gx', 'gy'), split_axis=0, concat_axis=0, tiled=True)  7.98 us
    ppermute x1, starting transfers between devices, shards(): lax.ppermute(xb, 'gx', ways_x[1])  6.04 us
    all_to_all x1, starting transfers between devices, exchange(): lax.all_to_all(flat, ('gx', 'gy'), split_axis=0, concat_axis=0, tiled=True)  3.74 us
    ppermute x1, starting transfers between devices, shards(): lax.ppermute(ya, 'gy', ways_y[0])  0.96 us
    ppermute x1, waiting for transfers between devices, shards(): lax.ppermute(yb, 'gy', ways_y[1])  0.94 us
  transfers between devices with their start and end apart: 5, of which 3 were waited for; matrix products, arithmetic and copies ran while one was open for 0% of the time, Pallas kernels for 9%

profile of v5, /device:TPU:0, one launch (start us, length us, event | category | flops | bytes accessed | tf_op | source)
XLA Modules:
  0.0 44.6 jit_solution(12523056056356114128)
XLA Ops:
  0.6 0.0 copy-start.1
  0.6 0.0 copy-start
  0.7 0.0 copy-start.2
  0.7 1.1 %shard_map.184 = (f32[6,32,128]{2,1,0:T(8,128)S(1)}, f32[6,32,128]{2,1,0:T(8,128)S(1)}) custom-call(f32[3,16,32,128]{3,2,1,0:T(8,128)} %vel.7, f32[16,32,128]{2,1,0:T(8,128)} %theta.7, f32[16,32,128]{2,1,0:T(8,128)} %vapour.5), custom_call_target="tpu_custom_call" | custom-call | flops 65536 | bytes 1507328 | tf_op jit(solution)/shard_map/pallas_call | solution.py:653
  1.7 6.0 %collective-permute-start = (f32[6,32,128]{2,1,0:T(8,128)S(1)}, f32[6,32,128]{2,1,0:T(8,128)S(1)}, u32[]{:S(2)}, u32[]{:S(2)}) collective-permute-start(f32[6,32,128]{2,1,0:T(8,128)S(1)} %get-tuple-element.21), channel_id=1, source_target_pairs={{0,28},{4,8},{8,4},{12,16},{16,12},{20,24},{24,20},{28,0},{1,29},{... | collective-permute-start | bytes 294920 | tf_op jit(solution)/shard_map/ppermute | solution.py:688
  7.8 0.0 collective-permute-start.2
  7.8 0.0 copy-done.1
  7.8 0.0 copy-done
  7.8 0.0 copy-done.2
  7.8 0.1 shard_map.185
  7.9 0.7 %collective-permute-start.1 = (f32[6,16,128]{2,1,0:T(8,128)S(1)}, f32[6,16,128]{2,1,0:T(8,128)S(1)}, u32[]{:S(2)}, u32[]{:S(2)}) collective-permute-start(f32[6,16,128]{2,1,0:T(8,128)S(1)} %get-tuple-element.23), channel_id=1, source_target_pairs={{0,3},{1,2},{2,1},{3,0},{4,7},{5,6},{6,5},{7,4},{8,11},{9,10},{10,... | collective-permute-start | bytes 147464 | tf_op jit(solution)/shard_map/ppermute | solution.py:689
  8.6 0.0 copy-start.9
  8.6 1.0 %collective-permute-start.3 = (f32[6,16,128]{2,1,0:T(8,128)S(1)}, f32[6,16,128]{2,1,0:T(8,128)S(1)}, u32[]{:S(2)}, u32[]{:S(2)}) collective-permute-start(f32[6,16,128]{2,1,0:T(8,128)S(1)} %get-tuple-element.24), channel_id=1, source_target_pairs={{0,1},{1,0},{2,3},{3,2},{4,5},{5,4},{6,7},{7,6},{8,9},{9,8},{10,11... | collective-permute-start | bytes 147464 | tf_op jit(solution)/shard_map/ppermute | solution.py:689
  9.6 1.4 %shard_map.183 = (f32[16,32,128]{2,1,0:T(8,128)S(1)}, f32[4,32,128]{2,1,0:T(8,128)S(1)}, f32[4,16,128]{2,1,0:T(8,128)S(1)}) custom-call(f32[3,16,32,128]{3,2,1,0:T(8,128)S(1)} %copy-done, f32[16,32,128]{2,1,0:T(8,128)S(1)} %copy-done.1), custom_call_target="tpu_custom_call" | custom-call | flops 6553600 | bytes 1409024 | tf_op jit(solution)/shard_map/pallas_call | solution.py:653
  11.0 0.9 %collective-permute-done.1.yb = f32[6,16,128]{2,1,0:T(8,128)S(1)} collective-permute-done((f32[6,16,128]{2,1,0:T(8,128)S(1)}, f32[6,16,128]{2,1,0:T(8,128)S(1)}, u32[]{:S(2)}, u32[]{:S(2)}) %collective-permute-start.1) | collective-permute-done | bytes 49184 | tf_op jit(solution)/shard_map/ppermute | solution.py:689
  11.9 0.0 collective-permute-done.3.ya
  11.9 0.0 collective-permute-done.xb
  11.9 0.8 %collective-permute-done.2.xa = f32[6,32,128]{2,1,0:T(8,128)S(1)} collective-permute-done((f32[6,32,128]{2,1,0:T(8,128)S(1)}, f32[6,32,128]{2,1,0:T(8,128)S(1)}, u32[]{:S(2)}, u32[]{:S(2)}) %collective-permute-start.2) | collective-permute-done | bytes 98336 | tf_op jit(solution)/shard_map/ppermute | solution.py:688
  12.7 0.0 copy-done.9
  12.7 1.1 %shard_map.186 = f32[544,128]{1,0:T(8,128)} custom-call(f32[16,32,128]{2,1,0:T(8,128)S(1)} %get-tuple-element.18.div, f32[4,32,128]{2,1,0:T(8,128)S(1)} %get-tuple-element.19.along_x, f32[4,16,128]{2,1,0:T(8,128)S(1)} %get-tuple-element.20.along_y, f32[6,32,128]{2,1,0:T(8,128)S(1)} %collective-permute-done.xb, f32[6,16,128]{2,1,0:T(8,128)S(1)} %collective-permute-done.1.yb, ...), custom_call_target="tpu_custom_call" | custom-call | flops 6553600 | bytes 999424 | tf_op jit(solution)/shard_map/pallas_call | solution.py:653
  13.8 0.0 copy-start.4
  13.8 0.0 copy-start.10
  13.8 0.0 copy-start.11
  13.8 0.0 copy-start.12
  13.8 0.0 copy-start.13
  13.8 3.7 %all-to-all-start = ((f32[32,1,2176]{2,1,0:T(1,128)}), f32[32,1,2176]{2,1,0:T(1,128)S(1)}, u32[]{:S(2)}, u32[]{:S(2)}) async-start(f32[32,1,2176]{2,1,0:T(1,128)} %bitcast), calls=%async_computation | async-start | bytes 557056 | tf_op jit(solution)/shard_map/all_to_all | solution.py:666
  17.6 0.0 copy-start.14
  17.6 0.0 copy-start.15
  17.6 0.0 copy-done.4
  17.6 0.0 copy-done.10
  17.6 0.0 copy-done.11
  17.6 0.0 copy-done.12
  17.6 0.0 copy-done.13
  17.6 0.6 %copy-done.14 = s32[32]{0:T(128)S(1)} copy-done((s32[32]{0:T(128)S(1)}, s32[32]{0:T(128)}, u32[]{:S(2)}) %copy-start.14) | copy-done | bytes 152
  18.2 0.0 copy-done.15
  18.2 0.0 copy-start.3
  18.2 0.0 copy-start.7
  18.2 0.0 copy-start.8
  18.2 2.4 %shard_map.187 = (f32[3,16,32,128]{3,2,1,0:T(8,128)S(1)}, f32[16,32,128]{2,1,0:T(8,128)}, f32[16,32,128]{2,1,0:T(8,128)}, f32[8,128]{1,0:T(8,128)S(1)}, f32[32,128]{1,0:T(8,128)S(1)}) custom-call(f32[3,16,32,128]{3,2,1,0:T(8,128)S(1)} %copy-done, f32[16,32,128]{2,1,0:T(8,128)S(1)} %copy-done.1, f32[16,32,128]{2,1,0:T(8,128)S(1)} %copy-done.2, ...), custom_call_target="tpu_custom_call" | custom-call | flops 6553600 | bytes 3117696 | tf_op jit(solution)/shard_map/pallas_call | solution.py:653
  20.7 8.0 %all-to-all-done = f32[32,1,2176]{2,1,0:T(1,128)S(1)} async-done(((f32[32,1,2176]{2,1,0:T(1,128)}), f32[32,1,2176]{2,1,0:T(1,128)S(1)}, u32[]{:S(2)}, u32[]{:S(2)}) %all-to-all-start) | async-done | bytes 278560 | tf_op jit(solution)/shard_map/all_to_all | solution.py:666
  28.7 0.0 copy-done.3
  28.7 0.0 copy-done.7
  28.7 0.0 copy-done.8
  28.7 1.3 %shard_map.188 = f32[544,128]{1,0:T(8,128)S(1)} custom-call(f32[544,128]{1,0:T(8,128)S(1)} %bitcast.8, f32[32,128]{1,0:T(8,128)S(1)} %get-tuple-element.25.leave, f32[128,1]{1,0:T(8,128)S(1)} %copy-done.8, f32[32,512]{1,0:T(8,128)S(1)} %copy-done.7, bf16[4,256,128]{2,1,0:T(8,128)(2,1)S(1)} %copy-done.3), custom_call_target="tpu_custom_call" | custom-call | flops 65536000 | bytes 901632 | tf_op jit(solution)/shard_map/pallas_call | solution.py:653
  30.0 0.0 copy-start.5
  30.0 0.0 copy-start.6
  30.0 13.2 %all_to_all.10 = f32[32,1,2176]{2,1,0:T(1,128)S(1)} all-to-all(f32[32,1,2176]{2,1,0:T(1,128)S(1)} %bitcast.10), channel_id=1, replica_groups=mesh['gx'=8,'gy'=4] {'gx','gy'}, dimensions={0} | all-to-all | bytes 557056 | tf_op jit(solution)/shard_map/all_to_all | solution.py:666
  43.2 0.0 copy-done.5
  43.2 0.0 copy-done.6
  43.2 1.4 %shard_map.189 = (f32[3,16,32,128]{3,2,1,0:T(8,128)}, f32[3,32]{1,0:T(4,128)}) custom-call(f32[544,128]{1,0:T(8,128)S(1)} %bitcast.9, f32[3,16,32,128]{3,2,1,0:T(8,128)S(1)} %get-tuple-element.26.star, f32[8,128]{1,0:T(8,128)S(1)} %get-tuple-element.27.stay, bf16[256,128]{1,0:T(8,128)(2,1)S(1)} %copy-done.6, f32[128,128]{1,0:T(8,128)S(1)} %copy-done.5), custom_call_target="tpu_custom_call" | custom-call | flops 6553600 | bytes 1986944 | tf_op jit(solution)/shard_map/pallas_call | solution.py:653
Async XLA Ops:
  0.6 7.2 %copy-start.1 = (f32[16,32,128]{2,1,0:T(8,128)S(1)}, f32[16,32,128]{2,1,0:T(8,128)}, u32[]{:S(2)}) copy-start(f32[16,32,128]{2,1,0:T(8,128)} %theta.7) | copy-start | bytes 786436
  0.6 7.1 %copy-start = (f32[3,16,32,128]{3,2,1,0:T(8,128)S(1)}, f32[3,16,32,128]{3,2,1,0:T(8,128)}, u32[]{:S(2)}) copy-start(f32[3,16,32,128]{3,2,1,0:T(8,128)} %vel.7) | copy-start | bytes 2359300
  0.7 7.1 %copy-start.2 = (f32[16,32,128]{2,1,0:T(8,128)S(1)}, f32[16,32,128]{2,1,0:T(8,128)}, u32[]{:S(2)}) copy-start(f32[16,32,128]{2,1,0:T(8,128)} %vapour.5) | copy-start | bytes 786436
  1.7 10.2 %collective-permute-start = (f32[6,32,128]{2,1,0:T(8,128)S(1)}, f32[6,32,128]{2,1,0:T(8,128)S(1)}, u32[]{:S(2)}, u32[]{:S(2)}) collective-permute-start(f32[6,32,128]{2,1,0:T(8,128)S(1)} %get-tuple-element.21), channel_id=1, source_target_pairs={{0,28},{4,8},{8,4},{12,16},{16,12},{20,24},{24,20},{28,0},{1,29},{... | collective-permute-start | bytes 294920 | tf_op jit(solution)/shard_map/ppermute | solution.py:688
  7.8 4.9 %collective-permute-start.2 = (f32[6,32,128]{2,1,0:T(8,128)S(1)}, f32[6,32,128]{2,1,0:T(8,128)S(1)}, u32[]{:S(2)}, u32[]{:S(2)}) collective-permute-start(f32[6,32,128]{2,1,0:T(8,128)S(1)} %get-tuple-element.22.after), channel_id=1, source_target_pairs={{0,4},{4,0},{8,12},{12,8},{16,20},{20,16},{24,28},{28,24},{1,5},{5... | collective-permute-start | bytes 294920 | tf_op jit(solution)/shard_map/ppermute | solution.py:688
  7.9 4.0 %collective-permute-start.1 = (f32[6,16,128]{2,1,0:T(8,128)S(1)}, f32[6,16,128]{2,1,0:T(8,128)S(1)}, u32[]{:S(2)}, u32[]{:S(2)}) collective-permute-start(f32[6,16,128]{2,1,0:T(8,128)S(1)} %get-tuple-element.23), channel_id=1, source_target_pairs={{0,3},{1,2},{2,1},{3,0},{4,7},{5,6},{6,5},{7,4},{8,11},{9,10},{10,... | collective-permute-start | bytes 147464 | tf_op jit(solution)/shard_map/ppermute | solution.py:689
  8.6 4.1 %copy-start.9 = (bf16[256,128]{1,0:T(8,128)(2,1)S(1)}, bf16[256,128]{1,0:T(8,128)(2,1)}, u32[]{:S(2)}) copy-start(bf16[256,128]{1,0:T(8,128)(2,1)} %constant.16.clone.forward) | copy-start | bytes 196612
  8.6 3.3 %collective-permute-start.3 = (f32[6,16,128]{2,1,0:T(8,128)S(1)}, f32[6,16,128]{2,1,0:T(8,128)S(1)}, u32[]{:S(2)}, u32[]{:S(2)}) collective-permute-start(f32[6,16,128]{2,1,0:T(8,128)S(1)} %get-tuple-element.24), channel_id=1, source_target_pairs={{0,1},{1,0},{2,3},{3,2},{4,5},{5,4},{6,7},{7,6},{8,9},{9,8},{10,11... | collective-permute-start | bytes 147464 | tf_op jit(solution)/shard_map/ppermute | solution.py:689
  13.8 3.8 %copy-start.4 = (f32[288,128]{1,0:T(8,128)S(1)}, f32[288,128]{1,0:T(8,128)}, u32[]{:S(2)}) copy-start(f32[288,128]{1,0:T(8,128)} %constant.17.clone.goes) | copy-start | bytes 442372
  13.8 3.8 %copy-start.10 = (f32[64,32]{0,1:T(8,128)S(1)}, f32[64,32]{0,1:T(8,128)}, u32[]{:S(2)}) copy-start(f32[64,32]{0,1:T(8,128)} %param.19) | copy-start | bytes 24580
  13.8 3.8 %copy-start.11 = (f32[64,32]{0,1:T(8,128)S(1)}, f32[64,32]{0,1:T(8,128)}, u32[]{:S(2)}) copy-start(f32[64,32]{0,1:T(8,128)} %param.20) | copy-start | bytes 24580
  13.8 3.8 %copy-start.12 = (s32[32,64]{1,0:T(8,128)S(1)}, s32[32,64]{1,0:T(8,128)}, u32[]{:S(2)}) copy-start(s32[32,64]{1,0:T(8,128)} %pairing.1) | copy-start | bytes 24580
  13.8 3.8 %copy-start.13 = (s32[64,32]{0,1:T(8,128)S(1)}, s32[64,32]{0,1:T(8,128)}, u32[]{:S(2)}) copy-start(s32[64,32]{0,1:T(8,128)} %param.23) | copy-start | bytes 24580
  13.8 14.8 %all-to-all-start = ((f32[32,1,2176]{2,1,0:T(1,128)}), f32[32,1,2176]{2,1,0:T(1,128)S(1)}, u32[]{:S(2)}, u32[]{:S(2)}) async-start(f32[32,1,2176]{2,1,0:T(1,128)} %bitcast), calls=%async_computation | async-start | bytes 557056 | tf_op jit(solution)/shard_map/all_to_all | solution.py:666
  17.6 0.7 %copy-start.14 = (s32[32]{0:T(128)S(1)}, s32[32]{0:T(128)}, u32[]{:S(2)}) copy-start(s32[32]{0:T(128)} %param.21) | copy-start | bytes 388
  17.6 0.7 %copy-start.15 = (s32[1,128]{1,0:T(1,128)S(1)}, s32[1,128]{1,0:T(1,128)}, u32[]{:S(2)}) copy-start(s32[1,128]{1,0:T(1,128)} %constant.18.clone.kind) | copy-start | bytes 1540
  18.2 10.4 %copy-start.3 = (bf16[4,256,128]{2,1,0:T(8,128)(2,1)S(1)}, bf16[4,256,128]{2,1,0:T(8,128)(2,1)}, u32[]{:S(2)}) copy-start(bf16[4,256,128]{2,1,0:T(8,128)(2,1)} %constant.21.clone.tables) | copy-start | bytes 786436
  18.2 10.4 %copy-start.7 = (f32[32,512]{1,0:T(8,128)S(1)}, f32[32,512]{1,0:T(8,128)}, u32[]{:S(2)}) copy-start(f32[32,512]{1,0:T(8,128)} %constant.20.clone.eigen_yz) | copy-start | bytes 196612
  18.2 10.4 %copy-start.8 = (f32[128,1]{1,0:T(8,128)S(1)}, f32[128,1]{1,0:T(8,128)}, u32[]{:S(2)}) copy-start(f32[128,1]{1,0:T(8,128)} %constant.19.clone.eigen_x) | copy-start | bytes 1540
  30.0 13.2 %copy-start.5 = (f32[128,128]{1,0:T(8,128)S(1)}, f32[128,128]{1,0:T(8,128)}, u32[]{:S(2)}) copy-start(f32[128,128]{1,0:T(8,128)} %constant.23.clone.place) | copy-start | bytes 196612
  30.0 13.2 %copy-start.6 = (bf16[256,128]{1,0:T(8,128)(2,1)S(1)}, bf16[256,128]{1,0:T(8,128)(2,1)}, u32[]{:S(2)}) copy-start(bf16[256,128]{1,0:T(8,128)(2,1)} %constant.22.clone.backward) | copy-start | bytes 196612

commit v6 on v5

--- a/solution.py
+++ b/solution.py
@@ -29,26 +29,30 @@
 KINDS = [(sx, sy) for sx in (-1, 0, 1) for sy in (-1, 0, 1) if (sx, sy) != (0, 0)]
 
 
-def halves(table):
-    high = table.astype(np.float32).astype(ml_dtypes.bfloat16)
-    low = (table - high.astype(np.float64)).astype(np.float32).astype(ml_dtypes.bfloat16)
-    return np.concatenate([high, low], axis=0)
-
-
-def on_left(pair):
-    return jnp.concatenate([pair, pair], axis=1)
-
-
-def on_right(pair):
-    size = pair.shape[0] // 2
-    once = jnp.concatenate([pair[:size], pair[size:]], axis=1)
-    return jnp.concatenate([once, once], axis=0)
+def thirds(table):
+    parts = []
+    for _ in range(3):
+        parts.append(table.astype(np.float32).astype(ml_dtypes.bfloat16))
+        table = table - parts[-1].astype(np.float64)
+    return np.concatenate(parts, axis=0)
+
+
+def on_left(parts):
+    return jnp.concatenate([parts] * 3, axis=1)
+
+
+def on_right(parts):
+    size = parts.shape[0] // 3
+    once = jnp.concatenate([parts[i * size : (i + 1) * size] for i in range(3)], axis=1)
+    return jnp.concatenate([once] * 3, axis=0)
 
 
 def split(value, axis):
-    high = value.astype(jnp.bfloat16)
-    low = (value - high.astype(jnp.float32)).astype(jnp.bfloat16)
-    return jnp.concatenate([high, low], axis=axis)
+    parts = []
+    for _ in range(3):
+        parts.append(value.astype(jnp.bfloat16))
+        value = value - parts[-1].astype(jnp.float32)
+    return jnp.concatenate(parts, axis=axis)
 
 
 def from_left(table, value, turned=False):
@@ -56,8 +60,8 @@
         table, split(value, 1 if turned else 0), NT if turned else NN,
         preferred_element_type=jnp.float32,
     )
-    rows = out.shape[0] // 2
-    return out[:rows] + out[rows:]
+    rows = out.shape[0] // 3
+    return out[:rows] + (out[rows : 2 * rows] + out[2 * rows :])
 
 
 def from_right(value, table, turned=False):
@@ -65,8 +69,8 @@
         split(value, 0 if turned else 1), table, TN if turned else NN,
         preferred_element_type=jnp.float32,
     )
-    columns = out.shape[1] // 2
-    return out[:, :columns] + out[:, columns:]
+    columns = out.shape[1] // 3
+    return out[:, :columns] + (out[:, columns : 2 * columns] + out[:, 2 * columns :])
 
 
 def real_basis(length):
@@ -332,7 +336,7 @@
 
 
 def solve_kernel(plan, r, leave, eigen_x, eigen_yz, tables, out):
-    wide_x, wide_y = 2 * plan.tx, 2 * plan.ty
+    wide_x, wide_y = 3 * plan.tx, 3 * plan.ty
     fy, by = (on_right(tables[i, :wide_y, : plan.ty]) for i in (0, 1))
     fx, bx = (on_left(tables[i, :wide_x, : plan.tx]) for i in (2, 3))
     rank = lax.axis_index("gx") * plan.gy + lax.axis_index("gy")
@@ -695,11 +699,11 @@
     )
     (chunks,) = call(
         functools.partial(spread_kernel, plan), ((plan.nd * plan.rows1, LANES),),
-        (*inner, *halo, halves(forward)), 100 * cells,
+        (*inner, *halo, thirds(forward)), 100 * cells,
     )
     spectral = exchange(chunks, plan, plan.rows1)
 
-    tables = [halves(qy), halves(qy.T), halves(q1), halves(q1.T)]
+    tables = [thirds(qy), thirds(qy.T), thirds(q1), thirds(q1.T)]
     rows, columns = (max(t.shape[i] for t in tables) for i in (0, 1))
     tables = np.stack(
         [np.pad(t, ((0, rows - t.shape[0]), (0, columns - t.shape[1]))) for t in tables]
@@ -726,7 +730,7 @@
     velocity_new, moments = call(
         functools.partial(project_kernel, plan),
         ((3,) + block, (3, plan.boxes)),
-        (modal, star, stay, halves(backward), place),
+        (modal, star, stay, thirds(backward), place),
         100 * cells,
     )
     return (velocity_new, theta_new, vapour_new, moments)

time: 44.9 us -> 45.9 us (1.022)
  Pallas kernels: 8.78 us -> 9.79 us
    pallas_call x7, Pallas kernels: 8.78 us -> 9.79 us  [call(): pl.pallas_call(body, out_shape=[jax.ShapeDtypeStruct(o, jnp.float32) for...]
where the time goes in v6:
time: 45.9 us; the launch traced here: 45.6 us
  blocking collectives  13.2 us (29%)
  starting transfers between devices  11.5 us (25%)
  Pallas kernels  9.79 us (21%)
  waiting for transfers between devices  9.68 us (21%)
  between operations  0.79 us (2%)
  local copies, waits for them, and re-layouts  0.67 us (1%)
    all_to_all x1, blocking collectives, exchange(): lax.all_to_all(flat, ('gx', 'gy'), split_axis=0, concat_axis=0, tiled=True)  13.2 us
    pallas_call x7, Pallas kernels, call(): pl.pallas_call(body, out_shape=[jax.ShapeDtypeStruct(o, jnp.float32) for...  9.79 us
    all_to_all x1, waiting for transfers between devices, exchange(): lax.all_to_all(flat, ('gx', 'gy'), split_axis=0, concat_axis=0, tiled=True)  7.98 us
    ppermute x1, starting transfers between devices, shards(): lax.ppermute(xb, 'gx', ways_x[1])  6.04 us
    all_to_all x1, starting transfers between devices, exchange(): lax.all_to_all(flat, ('gx', 'gy'), split_axis=0, concat_axis=0, tiled=True)  3.74 us
    ppermute x1, starting transfers between devices, shards(): lax.ppermute(ya, 'gy', ways_y[0])  0.96 us
    ppermute x1, waiting for transfers between devices, shards(): lax.ppermute(yb, 'gy', ways_y[1])  0.94 us
  transfers between devices with their start and end apart: 5, of which 3 were waited for; matrix products, arithmetic and copies ran while one was open for 0% of the time, Pallas kernels for 9%

profile of v6, /device:TPU:0, one launch (start us, length us, event | category | flops | bytes accessed | tf_op | source)
XLA Modules:
  0.0 45.6 jit_solution(11293167682875877882)
XLA Ops:
  0.6 0.0 copy-start.1
  0.6 0.0 copy-start
  0.7 0.0 copy-start.2
  0.7 1.1 %shard_map.184 = (f32[6,32,128]{2,1,0:T(8,128)S(1)}, f32[6,32,128]{2,1,0:T(8,128)S(1)}) custom-call(f32[3,16,32,128]{3,2,1,0:T(8,128)} %vel.7, f32[16,32,128]{2,1,0:T(8,128)} %theta.7, f32[16,32,128]{2,1,0:T(8,128)} %vapour.5), custom_call_target="tpu_custom_call" | custom-call | flops 65536 | bytes 1507328 | tf_op jit(solution)/shard_map/pallas_call | solution.py:657
  1.7 6.0 %collective-permute-start = (f32[6,32,128]{2,1,0:T(8,128)S(1)}, f32[6,32,128]{2,1,0:T(8,128)S(1)}, u32[]{:S(2)}, u32[]{:S(2)}) collective-permute-start(f32[6,32,128]{2,1,0:T(8,128)S(1)} %get-tuple-element.21), channel_id=1, source_target_pairs={{0,28},{4,8},{8,4},{12,16},{16,12},{20,24},{24,20},{28,0},{1,29},{... | collective-permute-start | bytes 294920 | tf_op jit(solution)/shard_map/ppermute | solution.py:692
  7.8 0.0 collective-permute-start.2
  7.8 0.0 copy-done.1
  7.8 0.0 copy-done
  7.8 0.0 copy-done.2
  7.8 0.1 shard_map.185
  7.9 0.7 %collective-permute-start.1 = (f32[6,16,128]{2,1,0:T(8,128)S(1)}, f32[6,16,128]{2,1,0:T(8,128)S(1)}, u32[]{:S(2)}, u32[]{:S(2)}) collective-permute-start(f32[6,16,128]{2,1,0:T(8,128)S(1)} %get-tuple-element.23), channel_id=1, source_target_pairs={{0,3},{1,2},{2,1},{3,0},{4,7},{5,6},{6,5},{7,4},{8,11},{9,10},{10,... | collective-permute-start | bytes 147464 | tf_op jit(solution)/shard_map/ppermute | solution.py:693
  8.6 0.0 copy-start.6
  8.6 1.0 %collective-permute-start.3 = (f32[6,16,128]{2,1,0:T(8,128)S(1)}, f32[6,16,128]{2,1,0:T(8,128)S(1)}, u32[]{:S(2)}, u32[]{:S(2)}) collective-permute-start(f32[6,16,128]{2,1,0:T(8,128)S(1)} %get-tuple-element.24), channel_id=1, source_target_pairs={{0,1},{1,0},{2,3},{3,2},{4,5},{5,4},{6,7},{7,6},{8,9},{9,8},{10,11... | collective-permute-start | bytes 147464 | tf_op jit(solution)/shard_map/ppermute | solution.py:693
  9.6 1.4 %shard_map.183 = (f32[16,32,128]{2,1,0:T(8,128)S(1)}, f32[4,32,128]{2,1,0:T(8,128)S(1)}, f32[4,16,128]{2,1,0:T(8,128)S(1)}) custom-call(f32[3,16,32,128]{3,2,1,0:T(8,128)S(1)} %copy-done, f32[16,32,128]{2,1,0:T(8,128)S(1)} %copy-done.1), custom_call_target="tpu_custom_call" | custom-call | flops 6553600 | bytes 1409024 | tf_op jit(solution)/shard_map/pallas_call | solution.py:657
  11.0 0.9 %collective-permute-done.1.yb = f32[6,16,128]{2,1,0:T(8,128)S(1)} collective-permute-done((f32[6,16,128]{2,1,0:T(8,128)S(1)}, f32[6,16,128]{2,1,0:T(8,128)S(1)}, u32[]{:S(2)}, u32[]{:S(2)}) %collective-permute-start.1) | collective-permute-done | bytes 49184 | tf_op jit(solution)/shard_map/ppermute | solution.py:693
  11.9 0.0 collective-permute-done.3.ya
  11.9 0.0 collective-permute-done.xb
  11.9 0.8 %collective-permute-done.2.xa = f32[6,32,128]{2,1,0:T(8,128)S(1)} collective-permute-done((f32[6,32,128]{2,1,0:T(8,128)S(1)}, f32[6,32,128]{2,1,0:T(8,128)S(1)}, u32[]{:S(2)}, u32[]{:S(2)}) %collective-permute-start.2) | collective-permute-done | bytes 98336 | tf_op jit(solution)/shard_map/ppermute | solution.py:692
  12.7 0.0 copy-done.6
  12.7 1.3 %shard_map.186 = f32[544,128]{1,0:T(8,128)} custom-call(f32[16,32,128]{2,1,0:T(8,128)S(1)} %get-tuple-element.18.div, f32[4,32,128]{2,1,0:T(8,128)S(1)} %get-tuple-element.19.along_x, f32[4,16,128]{2,1,0:T(8,128)S(1)} %get-tuple-element.20.along_y, f32[6,32,128]{2,1,0:T(8,128)S(1)} %collective-permute-done.xb, f32[6,16,128]{2,1,0:T(8,128)S(1)} %collective-permute-done.1.yb, ...), custom_call_target="tpu_custom_call" | custom-call | flops 6553600 | bytes 1032192 | tf_op jit(solution)/shard_map/pallas_call | solution.py:657
  14.0 0.0 copy-start.4
  14.0 0.0 copy-start.10
  14.0 0.0 copy-start.11
  14.0 0.0 copy-start.12
  14.0 0.0 copy-start.13
  14.0 3.7 %all-to-all-start = ((f32[32,1,2176]{2,1,0:T(1,128)}), f32[32,1,2176]{2,1,0:T(1,128)S(1)}, u32[]{:S(2)}, u32[]{:S(2)}) async-start(f32[32,1,2176]{2,1,0:T(1,128)} %bitcast), calls=%async_computation | async-start | bytes 557056 | tf_op jit(solution)/shard_map/all_to_all | solution.py:670
  17.7 0.0 copy-start.14
  17.7 0.0 copy-start.15
  17.8 0.0 copy-done.4
  17.8 0.0 copy-done.10
  17.8 0.0 copy-done.11
  17.8 0.0 copy-done.12
  17.8 0.0 copy-done.13
  17.8 0.6 %copy-done.14 = s32[32]{0:T(128)S(1)} copy-done((s32[32]{0:T(128)S(1)}, s32[32]{0:T(128)}, u32[]{:S(2)}) %copy-start.14) | copy-done | bytes 152
  18.4 0.0 copy-done.15
  18.4 0.0 copy-start.3
  18.4 0.0 copy-start.8
  18.4 0.0 copy-start.9
  18.4 2.4 %shard_map.187 = (f32[3,16,32,128]{3,2,1,0:T(8,128)S(1)}, f32[16,32,128]{2,1,0:T(8,128)}, f32[16,32,128]{2,1,0:T(8,128)}, f32[8,128]{1,0:T(8,128)S(1)}, f32[32,128]{1,0:T(8,128)S(1)}) custom-call(f32[3,16,32,128]{3,2,1,0:T(8,128)S(1)} %copy-done, f32[16,32,128]{2,1,0:T(8,128)S(1)} %copy-done.1, f32[16,32,128]{2,1,0:T(8,128)S(1)} %copy-done.2, ...), custom_call_target="tpu_custom_call" | custom-call | flops 6553600 | bytes 3117696 | tf_op jit(solution)/shard_map/pallas_call | solution.py:657
  20.8 8.0 %all-to-all-done = f32[32,1,2176]{2,1,0:T(1,128)S(1)} async-done(((f32[32,1,2176]{2,1,0:T(1,128)}), f32[32,1,2176]{2,1,0:T(1,128)S(1)}, u32[]{:S(2)}, u32[]{:S(2)}) %all-to-all-start) | async-done | bytes 278560 | tf_op jit(solution)/shard_map/all_to_all | solution.py:670
  28.8 0.0 copy-done.3
  28.8 0.0 copy-done.8
  28.8 0.0 copy-done.9
  28.8 2.0 %shard_map.188 = f32[544,128]{1,0:T(8,128)S(1)} custom-call(f32[544,128]{1,0:T(8,128)S(1)} %bitcast.9, f32[32,128]{1,0:T(8,128)S(1)} %get-tuple-element.25.leave, f32[128,1]{1,0:T(8,128)S(1)} %copy-done.9, f32[32,512]{1,0:T(8,128)S(1)} %copy-done.8, bf16[4,384,128]{2,1,0:T(8,128)(2,1)S(1)} %copy-done.3), custom_call_target="tpu_custom_call" | custom-call | flops 65536000 | bytes 1032704 | tf_op jit(solution)/shard_map/pallas_call | solution.py:657
  30.8 0.0 copy-start.5
  30.9 0.0 copy-start.7
  30.9 13.2 %all_to_all.10 = f32[32,1,2176]{2,1,0:T(1,128)S(1)} all-to-all(f32[32,1,2176]{2,1,0:T(1,128)S(1)} %bitcast.10), channel_id=1, replica_groups=mesh['gx'=8,'gy'=4] {'gx','gy'}, dimensions={0} | all-to-all | bytes 557056 | tf_op jit(solution)/shard_map/all_to_all | solution.py:670
  44.0 0.0 copy-done.5
  44.0 0.0 copy-done.7
  44.0 1.5 %shard_map.189 = (f32[3,16,32,128]{3,2,1,0:T(8,128)}, f32[3,32]{1,0:T(4,128)}) custom-call(f32[544,128]{1,0:T(8,128)S(1)} %bitcast.8, f32[3,16,32,128]{3,2,1,0:T(8,128)S(1)} %get-tuple-element.26.star, f32[8,128]{1,0:T(8,128)S(1)} %get-tuple-element.27.stay, bf16[384,128]{1,0:T(8,128)(2,1)S(1)} %copy-done.5, f32[128,128]{1,0:T(8,128)S(1)} %copy-done.7), custom_call_target="tpu_custom_call" | custom-call | flops 6553600 | bytes 2019712 | tf_op jit(solution)/shard_map/pallas_call | solution.py:657
Async XLA Ops:
  0.6 7.2 %copy-start.1 = (f32[16,32,128]{2,1,0:T(8,128)S(1)}, f32[16,32,128]{2,1,0:T(8,128)}, u32[]{:S(2)}) copy-start(f32[16,32,128]{2,1,0:T(8,128)} %theta.7) | copy-start | bytes 786436
  0.6 7.1 %copy-start = (f32[3,16,32,128]{3,2,1,0:T(8,128)S(1)}, f32[3,16,32,128]{3,2,1,0:T(8,128)}, u32[]{:S(2)}) copy-start(f32[3,16,32,128]{3,2,1,0:T(8,128)} %vel.7) | copy-start | bytes 2359300
  0.7 7.1 %copy-start.2 = (f32[16,32,128]{2,1,0:T(8,128)S(1)}, f32[16,32,128]{2,1,0:T(8,128)}, u32[]{:S(2)}) copy-start(f32[16,32,128]{2,1,0:T(8,128)} %vapour.5) | copy-start | bytes 786436
  1.7 10.2 %collective-permute-start = (f32[6,32,128]{2,1,0:T(8,128)S(1)}, f32[6,32,128]{2,1,0:T(8,128)S(1)}, u32[]{:S(2)}, u32[]{:S(2)}) collective-permute-start(f32[6,32,128]{2,1,0:T(8,128)S(1)} %get-tuple-element.21), channel_id=1, source_target_pairs={{0,28},{4,8},{8,4},{12,16},{16,12},{20,24},{24,20},{28,0},{1,29},{... | collective-permute-start | bytes 294920 | tf_op jit(solution)/shard_map/ppermute | solution.py:692
  7.8 4.9 %collective-permute-start.2 = (f32[6,32,128]{2,1,0:T(8,128)S(1)}, f32[6,32,128]{2,1,0:T(8,128)S(1)}, u32[]{:S(2)}, u32[]{:S(2)}) collective-permute-start(f32[6,32,128]{2,1,0:T(8,128)S(1)} %get-tuple-element.22.after), channel_id=1, source_target_pairs={{0,4},{4,0},{8,12},{12,8},{16,20},{20,16},{24,28},{28,24},{1,5},{5... | collective-permute-start | bytes 294920 | tf_op jit(solution)/shard_map/ppermute | solution.py:692
  7.9 4.0 %collective-permute-start.1 = (f32[6,16,128]{2,1,0:T(8,128)S(1)}, f32[6,16,128]{2,1,0:T(8,128)S(1)}, u32[]{:S(2)}, u32[]{:S(2)}) collective-permute-start(f32[6,16,128]{2,1,0:T(8,128)S(1)} %get-tuple-element.23), channel_id=1, source_target_pairs={{0,3},{1,2},{2,1},{3,0},{4,7},{5,6},{6,5},{7,4},{8,11},{9,10},{10,... | collective-permute-start | bytes 147464 | tf_op jit(solution)/shard_map/ppermute | solution.py:693
  8.6 4.1 %copy-start.6 = (bf16[384,128]{1,0:T(8,128)(2,1)S(1)}, bf16[384,128]{1,0:T(8,128)(2,1)}, u32[]{:S(2)}) copy-start(bf16[384,128]{1,0:T(8,128)(2,1)} %constant.16.clone.forward) | copy-start | bytes 294916
  8.6 3.3 %collective-permute-start.3 = (f32[6,16,128]{2,1,0:T(8,128)S(1)}, f32[6,16,128]{2,1,0:T(8,128)S(1)}, u32[]{:S(2)}, u32[]{:S(2)}) collective-permute-start(f32[6,16,128]{2,1,0:T(8,128)S(1)} %get-tuple-element.24), channel_id=1, source_target_pairs={{0,1},{1,0},{2,3},{3,2},{4,5},{5,4},{6,7},{7,6},{8,9},{9,8},{10,11... | collective-permute-start | bytes 147464 | tf_op jit(solution)/shard_map/ppermute | solution.py:693
  14.0 3.8 %copy-start.4 = (f32[288,128]{1,0:T(8,128)S(1)}, f32[288,128]{1,0:T(8,128)}, u32[]{:S(2)}) copy-start(f32[288,128]{1,0:T(8,128)} %constant.17.clone.goes) | copy-start | bytes 442372
  14.0 3.8 %copy-start.10 = (f32[64,32]{0,1:T(8,128)S(1)}, f32[64,32]{0,1:T(8,128)}, u32[]{:S(2)}) copy-start(f32[64,32]{0,1:T(8,128)} %param.19) | copy-start | bytes 24580
  14.0 3.8 %copy-start.11 = (f32[64,32]{0,1:T(8,128)S(1)}, f32[64,32]{0,1:T(8,128)}, u32[]{:S(2)}) copy-start(f32[64,32]{0,1:T(8,128)} %param.20) | copy-start | bytes 24580
  14.0 3.8 %copy-start.12 = (s32[32,64]{1,0:T(8,128)S(1)}, s32[32,64]{1,0:T(8,128)}, u32[]{:S(2)}) copy-start(s32[32,64]{1,0:T(8,128)} %pairing.1) | copy-start | bytes 24580
  14.0 3.8 %copy-start.13 = (s32[64,32]{0,1:T(8,128)S(1)}, s32[64,32]{0,1:T(8,128)}, u32[]{:S(2)}) copy-start(s32[64,32]{0,1:T(8,128)} %param.23) | copy-start | bytes 24580
  14.0 14.8 %all-to-all-start = ((f32[32,1,2176]{2,1,0:T(1,128)}), f32[32,1,2176]{2,1,0:T(1,128)S(1)}, u32[]{:S(2)}, u32[]{:S(2)}) async-start(f32[32,1,2176]{2,1,0:T(1,128)} %bitcast), calls=%async_computation | async-start | bytes 557056 | tf_op jit(solution)/shard_map/all_to_all | solution.py:670
  17.7 0.7 %copy-start.14 = (s32[32]{0:T(128)S(1)}, s32[32]{0:T(128)}, u32[]{:S(2)}) copy-start(s32[32]{0:T(128)} %param.21) | copy-start | bytes 388
  17.7 0.7 %copy-start.15 = (s32[1,128]{1,0:T(1,128)S(1)}, s32[1,128]{1,0:T(1,128)}, u32[]{:S(2)}) copy-start(s32[1,128]{1,0:T(1,128)} %constant.18.clone.kind) | copy-start | bytes 1540
  18.4 10.4 %copy-start.3 = (bf16[4,384,128]{2,1,0:T(8,128)(2,1)S(1)}, bf16[4,384,128]{2,1,0:T(8,128)(2,1)}, u32[]{:S(2)}) copy-start(bf16[4,384,128]{2,1,0:T(8,128)(2,1)} %constant.21.clone.tables) | copy-start | bytes 1179652
  18.4 10.4 %copy-start.8 = (f32[32,512]{1,0:T(8,128)S(1)}, f32[32,512]{1,0:T(8,128)}, u32[]{:S(2)}) copy-start(f32[32,512]{1,0:T(8,128)} %constant.20.clone.eigen_yz) | copy-start | bytes 196612
  18.4 10.4 %copy-start.9 = (f32[128,1]{1,0:T(8,128)S(1)}, f32[128,1]{1,0:T(8,128)}, u32[]{:S(2)}) copy-start(f32[128,1]{1,0:T(8,128)} %constant.19.clone.eigen_x) | copy-start | bytes 1540
  30.8 13.2 %copy-start.5 = (bf16[384,128]{1,0:T(8,128)(2,1)S(1)}, bf16[384,128]{1,0:T(8,128)(2,1)}, u32[]{:S(2)}) copy-start(bf16[384,128]{1,0:T(8,128)(2,1)} %constant.22.clone.backward) | copy-start | bytes 294916
  30.9 13.2 %copy-start.7 = (f32[128,128]{1,0:T(8,128)S(1)}, f32[128,128]{1,0:T(8,128)}, u32[]{:S(2)}) copy-start(f32[128,128]{1,0:T(8,128)} %constant.23.clone.place) | copy-start | bytes 196612
